TPU v7x, 32 devices: a whole 2x2x4 slice. The times are simulated.
32 devices in a mesh: shard: 4 (over z), tensor: 4 (over y, x), section: 2 (over core).
Axes of the slice: x: 2, y: 2, z: 4, core: 2. Of those that a mesh axis runs over, the one named last changes fastest.
Arguments:
- grad_parts: bfloat16 [4, 2, 4, 1024, 1024], P('shard', 'section', None, 'tensor'), may hold values from -45 to 45
- vector_grads: bfloat16 [4, 2, 4, 1024], P('shard', 'section', None, 'tensor'), may hold values from -6 to 6
- momentum: float32 [2, 4, 1024, 1024], P('section', None, ('tensor', 'shard')), may hold values from -6 to 6
- weights: bfloat16 [2, 4, 1024, 1024], P('section', None, ('tensor', 'shard')), may hold values from -0.1875 to 0.1875
- vectors: float32 [2, 4, 1024], P('section', None, ('tensor', 'shard')), may hold values from 0.5 to 1.5
- first_moment: float32 [2, 4, 1024], P('section', None, ('tensor', 'shard')), may hold values from -3 to 3
- second_moment: float32 [2, 4, 1024], P('section', None, ('tensor', 'shard')), may hold values from 0.05 to 2
Outputs:
- new_momentum: float32 [2, 4, 1024, 1024], P('section', None, ('tensor', 'shard'))
- orthogonal_update: bfloat16 [2, 4, 1024, 1024], P('section', None, ('tensor', 'shard'))
- new_weights: bfloat16 [2, 4, 1024, 1024], P('section', None, ('tensor', 'shard'))
- adam_direction: float32 [2, 4, 1024], P('section', None, ('tensor', 'shard'))
- new_vectors: float32 [2, 4, 1024], P('section', None, ('tensor', 'shard'))
All inputs are finite; a program needn't handle non-finite values.
Results may differ from a plain program's by a relative error of at most 0.0048.
The roundings to bfloat16 on the way count: a program that leaves them out, or rounds other values in their place, can miss the bound.
Values may be sent and summed in bfloat16 or wider, within the bound.
No kernel may reach another device: no remote copies, remote signals or barrier semaphores. Data moves between devices by JAX's collectives and lax.ppermute only.
A program may use at most 64 MiB of HBM per device.

v0:
```python
import functools
import math

import jax
import jax.numpy as jnp
from jax import lax
from jax.experimental import pallas as pl
from jax.experimental.pallas import tpu as pltpu
from jax.sharding import PartitionSpec as P

D = 1024
NS_STEPS = 2


ns_first = 3.4445
ns_second = -4.775
ns_third = 2.0315
mom_beta = 0.95
max_norm = 1024.0
muon_rate = 0.02
muon_decay = 0.1
adam_rate = 0.001
adam_decay = 0.01

VECTOR_ROWS = 16
FIGURES = 16
MIB = 2**20
LANES = 128
MESH_AXES = ("shard", "tensor", "section")


def gram_of(blocks, gram_ref):
    width = blocks[0].shape[1]
    step = 256
    for start in range(0, width, step):
        stop = start + step
        total = None
        for block in blocks:
            whole = block[...]
            product = lax.dot_general(
                whole[:, :stop],
                whole[:, start:stop],
                (((0,), (0,)), ((), ())),
                preferred_element_type=jnp.float32,
            )
            rounded = product.astype(jnp.bfloat16).astype(jnp.float32)
            total = rounded if total is None else total + rounded
        gram_ref[:stop, start:stop] = total.astype(jnp.bfloat16)
        for above in range(0, start, step):
            tile = gram_ref[above : above + step, start:stop]
            gram_ref[start:stop, above : above + step] = tile.T


def polynomial(block, gram_ref):
    gram = gram_ref[...]
    first = jnp.dot(block, gram, preferred_element_type=jnp.float32).astype(jnp.bfloat16)
    second = jnp.dot(first, gram, preferred_element_type=jnp.float32)
    combined = (
        ns_first * block.astype(jnp.float32)
        + ns_second * first.astype(jnp.float32)
        + ns_third * second
    )
    return combined.astype(jnp.bfloat16)


def orthogonalize_kernel(count, pieces, *refs):
    height, width = refs[0].shape
    inputs = refs[: count * pieces]
    outputs = refs[count * pieces : count * pieces + pieces]
    gram_ref, start_ref, next_ref = refs[count * pieces + pieces :]
    for position in range(count):
        for piece in range(pieces):
            start_ref[position, piece * height : (piece + 1) * height, :] = inputs[
                position * pieces + piece
            ][...]
    current, other = start_ref, next_ref
    for iteration in range(NS_STEPS - 1):
        gram_of([current.at[position] for position in range(count)], gram_ref)
        for position in range(count):
            other[position] = polynomial(current[position], gram_ref)
        current, other = other, current
    gram_of([current.at[position] for position in range(count)], gram_ref)
    result = polynomial(current[0], gram_ref)
    for piece in range(pieces):
        outputs[piece][...] = result[piece * height : (piece + 1) * height, :]


def orthogonalize(blocks):
    count, pieces = len(blocks), len(blocks[0])
    height, width = blocks[0][0].shape
    return pl.pallas_call(
        functools.partial(orthogonalize_kernel, count, pieces),
        out_shape=[jax.ShapeDtypeStruct((height, width), jnp.bfloat16)] * pieces,
        scratch_shapes=[
            pltpu.VMEM((width, width), jnp.bfloat16),
            pltpu.VMEM((count, pieces * height, width), jnp.bfloat16),
            pltpu.VMEM((count, pieces * height, width), jnp.bfloat16),
        ],
        compiler_params=pltpu.CompilerParams(vmem_limit_bytes=32 * MIB),
    )(*[piece for block in blocks for piece in block])


def folded(array):
    line = jnp.sum(array, axis=0, keepdims=True)
    total = line[:, :LANES]
    for start in range(LANES, line.shape[1], LANES):
        total = total + line[:, start : start + LANES]
    return total


def slices_kernel(count, place_ref, grad_ref, *refs):
    outputs, semaphores = refs[:count], refs[count]
    copies = [
        pltpu.make_async_copy(
            grad_ref.at[:, place_ref[offset]], outputs[offset], semaphores.at[offset]
        )
        for offset in range(count)
    ]
    for copy in reversed(copies):
        copy.start()
    for copy in reversed(copies):
        copy.wait()


def row_slices(place, by_rows):
    matrix_count, shard_count, height, width = by_rows.shape
    return pl.pallas_call(
        functools.partial(slices_kernel, shard_count),
        out_shape=[jax.ShapeDtypeStruct((matrix_count, height, width), by_rows.dtype)]
        * shard_count,
        in_specs=[
            pl.BlockSpec(memory_space=pltpu.SMEM),
            pl.BlockSpec(memory_space=pltpu.HBM),
        ],
        out_specs=[pl.BlockSpec(memory_space=pltpu.VMEM)] * shard_count,
        scratch_shapes=[pltpu.SemaphoreType.DMA((shard_count,))],
        compiler_params=pltpu.CompilerParams(vmem_limit_bytes=4 * MIB),
    )(place, by_rows)


def sum_kernel(shard_count, place_ref, *refs):
    parts = refs[:shard_count]
    vector_parts, momentum_ref, grad_ref, vector_ref, figures_ref = refs[shard_count:]
    vector = jnp.sum(vector_parts[...].astype(jnp.float32), axis=0)
    vector_ref[...] = vector
    total = folded(vector * vector) * (1.0 / shard_count)
    squares, crosses, momentum_squares = [], [], []
    for matrix in range(momentum_ref.shape[0]):
        grad = parts[0][matrix].astype(jnp.float32)
        for part in parts[1:]:
            grad = grad + part[matrix].astype(jnp.float32)
        grad_ref[matrix] = grad
        old = momentum_ref[matrix]
        squares.append(folded(grad * grad))
        crosses.append(folded(grad * old))
        momentum_squares.append(folded(old * old))
        total = total + squares[-1]
    lines = squares + crosses + momentum_squares + [total]
    lines = lines + [jnp.zeros_like(total)] * (FIGURES - len(lines))
    tile = jnp.concatenate(lines, axis=0)
    sums = jnp.sum(tile, axis=1, keepdims=True)
    line_index = lax.broadcasted_iota(jnp.int32, tile.shape, 0)
    lane_index = lax.broadcasted_iota(jnp.int32, tile.shape, 1)
    line = jnp.sum(jnp.where(line_index == lane_index, sums, 0.0), axis=0, keepdims=True)
    total_only = jnp.where(lane_index[:1] == 3 * momentum_ref.shape[0], line, 0.0)
    for section in range(figures_ref.shape[1]):
        chosen = jnp.where(place_ref[shard_count] == section, line, total_only)
        figures_ref[:, section] = jnp.broadcast_to(
            chosen[None], (figures_ref.shape[0],) + line.shape
        )


def scale_kernel(matrix_count, place_ref, figures_ref, grad_ref, momentum_ref, *refs):
    outputs = refs[:matrix_count]
    clip_ref = refs[matrix_count]
    line = jnp.sum(figures_ref[...], axis=0)
    line_index = lax.broadcasted_iota(jnp.int32, (FIGURES, LANES), 0)
    lane_index = lax.broadcasted_iota(jnp.int32, (FIGURES, LANES), 1)
    sums = jnp.sum(jnp.where(line_index == lane_index, line, 0.0), axis=1, keepdims=True)
    total = sums[3 * matrix_count : 3 * matrix_count + 1]
    clip = jnp.minimum(1.0, max_norm / (jnp.sqrt(total) + 1e-06))
    clip_ref[...] = jnp.broadcast_to(clip, clip_ref.shape)
    grad_scale = (1.0 + mom_beta) * clip
    momentum_scale = mom_beta * mom_beta
    update_norm = (
        grad_scale * grad_scale * sums[:matrix_count]
        + 2.0 * grad_scale * momentum_scale * sums[matrix_count : 2 * matrix_count]
        + momentum_scale * momentum_scale * sums[2 * matrix_count : 3 * matrix_count]
    )
    inverse = 1.0 / (jnp.sqrt(jnp.maximum(update_norm, 0.0)) + 1e-07)
    position = lax.broadcasted_iota(jnp.int32, inverse.shape, 0)
    for place in range(matrix_count):
        matrix = place_ref[place]
        factor = jnp.sum(jnp.where(position == matrix, inverse, 0.0), axis=0, keepdims=True)
        clipped = clip * grad_ref[matrix]
        new_momentum = mom_beta * momentum_ref[matrix] + clipped
        nesterov = clipped + mom_beta * new_momentum
        outputs[place][...] = (nesterov * factor).astype(jnp.bfloat16)


def end_kernel(offsets, place_ref, *refs):
    arrived = refs[: len(offsets)]
    weights_ref = refs[len(offsets)]
    update_ref, new_weights_ref, update_rows, weight_rows, semaphores = refs[-5:]
    step_size = muon_rate * (0.2 * math.sqrt(D))
    copies = []
    for slot, offset in enumerate(offsets):
        matrix = place_ref[offset]
        update = arrived[slot][...]
        update_rows[slot] = update
        weight_rows[slot] = (
            weights_ref[matrix].astype(jnp.float32) * (1.0 - muon_rate * muon_decay)
            - step_size * update.astype(jnp.float32)
        ).astype(jnp.bfloat16)
        for kind, (rows, target) in enumerate(
            ((update_rows, update_ref), (weight_rows, new_weights_ref))
        ):
            copies.append(
                pltpu.make_async_copy(
                    rows.at[slot], target.at[matrix], semaphores.at[2 * slot + kind]
                )
            )
            copies[-1].start()
    for copy in copies:
        copy.wait()


def finished(offsets, place, arrived, weights, partial=()):
    height, width = arrived[0].shape
    anywhere = pl.BlockSpec(memory_space=pltpu.HBM)
    return pl.pallas_call(
        functools.partial(end_kernel, offsets),
        out_shape=[jax.ShapeDtypeStruct(weights.shape, weights.dtype)] * 2,
        in_specs=[pl.BlockSpec(memory_space=pltpu.SMEM)]
        + [pl.BlockSpec(memory_space=pltpu.VMEM)] * (len(arrived) + 1)
        + [anywhere] * len(partial),
        out_specs=[anywhere] * 2,
        scratch_shapes=[
            pltpu.VMEM((len(offsets), height, width), weights.dtype),
            pltpu.VMEM((len(offsets), height, width), weights.dtype),
            pltpu.SemaphoreType.DMA((2 * len(offsets),)),
        ],
        input_output_aliases={len(arrived) + 2 + i: i for i in range(len(partial))},
        compiler_params=pltpu.CompilerParams(vmem_limit_bytes=8 * MIB),
    )(place, *arrived, weights, *partial)


def state_kernel(
    place_ref,
    clip_ref,
    grad_ref,
    momentum_ref,
    sums_ref,
    vectors_ref,
    first_ref,
    second_ref,
    new_momentum_ref,
    direction_ref,
    new_ref,
):
    new_momentum_ref[...] = mom_beta * momentum_ref[...] + clip_ref[0:1, 0:1] * grad_ref[...]
    width = vectors_ref.shape[1]
    count = sums_ref.shape[1] // width
    rows = sums_ref[:, :width]
    for position in range(1, count):
        part = sums_ref[:, position * width : (position + 1) * width]
        rows = jnp.where(place_ref[0] == position, part, rows)
    clipped = clip_ref[0:1, 0:1] * rows
    updated_first = 0.9 * first_ref[...] + 0.1 * clipped
    updated_second = 0.999 * second_ref[...] + 0.001 * clipped * clipped
    direction = updated_first / (jnp.sqrt(updated_second) + 1e-08)
    direction_ref[...] = direction
    new_ref[...] = vectors_ref[...] * (1.0 - adam_rate * adam_decay) - adam_rate * direction


def on_device(kernel, scalars, operands, out_shape):
    return pl.pallas_call(
        kernel,
        out_shape=out_shape,
        in_specs=[pl.BlockSpec(memory_space=pltpu.SMEM)]
        + [pl.BlockSpec(memory_space=pltpu.VMEM)] * len(operands),
        compiler_params=pltpu.CompilerParams(vmem_limit_bytes=16 * MIB),
    )(scalars, *operands)


def swapped(array, axis, offset):
    pairs = [(i, i ^ offset) for i in range(lax.axis_size(axis))]
    return lax.ppermute(array, axis, pairs)


def after(array, earlier):
    return lax.optimization_barrier((array, earlier))[0]


def per_device(grad_parts, vector_grads, momentum, weights, vectors, first_moment, second_moment):
    shard_count = lax.axis_size("shard")
    tensor_count = lax.axis_size("tensor")
    section_count = lax.axis_size("section")
    _, matrix_count, local_height, width = momentum.shape
    if shard_count != matrix_count or shard_count != 4 or tensor_count != 4:
        return general_device(
            grad_parts, vector_grads, momentum, weights, vectors, first_moment, second_moment
        )
    vector_count, vector_width = vectors.shape[1:]
    own_momentum = momentum[0]
    position = jnp.arange(shard_count + 1, dtype=jnp.int32)
    place = jnp.where(
        position == shard_count,
        lax.axis_index("section").astype(jnp.int32),
        lax.axis_index("shard").astype(jnp.int32) ^ position,
    )

    by_rows = grad_parts.reshape(matrix_count, shard_count, local_height, width)
    parts = list(row_slices(place, by_rows))
    for offset in reversed(range(1, shard_count)):
        parts[offset] = swapped(parts[offset], "shard", offset)
    vector_parts = lax.all_to_all(
        jnp.broadcast_to(vector_grads[0], (shard_count, vector_count, vector_width * shard_count)),
        "shard",
        split_axis=0,
        concat_axis=0,
        tiled=True,
    )

    others = shard_count * tensor_count
    grad_rows, vector_whole, figures = on_device(
        functools.partial(sum_kernel, shard_count),
        place,
        parts[::-1] + [vector_parts, own_momentum],
        [
            jax.ShapeDtypeStruct(own_momentum.shape, jnp.float32),
            jax.ShapeDtypeStruct(vector_parts.shape[1:], jnp.float32),
            jax.ShapeDtypeStruct((others, section_count, 1, LANES), jnp.float32),
        ],
    )
    figures = lax.all_to_all(
        figures.reshape(others * section_count, 1, LANES),
        MESH_AXES,
        split_axis=0,
        concat_axis=0,
        tiled=True,
    )
    *scaled, clip_tile = on_device(
        functools.partial(scale_kernel, matrix_count),
        place,
        [figures, grad_rows, own_momentum],
        [jax.ShapeDtypeStruct((local_height, width), jnp.bfloat16)] * matrix_count
        + [jax.ShapeDtypeStruct((8, LANES), jnp.float32)],
    )

    pieces = [scaled[0]] + [None] * 3
    for offset in (2, 3, 1):
        pieces[offset] = swapped(scaled[offset], "shard", offset)
    near, side, far = [None] * 4, [None] * 4, [None] * 4
    near[0] = swapped(pieces[0], "tensor", 1)
    side[0] = swapped(pieces[0], "tensor", 2)
    far[0] = swapped(near[0], "tensor", 2)
    near[1] = swapped(pieces[1], "tensor", 1)
    side[1] = swapped(after(pieces[1], near[0]), "tensor", 2)
    far[1] = swapped(side[1], "tensor", 1)
    near[2] = swapped(pieces[2], "tensor", 1)
    side[2] = swapped(after(pieces[2], side[0]), "tensor", 2)
    far[2] = swapped(near[2], "tensor", 2)
    near[3] = swapped(after(pieces[3], near[1]), "tensor", 1)
    side[3] = swapped(after(pieces[3], near[1]), "tensor", 2)
    far[3] = swapped(side[3], "tensor", 1)
    results = orthogonalize([pieces, near, side, far])

    returned = {
        offset: swapped(results[offset], "shard", offset)
        for offset in reversed(range(1, shard_count))
    }
    early = finished((0,), place, [results[0]], weights[0])
    orthogonal_update, new_weights = finished(
        (3, 2, 1), place, [returned[offset] for offset in (3, 2, 1)], weights[0], early
    )
    new_momentum, adam_direction, new_vectors = on_device(
        state_kernel,
        place,
        [
            after(clip_tile, results[0]),
            grad_rows,
            own_momentum,
            vector_whole,
            vectors[0],
            first_moment[0],
            second_moment[0],
        ],
        [jax.ShapeDtypeStruct(own_momentum.shape, jnp.float32)]
        + [jax.ShapeDtypeStruct(vectors.shape[1:], jnp.float32)] * 2,
    )
    return (
        new_momentum[None],
        orthogonal_update[None],
        new_weights[None],
        adam_direction[None],
        new_vectors[None],
    )


def general_device(grad_parts, vector_grads, momentum, weights, vectors, first_moment, second_moment):
    shard_count = lax.axis_size("shard")
    tensor_count = lax.axis_size("tensor")
    section_count = lax.axis_size("section")
    shard_index = lax.axis_index("shard")
    _, matrix_count, local_height, width = momentum.shape
    vector_width = vectors.shape[2]
    own_momentum = momentum[0]

    rows = matrix_count * local_height
    by_target = (
        grad_parts.reshape(matrix_count, shard_count, local_height, width)
        .transpose(1, 0, 2, 3)
        .reshape(shard_count, rows, width)
    )
    vector_line = jnp.broadcast_to(
        vector_grads.reshape(1, 1, width), (shard_count, VECTOR_ROWS, width)
    )
    payload = jnp.concatenate([by_target, vector_line], axis=1)
    arrived = lax.all_to_all(payload, "shard", split_axis=0, concat_axis=0, tiled=True)
    grad_rows = jnp.sum(arrived[:, :rows].astype(jnp.float32), axis=0).reshape(
        matrix_count, local_height, width
    )
    vector_whole = jnp.sum(arrived[:, rows].astype(jnp.float32), axis=0).reshape(
        vectors.shape[1], vector_width * shard_count
    )
    vector_rows = lax.dynamic_slice_in_dim(
        vector_whole, shard_index * vector_width, vector_width, 1
    )

    grad_squares = jnp.sum(grad_rows * grad_rows, axis=(1, 2))
    cross = jnp.sum(grad_rows * own_momentum, axis=(1, 2))
    momentum_squares = jnp.sum(own_momentum * own_momentum, axis=(1, 2))
    own_total = jnp.sum(grad_squares) + jnp.sum(vector_rows * vector_rows)
    same_section = (
        jnp.arange(section_count) == lax.axis_index("section")
    ).astype(jnp.float32)[:, None]
    matrix_figures = jnp.concatenate([grad_squares, cross, momentum_squares])
    line = jnp.concatenate(
        [
            same_section * matrix_figures[None],
            jnp.broadcast_to(own_total, (section_count, 1)),
            jnp.zeros((section_count, 127 - 3 * matrix_count), jnp.float32),
        ],
        axis=1,
    )
    others = shard_count * tensor_count
    figures = jnp.broadcast_to(line[None, :, None, :], (others, section_count, 8, 128)).reshape(
        others * section_count, 8, 128
    )
    figures = lax.all_to_all(figures, MESH_AXES, split_axis=0, concat_axis=0, tiled=True)
    sums = jnp.sum(figures[:, 0, :], axis=0)
    grand_total = sums[3 * matrix_count]
    clip_factor = jnp.minimum(1.0, max_norm / (jnp.sqrt(grand_total) + 1e-06))
    grad_scale = (1.0 + mom_beta) * clip_factor
    momentum_scale = mom_beta * mom_beta
    update_norm = (
        grad_scale * grad_scale * sums[:matrix_count]
        + 2.0 * grad_scale * momentum_scale * sums[matrix_count : 2 * matrix_count]
        + momentum_scale * momentum_scale * sums[2 * matrix_count : 3 * matrix_count]
    )
    update_norm = jnp.maximum(update_norm, 0.0)[:, None, None]

    new_momentum = mom_beta * own_momentum + clip_factor * grad_rows
    nesterov = clip_factor * grad_rows + mom_beta * new_momentum
    scaled = (nesterov / (jnp.sqrt(update_norm) + 1e-07)).astype(jnp.bfloat16)

    owner_count = shard_count // matrix_count
    if owner_count == 1:
        row_block = lax.all_to_all(scaled, "shard", split_axis=0, concat_axis=0, tiled=True)
        row_block = row_block.reshape(shard_count * local_height, width)
    else:
        everything = lax.all_gather(scaled, "shard", axis=1, tiled=True)
        row_block = lax.dynamic_index_in_dim(
            everything, shard_index // owner_count, 0, keepdims=False
        )

    blocks = [row_block]
    for offset in range(1, tensor_count):
        pairs = [(i, i ^ offset) for i in range(tensor_count)]
        blocks.append(lax.ppermute(row_block, "tensor", pairs))
    (own_result,) = orthogonalize([[block] for block in blocks])

    if owner_count == 1:
        own_update = lax.all_to_all(
            own_result.reshape(shard_count, local_height, width),
            "shard",
            split_axis=0,
            concat_axis=0,
            tiled=True,
        )
    else:
        piece_length = local_height * width // owner_count
        split_rows = own_result.reshape(shard_count, owner_count, piece_length)
        returning = lax.dynamic_index_in_dim(
            split_rows, shard_index % owner_count, 1, keepdims=False
        )
        received = lax.all_to_all(returning, "shard", split_axis=0, concat_axis=0, tiled=True)
        own_update = received.reshape(matrix_count, local_height, width)
    orthogonal_update = own_update[None]
    muon_scale = 0.2 * math.sqrt(D)
    new_weights = (
        weights.astype(jnp.float32) * (1.0 - muon_rate * muon_decay)
        - muon_rate * muon_scale * orthogonal_update.astype(jnp.float32)
    ).astype(jnp.bfloat16)
    vector_clipped = clip_factor * vector_rows
    updated_first = 0.9 * first_moment + 0.1 * vector_clipped
    updated_second = 0.999 * second_moment + 0.001 * vector_clipped * vector_clipped
    adam_direction = updated_first / (jnp.sqrt(updated_second) + 1e-08)
    new_vectors = vectors * (1.0 - adam_rate * adam_decay) - adam_rate * adam_direction
    return (new_momentum[None], orthogonal_update, new_weights, adam_direction, new_vectors)


def solution(mesh):
    in_specs = (
        P("shard", "section", None, "tensor", None),
        P("shard", "section", None, "tensor"),
        P("section", None, ("tensor", "shard"), None),
        P("section", None, ("tensor", "shard"), None),
        P("section", None, ("tensor", "shard")),
        P("section", None, ("tensor", "shard")),
        P("section", None, ("tensor", "shard")),
    )
    out_specs = (
        P("section", None, ("tensor", "shard"), None),
        P("section", None, ("tensor", "shard"), None),
        P("section", None, ("tensor", "shard"), None),
        P("section", None, ("tensor", "shard")),
        P("section", None, ("tensor", "shard")),
    )
    return jax.shard_map(
        per_device, mesh=mesh, in_specs=in_specs, out_specs=out_specs, check_vma=False
    )
```

profile of v0, /device:TPU:0, one launch (start us, length us, event | category | flops | bytes accessed | tf_op | source)
XLA Modules:
  0.0 116.2 jit_solution(6293286012957362124)
XLA Ops:
  0.6 0.0 copy-start
  0.7 0.0 copy-start.2
  0.7 1.7 %copy-done.2 = bf16[1,1,4,256,1024]{4,3,2,1,0:T(8,128)(2,1)S(1)} copy-done((bf16[1,1,4,256,1024]{4,3,2,1,0:T(8,128)(2,1)S(1)}, bf16[1,1,4,256,1024]{4,3,2,1,0:T(8,128)(2,1)}, u32[]{:S(2)}) %copy-start.2) | copy-done | bytes 2097176
  2.3 0.0 copy-start.6
  2.3 0.7 shard_map.110
  3.1 5.1 %collective-permute-start = (bf16[4,64,1024]{2,1,0:T(8,128)(2,1)S(1)}, bf16[4,64,1024]{2,1,0:T(8,128)(2,1)S(1)}, u32[]{:S(2)}, u32[]{:S(2)}) collective-permute-start(bf16[4,64,1024]{2,1,0:T(8,128)(2,1)S(1)} %get-tuple-element.32), channel_id=1, source_target_pairs={{0,24},{8,16},{16,8},{24,0},{1,25},{9,17},{17,9},{25,1},{2,26},{10... | collective-permute-start | bytes 1572872 | tf_op jit(solution)/shard_map/ppermute | solution.py:288
  8.2 0.0 collective-permute-start.1
  8.2 0.6 collective-permute-start.2
  8.8 0.0 copy-done.6
  8.8 44.3 %all_to_all.10.refs_4_ = bf16[4,4,256]{2,1,0:T(4,128)(2,1)S(1)} all-to-all(bf16[4,4,256]{2,1,0:T(4,128)(2,1)S(1)} %broadcast_in_dim.28), channel_id=1, replica_groups=mesh['shard'=4,'tensor'=4,'section'=2] {'shard'}, dimensions={0} | all-to-all | bytes 16384 | tf_op jit(solution)/shard_map/all_to_all | solution.py:317
  53.1 0.0 collective-permute-done.refs_0_
  53.2 0.0 collective-permute-done.1.refs_1_
  53.2 0.0 collective-permute-done.2.refs_2_
  53.2 0.0 copy-done
  53.2 1.3 %shard_map.111 = (f32[4,64,1024]{2,1,0:T(8,128)S(1)}, f32[4,256]{1,0:T(4,128)S(1)}, f32[16,2,1,128]{3,2,1,0:T(1,128)S(1)}) custom-call(s32[5]{0:T(128)S(1)} %compare_select_fusion.place_ref, bf16[4,64,1024]{2,1,0:T(8,128)(2,1)S(1)} %collective-permute-done.refs_0_, bf16[4,64,1024]{2,1,0:T(8,128)(2,1)S(1)} %collective-permute-done.1.refs_1_, ...), custom_call_target="tpu_custom_call" | custom-call | tf_op jit(solution)/shard_map/pallas_call | solution.py:277
  54.5 11.7 %all_to_all.11.figures_ref = f32[32,1,128]{2,1,0:T(1,128)S(1)} all-to-all(f32[32,1,128]{2,1,0:T(1,128)S(1)} %bitcast.19), channel_id=1, replica_groups=mesh['shard'=4,'tensor'=4,'section'=2] {'shard','tensor','section'}, dimensions={0} | all-to-all | bytes 32768 | tf_op jit(solution)/shard_map/all_to_all | solution.py:336
  66.2 0.0 copy-start.1
  66.2 0.0 copy-start.3
  66.2 0.0 copy-start.4
  66.2 1.0 shard_map.112
  67.2 0.6 collective-permute-start.3
  67.9 0.6 collective-permute-start.4
  68.4 0.5 collective-permute-start.10
  69.0 0.6 collective-permute-start.6
  69.6 3.3 %collective-permute-start.5 = (bf16[64,1024]{1,0:T(8,128)(2,1)S(1)}, bf16[64,1024]{1,0:T(8,128)(2,1)S(1)}, u32[]{:S(2)}, u32[]{:S(2)}) collective-permute-start(bf16[64,1024]{1,0:T(8,128)(2,1)S(1)} %get-tuple-element.42), channel_id=1, source_target_pairs={{0,24},{8,16},{16,8},{24,0},{1,25},{9,17},{17,9},{25,1},{2,26},{10... | collective-permute-start | bytes 393224 | tf_op jit(solution)/shard_map/ppermute | solution.py:288
  72.9 1.3 %collective-permute-done.3.refs_1_ = bf16[64,1024]{1,0:T(8,128)(2,1)S(1)} collective-permute-done((bf16[64,1024]{1,0:T(8,128)(2,1)S(1)}, bf16[64,1024]{1,0:T(8,128)(2,1)S(1)}, u32[]{:S(2)}, u32[]{:S(2)}) %collective-permute-start.3) | collective-permute-done | bytes 131104 | tf_op jit(solution)/shard_map/ppermute | solution.py:288
  74.1 0.6 collective-permute-start.7
  74.8 5.8 %collective-permute-done.4.refs_2_ = bf16[64,1024]{1,0:T(8,128)(2,1)S(1)} collective-permute-done((bf16[64,1024]{1,0:T(8,128)(2,1)S(1)}, bf16[64,1024]{1,0:T(8,128)(2,1)S(1)}, u32[]{:S(2)}, u32[]{:S(2)}) %collective-permute-start.4) | collective-permute-done | bytes 131104 | tf_op jit(solution)/shard_map/ppermute | solution.py:288
  80.6 0.0 collective-permute-done.10.refs_8_
  80.6 0.5 collective-permute-start.12
  81.1 0.0 collective-permute-done.6.refs_4_
  81.1 1.5 %collective-permute-start.11 = (bf16[64,1024]{1,0:T(8,128)(2,1)S(1)}, bf16[64,1024]{1,0:T(8,128)(2,1)S(1)}, u32[]{:S(2)}, u32[]{:S(2)}) collective-permute-start(bf16[64,1024]{1,0:T(8,128)(2,1)S(1)} %collective-permute-done.3.refs_1_), channel_id=1, source_target_pairs={{0,4},{2,6},{4,0},{6,2},{1,5},{3,7},{5,1},{7,3},{8,12},{10,14},{12... | collective-permute-start | bytes 393224 | tf_op jit(solution)/shard_map/ppermute | solution.py:288
  82.6 0.5 collective-permute-start.8
  83.1 0.0 collective-permute-done.5.refs_3_
  83.1 0.0 collective-permute-done.7.refs_5_
  83.1 0.6 collective-permute-start.13
  83.7 1.4 %collective-permute-start.14 = (bf16[64,1024]{1,0:T(8,128)(2,1)S(1)}, bf16[64,1024]{1,0:T(8,128)(2,1)S(1)}, u32[]{:S(2)}, u32[]{:S(2)}) collective-permute-start(bf16[64,1024]{1,0:T(8,128)(2,1)S(1)} %collective-permute-done.6.refs_4_), channel_id=1, source_target_pairs={{0,4},{2,6},{4,0},{6,2},{1,5},{3,7},{5,1},{7,3},{8,12},{10,14},{12... | collective-permute-start | bytes 393224 | tf_op jit(solution)/shard_map/ppermute | solution.py:288
  85.2 3.3 %collective-permute-done.8.refs_6_ = bf16[64,1024]{1,0:T(8,128)(2,1)S(1)} collective-permute-done((bf16[64,1024]{1,0:T(8,128)(2,1)S(1)}, bf16[64,1024]{1,0:T(8,128)(2,1)S(1)}, u32[]{:S(2)}, u32[]{:S(2)}) %collective-permute-start.8) | collective-permute-done | bytes 131104 | tf_op jit(solution)/shard_map/ppermute | solution.py:288
  88.5 0.9 collective-permute-start.9
  89.4 0.0 collective-permute-done.12.refs_10_
  89.4 0.7 collective-permute-start.16
  90.2 0.0 collective-permute-done.11.refs_9_
  90.2 1.4 %collective-permute-start.15 = (bf16[64,1024]{1,0:T(8,128)(2,1)S(1)}, bf16[64,1024]{1,0:T(8,128)(2,1)S(1)}, u32[]{:S(2)}, u32[]{:S(2)}) collective-permute-start(bf16[64,1024]{1,0:T(8,128)(2,1)S(1)} %collective-permute-done.11.refs_9_), channel_id=1, source_target_pairs={{0,2},{2,0},{4,6},{6,4},{1,3},{3,1},{5,7},{7,5},{8,10},{10,8},{12,... | collective-permute-start | bytes 393224 | tf_op jit(solution)/shard_map/ppermute | solution.py:288
  91.5 0.0 collective-permute-done.13.refs_11_
  91.5 0.7 collective-permute-start.17
  92.2 0.0 collective-permute-done.14.refs_12_
  92.2 2.2 %collective-permute-done.16.refs_14_ = bf16[64,1024]{1,0:T(8,128)(2,1)S(1)} collective-permute-done((bf16[64,1024]{1,0:T(8,128)(2,1)S(1)}, bf16[64,1024]{1,0:T(8,128)(2,1)S(1)}, u32[]{:S(2)}, u32[]{:S(2)}) %collective-permute-start.16) | collective-permute-done | bytes 131104 | tf_op jit(solution)/shard_map/ppermute | solution.py:288
  94.4 0.0 collective-permute-done.9.refs_7_
  94.4 0.7 collective-permute-done.15.refs_13_
  95.1 1.4 %collective-permute-done.17.refs_15_ = bf16[64,1024]{1,0:T(8,128)(2,1)S(1)} collective-permute-done((bf16[64,1024]{1,0:T(8,128)(2,1)S(1)}, bf16[64,1024]{1,0:T(8,128)(2,1)S(1)}, u32[]{:S(2)}, u32[]{:S(2)}) %collective-permute-start.17) | collective-permute-done | bytes 131104 | tf_op jit(solution)/shard_map/ppermute | solution.py:288
  96.5 8.6 %shard_map.113 = (bf16[64,1024]{1,0:T(8,128)(2,1)S(1)}, bf16[64,1024]{1,0:T(8,128)(2,1)S(1)}, bf16[64,1024]{1,0:T(8,128)(2,1)S(1)}, bf16[64,1024]{1,0:T(8,128)(2,1)S(1)}) custom-call(bf16[64,1024]{1,0:T(8,128)(2,1)S(1)} %get-tuple-element.39.refs_0_, bf16[64,1024]{1,0:T(8,128)(2,1)S(1)} %collective-permute-done.3.refs_1_, ...), custom_call_target="tpu_custom_call" | custom-call | tf_op jit(solution)/shard_map/pallas_call | solution.py:91
  105.1 1.1 collective-permute-start.18
  106.2 0.0 collective-permute-start.19
  106.2 3.4 %collective-permute-start.20 = (bf16[64,1024]{1,0:T(8,128)(2,1)S(1)}, bf16[64,1024]{1,0:T(8,128)(2,1)S(1)}, u32[]{:S(2)}, u32[]{:S(2)}) collective-permute-start(bf16[64,1024]{1,0:T(8,128)(2,1)S(1)} %get-tuple-element.52), channel_id=1, source_target_pairs={{0,8},{8,0},{16,24},{24,16},{1,9},{9,1},{17,25},{25,17},{2,10},{10... | collective-permute-start | bytes 393224 | tf_op jit(solution)/shard_map/ppermute | solution.py:288
  109.6 0.0 copy-done.1
  109.6 1.3 %shard_map.115 = (bf16[4,64,1024]{2,1,0:T(8,128)(2,1)}, bf16[4,64,1024]{2,1,0:T(8,128)(2,1)}) custom-call(s32[5]{0:T(128)S(1)} %compare_select_fusion.place_ref, bf16[64,1024]{1,0:T(8,128)(2,1)S(1)} %get-tuple-element.46.refs_0_, bf16[4,64,1024]{2,1,0:T(8,128)(2,1)S(1)} %bitcast.16), custom_call_target="tpu_custom_call" | custom-call | tf_op jit(solution)/shard_map/pallas_call | solution.py:231
  110.8 0.0 copy-done.3
  110.8 0.0 copy-done.4
  110.9 0.0 copy-done.5
  110.9 1.8 %shard_map.114 = (f32[4,64,1024]{2,1,0:T(8,128)}, f32[4,64]{1,0:T(4,128)}, f32[4,64]{1,0:T(4,128)}) custom-call(s32[5]{0:T(128)S(1)} %compare_select_fusion.place_ref, f32[8,128]{1,0:T(8,128)S(1)} %get-tuple-element.47.clip_ref, f32[4,64,1024]{2,1,0:T(8,128)S(1)} %get-tuple-element.37.grad_ref, f32[4,64,1024]{2,1,0:T(8,128)S(1)} %bitcast.15, ...), custom_call_target="tpu_custom_call" | custom-call | tf_op jit(solution)/shard_map/pallas_call | solution.py:277
  112.7 0.0 collective-permute-done.18.refs_0_
  112.7 2.0 %collective-permute-done.19.refs_1_ = bf16[64,1024]{1,0:T(8,128)(2,1)S(1)} collective-permute-done((bf16[64,1024]{1,0:T(8,128)(2,1)S(1)}, bf16[64,1024]{1,0:T(8,128)(2,1)S(1)}, u32[]{:S(2)}, u32[]{:S(2)}) %collective-permute-start.19) | collective-permute-done | bytes 131104 | tf_op jit(solution)/shard_map/ppermute | solution.py:288
  114.7 0.0 collective-permute-done.20.refs_2_
  114.7 1.5 %shard_map.116 = (bf16[4,64,1024]{2,1,0:T(8,128)(2,1)}, bf16[4,64,1024]{2,1,0:T(8,128)(2,1)}) custom-call(s32[5]{0:T(128)S(1)} %compare_select_fusion.place_ref, bf16[64,1024]{1,0:T(8,128)(2,1)S(1)} %collective-permute-done.18.refs_0_, bf16[64,1024]{1,0:T(8,128)(2,1)S(1)} %collective-permute-done.19.refs_1_, ...), custom_call_target="tpu_custom_call", output_to_operand_aliasing={{0}: (5, {}), {1}: (6, {})} | custom-call | tf_op jit(solution)/shard_map/pallas_call | solution.py:231
  (3 shorter events, 0.0 us)
Async XLA Ops:
  0.6 52.5 %copy-start = (f32[1,4,64,1024]{3,2,1,0:T(8,128)S(1)}, f32[1,4,64,1024]{3,2,1,0:T(8,128)}, u32[]{:S(2)}) copy-start(f32[1,4,64,1024]{3,2,1,0:T(8,128)} %param.9) | copy-start | bytes 3145732
  0.7 1.7 %copy-start.2 = (bf16[1,1,4,256,1024]{4,3,2,1,0:T(8,128)(2,1)S(1)}, bf16[1,1,4,256,1024]{4,3,2,1,0:T(8,128)(2,1)}, u32[]{:S(2)}) copy-start(bf16[1,1,4,256,1024]{4,3,2,1,0:T(8,128)(2,1)} %param.7) | copy-start | bytes 6291460
  2.3 6.5 %copy-start.6 = (bf16[1,1,4,256]{3,2,1,0:T(4,128)(2,1)S(1)}, bf16[1,1,4,256]{3,2,1,0:T(4,128)(2,1)}, u32[]{:S(2)}) copy-start(bf16[1,1,4,256]{3,2,1,0:T(4,128)(2,1)} %param.8) | copy-start | bytes 6148
  3.1 50.1 %collective-permute-start = (bf16[4,64,1024]{2,1,0:T(8,128)(2,1)S(1)}, bf16[4,64,1024]{2,1,0:T(8,128)(2,1)S(1)}, u32[]{:S(2)}, u32[]{:S(2)}) collective-permute-start(bf16[4,64,1024]{2,1,0:T(8,128)(2,1)S(1)} %get-tuple-element.32), channel_id=1, source_target_pairs={{0,24},{8,16},{16,8},{24,0},{1,25},{9,17},{17,9},{25,1},{2,26},{10... | collective-permute-start | bytes 1572872 | tf_op jit(solution)/shard_map/ppermute | solution.py:288
  8.2 45.0 %collective-permute-start.1 = (bf16[4,64,1024]{2,1,0:T(8,128)(2,1)S(1)}, bf16[4,64,1024]{2,1,0:T(8,128)(2,1)S(1)}, u32[]{:S(2)}, u32[]{:S(2)}) collective-permute-start(bf16[4,64,1024]{2,1,0:T(8,128)(2,1)S(1)} %get-tuple-element.33), channel_id=1, source_target_pairs={{0,16},{8,24},{16,0},{24,8},{1,17},{9,25},{17,1},{25,9},{2,18},{10... | collective-permute-start | bytes 1572872 | tf_op jit(solution)/shard_map/ppermute | solution.py:288
  8.2 45.0 %collective-permute-start.2 = (bf16[4,64,1024]{2,1,0:T(8,128)(2,1)S(1)}, bf16[4,64,1024]{2,1,0:T(8,128)(2,1)S(1)}, u32[]{:S(2)}, u32[]{:S(2)}) collective-permute-start(bf16[4,64,1024]{2,1,0:T(8,128)(2,1)S(1)} %get-tuple-element.34), channel_id=1, source_target_pairs={{0,8},{8,0},{16,24},{24,16},{1,9},{9,1},{17,25},{25,17},{2,10},{10... | collective-permute-start | bytes 1572872 | tf_op jit(solution)/shard_map/ppermute | solution.py:288
  66.2 43.4 %copy-start.1 = (bf16[1,4,64,1024]{3,2,1,0:T(8,128)(2,1)S(1)}, bf16[1,4,64,1024]{3,2,1,0:T(8,128)(2,1)}, u32[]{:S(2)}) copy-start(bf16[1,4,64,1024]{3,2,1,0:T(8,128)(2,1)} %param.10) | copy-start | bytes 1572868
  66.2 44.6 %copy-start.3 = (f32[1,4,64]{2,1,0:T(4,128)S(1)}, f32[1,4,64]{2,1,0:T(4,128)}, u32[]{:S(2)}) copy-start(f32[1,4,64]{2,1,0:T(4,128)} %param.11) | copy-start | bytes 3076
  66.2 44.6 %copy-start.4 = (f32[1,4,64]{2,1,0:T(4,128)S(1)}, f32[1,4,64]{2,1,0:T(4,128)}, u32[]{:S(2)}) copy-start(f32[1,4,64]{2,1,0:T(4,128)} %param.12) | copy-start | bytes 3076
  66.2 44.6 %copy-start.5 = (f32[1,4,64]{2,1,0:T(4,128)S(1)}, f32[1,4,64]{2,1,0:T(4,128)}, u32[]{:S(2)}) copy-start(f32[1,4,64]{2,1,0:T(4,128)} %param.13) | copy-start | bytes 3076
  67.2 6.9 %collective-permute-start.3 = (bf16[64,1024]{1,0:T(8,128)(2,1)S(1)}, bf16[64,1024]{1,0:T(8,128)(2,1)S(1)}, u32[]{:S(2)}, u32[]{:S(2)}) collective-permute-start(bf16[64,1024]{1,0:T(8,128)(2,1)S(1)} %get-tuple-element.40), channel_id=1, source_target_pairs={{0,8},{8,0},{16,24},{24,16},{1,9},{9,1},{17,25},{25,17},{2,10},{10... | collective-permute-start | bytes 393224 | tf_op jit(solution)/shard_map/ppermute | solution.py:288
  67.9 12.7 %collective-permute-start.4 = (bf16[64,1024]{1,0:T(8,128)(2,1)S(1)}, bf16[64,1024]{1,0:T(8,128)(2,1)S(1)}, u32[]{:S(2)}, u32[]{:S(2)}) collective-permute-start(bf16[64,1024]{1,0:T(8,128)(2,1)S(1)} %get-tuple-element.41), channel_id=1, source_target_pairs={{0,16},{8,24},{16,0},{24,8},{1,17},{9,25},{17,1},{25,9},{2,18},{10... | collective-permute-start | bytes 393224 | tf_op jit(solution)/shard_map/ppermute | solution.py:288
  68.4 12.1 %collective-permute-start.10 = (bf16[64,1024]{1,0:T(8,128)(2,1)S(1)}, bf16[64,1024]{1,0:T(8,128)(2,1)S(1)}, u32[]{:S(2)}, u32[]{:S(2)}) collective-permute-start(bf16[64,1024]{1,0:T(8,128)(2,1)S(1)} %get-tuple-element.39.refs_0_), channel_id=1, source_target_pairs={{0,4},{2,6},{4,0},{6,2},{1,5},{3,7},{5,1},{7,3},{8,12},{10,14},{12... | collective-permute-start | bytes 393224 | tf_op jit(solution)/shard_map/ppermute | solution.py:288
  69.0 12.1 %collective-permute-start.6 = (bf16[64,1024]{1,0:T(8,128)(2,1)S(1)}, bf16[64,1024]{1,0:T(8,128)(2,1)S(1)}, u32[]{:S(2)}, u32[]{:S(2)}) collective-permute-start(bf16[64,1024]{1,0:T(8,128)(2,1)S(1)} %get-tuple-element.39.refs_0_), channel_id=1, source_target_pairs={{0,2},{2,0},{4,6},{6,4},{1,3},{3,1},{5,7},{7,5},{8,10},{10,8},{12,... | collective-permute-start | bytes 393224 | tf_op jit(solution)/shard_map/ppermute | solution.py:288
  69.6 13.6 %collective-permute-start.5 = (bf16[64,1024]{1,0:T(8,128)(2,1)S(1)}, bf16[64,1024]{1,0:T(8,128)(2,1)S(1)}, u32[]{:S(2)}, u32[]{:S(2)}) collective-permute-start(bf16[64,1024]{1,0:T(8,128)(2,1)S(1)} %get-tuple-element.42), channel_id=1, source_target_pairs={{0,24},{8,16},{16,8},{24,0},{1,25},{9,17},{17,9},{25,1},{2,26},{10... | collective-permute-start | bytes 393224 | tf_op jit(solution)/shard_map/ppermute | solution.py:288
  74.1 9.0 %collective-permute-start.7 = (bf16[64,1024]{1,0:T(8,128)(2,1)S(1)}, bf16[64,1024]{1,0:T(8,128)(2,1)S(1)}, u32[]{:S(2)}, u32[]{:S(2)}) collective-permute-start(bf16[64,1024]{1,0:T(8,128)(2,1)S(1)} %collective-permute-done.3.refs_1_), channel_id=1, source_target_pairs={{0,2},{2,0},{4,6},{6,4},{1,3},{3,1},{5,7},{7,5},{8,10},{10,8},{12,... | collective-permute-start | bytes 393224 | tf_op jit(solution)/shard_map/ppermute | solution.py:288
  80.6 8.8 %collective-permute-start.12 = (bf16[64,1024]{1,0:T(8,128)(2,1)S(1)}, bf16[64,1024]{1,0:T(8,128)(2,1)S(1)}, u32[]{:S(2)}, u32[]{:S(2)}) collective-permute-start(bf16[64,1024]{1,0:T(8,128)(2,1)S(1)} %collective-permute-done.4.refs_2_), channel_id=1, source_target_pairs={{0,4},{2,6},{4,0},{6,2},{1,5},{3,7},{5,1},{7,3},{8,12},{10,14},{12... | collective-permute-start | bytes 393224 | tf_op jit(solution)/shard_map/ppermute | solution.py:288
  81.1 9.1 %collective-permute-start.11 = (bf16[64,1024]{1,0:T(8,128)(2,1)S(1)}, bf16[64,1024]{1,0:T(8,128)(2,1)S(1)}, u32[]{:S(2)}, u32[]{:S(2)}) collective-permute-start(bf16[64,1024]{1,0:T(8,128)(2,1)S(1)} %collective-permute-done.3.refs_1_), channel_id=1, source_target_pairs={{0,4},{2,6},{4,0},{6,2},{1,5},{3,7},{5,1},{7,3},{8,12},{10,14},{12... | collective-permute-start | bytes 393224 | tf_op jit(solution)/shard_map/ppermute | solution.py:288
  82.6 5.9 %collective-permute-start.8 = (bf16[64,1024]{1,0:T(8,128)(2,1)S(1)}, bf16[64,1024]{1,0:T(8,128)(2,1)S(1)}, u32[]{:S(2)}, u32[]{:S(2)}) collective-permute-start(bf16[64,1024]{1,0:T(8,128)(2,1)S(1)} %collective-permute-done.4.refs_2_), channel_id=1, source_target_pairs={{0,2},{2,0},{4,6},{6,4},{1,3},{3,1},{5,7},{7,5},{8,10},{10,8},{12,... | collective-permute-start | bytes 393224 | tf_op jit(solution)/shard_map/ppermute | solution.py:288
  83.1 8.4 %collective-permute-start.13 = (bf16[64,1024]{1,0:T(8,128)(2,1)S(1)}, bf16[64,1024]{1,0:T(8,128)(2,1)S(1)}, u32[]{:S(2)}, u32[]{:S(2)}) collective-permute-start(bf16[64,1024]{1,0:T(8,128)(2,1)S(1)} %collective-permute-done.5.refs_3_), channel_id=1, source_target_pairs={{0,4},{2,6},{4,0},{6,2},{1,5},{3,7},{5,1},{7,3},{8,12},{10,14},{12... | collective-permute-start | bytes 393224 | tf_op jit(solution)/shard_map/ppermute | solution.py:288
  83.7 8.5 %collective-permute-start.14 = (bf16[64,1024]{1,0:T(8,128)(2,1)S(1)}, bf16[64,1024]{1,0:T(8,128)(2,1)S(1)}, u32[]{:S(2)}, u32[]{:S(2)}) collective-permute-start(bf16[64,1024]{1,0:T(8,128)(2,1)S(1)} %collective-permute-done.6.refs_4_), channel_id=1, source_target_pairs={{0,4},{2,6},{4,0},{6,2},{1,5},{3,7},{5,1},{7,3},{8,12},{10,14},{12... | collective-permute-start | bytes 393224 | tf_op jit(solution)/shard_map/ppermute | solution.py:288
  88.5 5.9 %collective-permute-start.9 = (bf16[64,1024]{1,0:T(8,128)(2,1)S(1)}, bf16[64,1024]{1,0:T(8,128)(2,1)S(1)}, u32[]{:S(2)}, u32[]{:S(2)}) collective-permute-start(bf16[64,1024]{1,0:T(8,128)(2,1)S(1)} %collective-permute-done.5.refs_3_), channel_id=1, source_target_pairs={{0,2},{2,0},{4,6},{6,4},{1,3},{3,1},{5,7},{7,5},{8,10},{10,8},{12,... | collective-permute-start | bytes 393224 | tf_op jit(solution)/shard_map/ppermute | solution.py:288
  89.4 5.0 %collective-permute-start.16 = (bf16[64,1024]{1,0:T(8,128)(2,1)S(1)}, bf16[64,1024]{1,0:T(8,128)(2,1)S(1)}, u32[]{:S(2)}, u32[]{:S(2)}) collective-permute-start(bf16[64,1024]{1,0:T(8,128)(2,1)S(1)} %collective-permute-done.8.refs_6_), channel_id=1, source_target_pairs={{0,4},{2,6},{4,0},{6,2},{1,5},{3,7},{5,1},{7,3},{8,12},{10,14},{12... | collective-permute-start | bytes 393224 | tf_op jit(solution)/shard_map/ppermute | solution.py:288
  90.2 5.0 %collective-permute-start.15 = (bf16[64,1024]{1,0:T(8,128)(2,1)S(1)}, bf16[64,1024]{1,0:T(8,128)(2,1)S(1)}, u32[]{:S(2)}, u32[]{:S(2)}) collective-permute-start(bf16[64,1024]{1,0:T(8,128)(2,1)S(1)} %collective-permute-done.11.refs_9_), channel_id=1, source_target_pairs={{0,2},{2,0},{4,6},{6,4},{1,3},{3,1},{5,7},{7,5},{8,10},{10,8},{12,... | collective-permute-start | bytes 393224 | tf_op jit(solution)/shard_map/ppermute | solution.py:288
  91.5 5.0 %collective-permute-start.17 = (bf16[64,1024]{1,0:T(8,128)(2,1)S(1)}, bf16[64,1024]{1,0:T(8,128)(2,1)S(1)}, u32[]{:S(2)}, u32[]{:S(2)}) collective-permute-start(bf16[64,1024]{1,0:T(8,128)(2,1)S(1)} %collective-permute-done.13.refs_11_), channel_id=1, source_target_pairs={{0,2},{2,0},{4,6},{6,4},{1,3},{3,1},{5,7},{7,5},{8,10},{10,8},{12,... | collective-permute-start | bytes 393224 | tf_op jit(solution)/shard_map/ppermute | solution.py:288
  105.1 7.6 %collective-permute-start.18 = (bf16[64,1024]{1,0:T(8,128)(2,1)S(1)}, bf16[64,1024]{1,0:T(8,128)(2,1)S(1)}, u32[]{:S(2)}, u32[]{:S(2)}) collective-permute-start(bf16[64,1024]{1,0:T(8,128)(2,1)S(1)} %get-tuple-element.50), channel_id=1, source_target_pairs={{0,24},{8,16},{16,8},{24,0},{1,25},{9,17},{17,9},{25,1},{2,26},{10... | collective-permute-start | bytes 393224 | tf_op jit(solution)/shard_map/ppermute | solution.py:288
  106.2 8.6 %collective-permute-start.19 = (bf16[64,1024]{1,0:T(8,128)(2,1)S(1)}, bf16[64,1024]{1,0:T(8,128)(2,1)S(1)}, u32[]{:S(2)}, u32[]{:S(2)}) collective-permute-start(bf16[64,1024]{1,0:T(8,128)(2,1)S(1)} %get-tuple-element.51), channel_id=1, source_target_pairs={{0,16},{8,24},{16,0},{24,8},{1,17},{9,25},{17,1},{25,9},{2,18},{10... | collective-permute-start | bytes 393224 | tf_op jit(solution)/shard_map/ppermute | solution.py:288
  106.2 8.6 %collective-permute-start.20 = (bf16[64,1024]{1,0:T(8,128)(2,1)S(1)}, bf16[64,1024]{1,0:T(8,128)(2,1)S(1)}, u32[]{:S(2)}, u32[]{:S(2)}) collective-permute-start(bf16[64,1024]{1,0:T(8,128)(2,1)S(1)} %get-tuple-element.52), channel_id=1, source_target_pairs={{0,8},{8,0},{16,24},{24,16},{1,9},{9,1},{17,25},{25,17},{2,10},{10... | collective-permute-start | bytes 393224 | tf_op jit(solution)/shard_map/ppermute | solution.py:288
where the time goes:
time: 116 us
  blocking collectives  56 us (48%)
  starting transfers between devices  24.7 us (21%)
  waiting for transfers between devices  16.8 us (14%)
  Pallas kernels  16.2 us (14%)
  local copies, waits for them, and re-layouts  1.7 us (1%)
    all_to_all x1, blocking collectives, per_device(): lax.all_to_all(jnp.broadcast_to(vector_grads[0], (shard_count, vector_cou...  44.3 us
    ppermute x21, starting transfers between devices, swapped(): return lax.ppermute(array, axis, pairs)  24.7 us
    ppermute x21, waiting for transfers between devices, swapped(): return lax.ppermute(array, axis, pairs)  16.8 us
    all_to_all x1, blocking collectives, per_device(): lax.all_to_all(figures.reshape(others * section_count, 1, LANES), MESH_AX...  11.7 us
    pallas_call x1, Pallas kernels, orthogonalize(): pl.pallas_call(functools.partial(orthogonalize_kernel, count, pieces), ou...  8.55 us
    pallas_call x3, Pallas kernels, on_device(): pl.pallas_call(kernel, out_shape=out_shape, in_specs=[pl.BlockSpec(memory...  4.2 us
    pallas_call x2, Pallas kernels, finished(): pl.pallas_call(functools.partial(end_kernel, offsets), out_shape=[jax.Sha...  2.74 us
  transfers between devices with their start and end apart: 21, of which 7 were waited for; matrix products, arithmetic and copies ran while one was open for 0% of the time, Pallas kernels for 3%

commit v1 on v0

--- a/solution.py
+++ b/solution.py
@@ -350,20 +350,21 @@
 
     pieces = [scaled[0]] + [None] * 3
     for offset in (2, 3, 1):
-        pieces[offset] = swapped(scaled[offset], "shard", offset)
+        ready = after(scaled[offset], pieces[2]) if offset == 3 else scaled[offset]
+        pieces[offset] = swapped(ready, "shard", offset)
     near, side, far = [None] * 4, [None] * 4, [None] * 4
     near[0] = swapped(pieces[0], "tensor", 1)
     side[0] = swapped(pieces[0], "tensor", 2)
     far[0] = swapped(near[0], "tensor", 2)
     near[1] = swapped(pieces[1], "tensor", 1)
-    side[1] = swapped(after(pieces[1], near[0]), "tensor", 2)
+    side[1] = swapped(pieces[1], "tensor", 2)
     far[1] = swapped(side[1], "tensor", 1)
     near[2] = swapped(pieces[2], "tensor", 1)
-    side[2] = swapped(after(pieces[2], side[0]), "tensor", 2)
+    side[2] = swapped(pieces[2], "tensor", 2)
     far[2] = swapped(near[2], "tensor", 2)
-    near[3] = swapped(after(pieces[3], near[1]), "tensor", 1)
-    side[3] = swapped(after(pieces[3], near[1]), "tensor", 2)
-    far[3] = swapped(side[3], "tensor", 1)
+    near[3] = swapped(pieces[3], "tensor", 1)
+    side[3] = swapped(pieces[3], "tensor", 2)
+    far[3] = swapped(pieces[3], "tensor", 3)
     results = orthogonalize([pieces, near, side, far])
 
     returned = {

time: 116 us -> 116 us (level)
  starting transfers between devices: 24.7 us -> 22.7 us
  waiting for transfers between devices: 16.8 us -> 18.3 us
    ppermute x21, starting transfers between devices: 24.7 us -> 22.7 us  [swapped(): return lax.ppermute(array, axis, pairs)]
    ppermute x21, waiting for transfers between devices: 16.8 us -> 18.3 us  [swapped(): return lax.ppermute(array, axis, pairs)]
  transfers between devices with their start and end apart: 21 -> 21, of which waited for: 7 -> 10; matrix products, arithmetic and copies ran while one was open for 0% -> 0% of each run, Pallas kernels for 3% -> 3%
where the time goes in v1:
time: 116 us
  blocking collectives  56 us (48%)
  starting transfers between devices  22.7 us (20%)
  waiting for transfers between devices  18.3 us (16%)
  Pallas kernels  16.2 us (14%)
  local copies, waits for them, and re-layouts  1.7 us (1%)
    all_to_all x1, blocking collectives, per_device(): lax.all_to_all(jnp.broadcast_to(vector_grads[0], (shard_count, vector_cou...  44.3 us
    ppermute x21, starting transfers between devices, swapped(): return lax.ppermute(array, axis, pairs)  22.7 us
    ppermute x21, waiting for transfers between devices, swapped(): return lax.ppermute(array, axis, pairs)  18.3 us
    all_to_all x1, blocking collectives, per_device(): lax.all_to_all(figures.reshape(others * section_count, 1, LANES), MESH_AX...  11.7 us
    pallas_call x1, Pallas kernels, orthogonalize(): pl.pallas_call(functools.partial(orthogonalize_kernel, count, pieces), ou...  8.55 us
    pallas_call x3, Pallas kernels, on_device(): pl.pallas_call(kernel, out_shape=out_shape, in_specs=[pl.BlockSpec(memory...  4.2 us
    pallas_call x2, Pallas kernels, finished(): pl.pallas_call(functools.partial(end_kernel, offsets), out_shape=[jax.Sha...  2.74 us
  transfers between devices with their start and end apart: 21, of which 10 were waited for; matrix products, arithmetic and copies ran while one was open for 0% of the time, Pallas kernels for 3%

profile of v1, /device:TPU:0, one launch (start us, length us, event | category | flops | bytes accessed | tf_op | source)
XLA Modules:
  0.0 115.7 jit_solution(2655634917072609058)
XLA Ops:
  0.6 0.0 copy-start
  0.7 0.0 copy-start.2
  0.7 1.7 %copy-done.2 = bf16[1,1,4,256,1024]{4,3,2,1,0:T(8,128)(2,1)S(1)} copy-done((bf16[1,1,4,256,1024]{4,3,2,1,0:T(8,128)(2,1)S(1)}, bf16[1,1,4,256,1024]{4,3,2,1,0:T(8,128)(2,1)}, u32[]{:S(2)}) %copy-start.2) | copy-done | bytes 2097176
  2.3 0.0 copy-start.6
  2.3 0.7 shard_map.110
  3.1 5.1 %collective-permute-start = (bf16[4,64,1024]{2,1,0:T(8,128)(2,1)S(1)}, bf16[4,64,1024]{2,1,0:T(8,128)(2,1)S(1)}, u32[]{:S(2)}, u32[]{:S(2)}) collective-permute-start(bf16[4,64,1024]{2,1,0:T(8,128)(2,1)S(1)} %get-tuple-element.30), channel_id=1, source_target_pairs={{0,24},{8,16},{16,8},{24,0},{1,25},{9,17},{17,9},{25,1},{2,26},{10... | collective-permute-start | bytes 1572872 | tf_op jit(solution)/shard_map/ppermute | solution.py:288
  8.2 0.0 collective-permute-start.1
  8.2 0.6 collective-permute-start.2
  8.8 0.0 copy-done.6
  8.8 44.3 %all_to_all.10.refs_4_ = bf16[4,4,256]{2,1,0:T(4,128)(2,1)S(1)} all-to-all(bf16[4,4,256]{2,1,0:T(4,128)(2,1)S(1)} %broadcast_in_dim.28), channel_id=1, replica_groups=mesh['shard'=4,'tensor'=4,'section'=2] {'shard'}, dimensions={0} | all-to-all | bytes 16384 | tf_op jit(solution)/shard_map/all_to_all | solution.py:317
  53.1 0.0 collective-permute-done.refs_0_
  53.2 0.0 collective-permute-done.1.refs_1_
  53.2 0.0 collective-permute-done.2.refs_2_
  53.2 0.0 copy-done
  53.2 1.3 %shard_map.111 = (f32[4,64,1024]{2,1,0:T(8,128)S(1)}, f32[4,256]{1,0:T(4,128)S(1)}, f32[16,2,1,128]{3,2,1,0:T(1,128)S(1)}) custom-call(s32[5]{0:T(128)S(1)} %compare_select_fusion.place_ref, bf16[4,64,1024]{2,1,0:T(8,128)(2,1)S(1)} %collective-permute-done.refs_0_, bf16[4,64,1024]{2,1,0:T(8,128)(2,1)S(1)} %collective-permute-done.1.refs_1_, ...), custom_call_target="tpu_custom_call" | custom-call | tf_op jit(solution)/shard_map/pallas_call | solution.py:277
  54.5 11.7 %all_to_all.11.figures_ref = f32[32,1,128]{2,1,0:T(1,128)S(1)} all-to-all(f32[32,1,128]{2,1,0:T(1,128)S(1)} %bitcast.19), channel_id=1, replica_groups=mesh['shard'=4,'tensor'=4,'section'=2] {'shard','tensor','section'}, dimensions={0} | all-to-all | bytes 32768 | tf_op jit(solution)/shard_map/all_to_all | solution.py:336
  66.2 0.0 copy-start.1
  66.2 0.0 copy-start.3
  66.2 0.0 copy-start.4
  66.2 1.0 shard_map.112
  67.2 0.6 collective-permute-start.3
  67.9 0.6 collective-permute-start.4
  68.4 0.5 collective-permute-start.10
  69.0 0.6 collective-permute-start.6
  69.6 4.6 %collective-permute-done.3.refs_1_ = bf16[64,1024]{1,0:T(8,128)(2,1)S(1)} collective-permute-done((bf16[64,1024]{1,0:T(8,128)(2,1)S(1)}, bf16[64,1024]{1,0:T(8,128)(2,1)S(1)}, u32[]{:S(2)}, u32[]{:S(2)}) %collective-permute-start.3) | collective-permute-done | bytes 131104 | tf_op jit(solution)/shard_map/ppermute | solution.py:288
  74.2 0.5 collective-permute-start.11
  74.7 1.8 %collective-permute-done.4.refs_2_ = bf16[64,1024]{1,0:T(8,128)(2,1)S(1)} collective-permute-done((bf16[64,1024]{1,0:T(8,128)(2,1)S(1)}, bf16[64,1024]{1,0:T(8,128)(2,1)S(1)}, u32[]{:S(2)}, u32[]{:S(2)}) %collective-permute-start.4) | collective-permute-done | bytes 131104 | tf_op jit(solution)/shard_map/ppermute | solution.py:288
  76.5 1.5 %collective-permute-start.5 = (bf16[64,1024]{1,0:T(8,128)(2,1)S(1)}, bf16[64,1024]{1,0:T(8,128)(2,1)S(1)}, u32[]{:S(2)}, u32[]{:S(2)}) collective-permute-start(bf16[64,1024]{1,0:T(8,128)(2,1)S(1)} %get-tuple-element.41), channel_id=1, source_target_pairs={{0,24},{8,16},{16,8},{24,0},{1,25},{9,17},{17,9},{25,1},{2,26},{10... | collective-permute-start | bytes 393224 | tf_op jit(solution)/shard_map/ppermute | solution.py:288
  78.0 0.7 collective-permute-start.7
  78.6 0.0 collective-permute-done.10.refs_8_
  78.6 0.5 collective-permute-start.12
  79.1 0.0 collective-permute-done.6.refs_4_
  79.2 1.5 %collective-permute-start.8 = (bf16[64,1024]{1,0:T(8,128)(2,1)S(1)}, bf16[64,1024]{1,0:T(8,128)(2,1)S(1)}, u32[]{:S(2)}, u32[]{:S(2)}) collective-permute-start(bf16[64,1024]{1,0:T(8,128)(2,1)S(1)} %collective-permute-done.4.refs_2_), channel_id=1, source_target_pairs={{0,2},{2,0},{4,6},{6,4},{1,3},{3,1},{5,7},{7,5},{8,10},{10,8},{12,... | collective-permute-start | bytes 393224 | tf_op jit(solution)/shard_map/ppermute | solution.py:288
  80.6 0.0 collective-permute-done.11.refs_9_
  80.7 1.4 %collective-permute-start.14 = (bf16[64,1024]{1,0:T(8,128)(2,1)S(1)}, bf16[64,1024]{1,0:T(8,128)(2,1)S(1)}, u32[]{:S(2)}, u32[]{:S(2)}) collective-permute-start(bf16[64,1024]{1,0:T(8,128)(2,1)S(1)} %collective-permute-done.6.refs_4_), channel_id=1, source_target_pairs={{0,4},{2,6},{4,0},{6,2},{1,5},{3,7},{5,1},{7,3},{8,12},{10,14},{12... | collective-permute-start | bytes 393224 | tf_op jit(solution)/shard_map/ppermute | solution.py:288
  82.0 1.2 %collective-permute-done.5.refs_3_ = bf16[64,1024]{1,0:T(8,128)(2,1)S(1)} collective-permute-done((bf16[64,1024]{1,0:T(8,128)(2,1)S(1)}, bf16[64,1024]{1,0:T(8,128)(2,1)S(1)}, u32[]{:S(2)}, u32[]{:S(2)}) %collective-permute-start.5) | collective-permute-done | bytes 131104 | tf_op jit(solution)/shard_map/ppermute | solution.py:288
  83.3 0.6 collective-permute-start.17
  83.9 0.0 collective-permute-done.7.refs_5_
  83.9 1.5 %collective-permute-start.13 = (bf16[64,1024]{1,0:T(8,128)(2,1)S(1)}, bf16[64,1024]{1,0:T(8,128)(2,1)S(1)}, u32[]{:S(2)}, u32[]{:S(2)}) collective-permute-start(bf16[64,1024]{1,0:T(8,128)(2,1)S(1)} %collective-permute-done.5.refs_3_), channel_id=1, source_target_pairs={{0,4},{2,6},{4,0},{6,2},{1,5},{3,7},{5,1},{7,3},{8,12},{10,14},{12... | collective-permute-start | bytes 393224 | tf_op jit(solution)/shard_map/ppermute | solution.py:288
  85.4 0.7 collective-permute-done.12.refs_10_
  86.1 1.3 %collective-permute-start.15 = (bf16[64,1024]{1,0:T(8,128)(2,1)S(1)}, bf16[64,1024]{1,0:T(8,128)(2,1)S(1)}, u32[]{:S(2)}, u32[]{:S(2)}) collective-permute-start(bf16[64,1024]{1,0:T(8,128)(2,1)S(1)} %collective-permute-done.11.refs_9_), channel_id=1, source_target_pairs={{0,2},{2,0},{4,6},{6,4},{1,3},{3,1},{5,7},{7,5},{8,10},{10,8},{12,... | collective-permute-start | bytes 393224 | tf_op jit(solution)/shard_map/ppermute | solution.py:288
  87.3 0.0 collective-permute-done.8.refs_6_
  87.3 0.8 collective-permute-start.9
  88.1 2.2 %collective-permute-done.14.refs_12_ = bf16[64,1024]{1,0:T(8,128)(2,1)S(1)} collective-permute-done((bf16[64,1024]{1,0:T(8,128)(2,1)S(1)}, bf16[64,1024]{1,0:T(8,128)(2,1)S(1)}, u32[]{:S(2)}, u32[]{:S(2)}) %collective-permute-start.14) | collective-permute-done | bytes 131104 | tf_op jit(solution)/shard_map/ppermute | solution.py:288
  90.3 0.0 collective-permute-start.16
  90.3 1.1 collective-permute-done.15.refs_13_
  91.4 0.0 collective-permute-done.17.refs_15_
  91.4 0.7 collective-permute-done.13.refs_11_
  92.0 0.7 collective-permute-done.9.refs_7_
  92.8 2.5 %collective-permute-done.16.refs_14_ = bf16[64,1024]{1,0:T(8,128)(2,1)S(1)} collective-permute-done((bf16[64,1024]{1,0:T(8,128)(2,1)S(1)}, bf16[64,1024]{1,0:T(8,128)(2,1)S(1)}, u32[]{:S(2)}, u32[]{:S(2)}) %collective-permute-start.16) | collective-permute-done | bytes 131104 | tf_op jit(solution)/shard_map/ppermute | solution.py:288
  95.3 8.5 %shard_map.113 = (bf16[64,1024]{1,0:T(8,128)(2,1)S(1)}, bf16[64,1024]{1,0:T(8,128)(2,1)S(1)}, bf16[64,1024]{1,0:T(8,128)(2,1)S(1)}, bf16[64,1024]{1,0:T(8,128)(2,1)S(1)}) custom-call(bf16[64,1024]{1,0:T(8,128)(2,1)S(1)} %get-tuple-element.37.refs_0_, bf16[64,1024]{1,0:T(8,128)(2,1)S(1)} %collective-permute-done.3.refs_1_, ...), custom_call_target="tpu_custom_call" | custom-call | tf_op jit(solution)/shard_map/pallas_call | solution.py:91
  103.8 1.8 %collective-permute-start.18 = (bf16[64,1024]{1,0:T(8,128)(2,1)S(1)}, bf16[64,1024]{1,0:T(8,128)(2,1)S(1)}, u32[]{:S(2)}, u32[]{:S(2)}) collective-permute-start(bf16[64,1024]{1,0:T(8,128)(2,1)S(1)} %get-tuple-element.46), channel_id=1, source_target_pairs={{0,24},{8,16},{16,8},{24,0},{1,25},{9,17},{17,9},{25,1},{2,26},{10... | collective-permute-start | bytes 393224 | tf_op jit(solution)/shard_map/ppermute | solution.py:288
  105.7 0.0 collective-permute-start.19
  105.7 2.6 %collective-permute-start.20 = (bf16[64,1024]{1,0:T(8,128)(2,1)S(1)}, bf16[64,1024]{1,0:T(8,128)(2,1)S(1)}, u32[]{:S(2)}, u32[]{:S(2)}) collective-permute-start(bf16[64,1024]{1,0:T(8,128)(2,1)S(1)} %get-tuple-element.48), channel_id=1, source_target_pairs={{0,8},{8,0},{16,24},{24,16},{1,9},{9,1},{17,25},{25,17},{2,10},{10... | collective-permute-start | bytes 393224 | tf_op jit(solution)/shard_map/ppermute | solution.py:288
  108.3 0.0 copy-done.1
  108.3 1.3 %shard_map.115 = (bf16[4,64,1024]{2,1,0:T(8,128)(2,1)}, bf16[4,64,1024]{2,1,0:T(8,128)(2,1)}) custom-call(s32[5]{0:T(128)S(1)} %compare_select_fusion.place_ref, bf16[64,1024]{1,0:T(8,128)(2,1)S(1)} %get-tuple-element.42.refs_0_, bf16[4,64,1024]{2,1,0:T(8,128)(2,1)S(1)} %bitcast.16), custom_call_target="tpu_custom_call" | custom-call | tf_op jit(solution)/shard_map/pallas_call | solution.py:231
  109.6 0.0 copy-done.3
  109.6 0.0 copy-done.4
  109.6 0.0 copy-done.5
  109.6 1.8 %shard_map.114 = (f32[4,64,1024]{2,1,0:T(8,128)}, f32[4,64]{1,0:T(4,128)}, f32[4,64]{1,0:T(4,128)}) custom-call(s32[5]{0:T(128)S(1)} %compare_select_fusion.place_ref, f32[8,128]{1,0:T(8,128)S(1)} %get-tuple-element.43.clip_ref, f32[4,64,1024]{2,1,0:T(8,128)S(1)} %get-tuple-element.35.grad_ref, f32[4,64,1024]{2,1,0:T(8,128)S(1)} %bitcast.15, ...), custom_call_target="tpu_custom_call" | custom-call | tf_op jit(solution)/shard_map/pallas_call | solution.py:277
  111.4 0.0 collective-permute-done.18.refs_0_
  111.4 2.8 %collective-permute-done.19.refs_1_ = bf16[64,1024]{1,0:T(8,128)(2,1)S(1)} collective-permute-done((bf16[64,1024]{1,0:T(8,128)(2,1)S(1)}, bf16[64,1024]{1,0:T(8,128)(2,1)S(1)}, u32[]{:S(2)}, u32[]{:S(2)}) %collective-permute-start.19) | collective-permute-done | bytes 131104 | tf_op jit(solution)/shard_map/ppermute | solution.py:288
  114.2 0.0 collective-permute-done.20.refs_2_
  114.2 1.5 %shard_map.116 = (bf16[4,64,1024]{2,1,0:T(8,128)(2,1)}, bf16[4,64,1024]{2,1,0:T(8,128)(2,1)}) custom-call(s32[5]{0:T(128)S(1)} %compare_select_fusion.place_ref, bf16[64,1024]{1,0:T(8,128)(2,1)S(1)} %collective-permute-done.18.refs_0_, bf16[64,1024]{1,0:T(8,128)(2,1)S(1)} %collective-permute-done.19.refs_1_, ...), custom_call_target="tpu_custom_call", output_to_operand_aliasing={{0}: (5, {}), {1}: (6, {})} | custom-call | tf_op jit(solution)/shard_map/pallas_call | solution.py:231
  (3 shorter events, 0.0 us)
Async XLA Ops:
  0.6 52.5 %copy-start = (f32[1,4,64,1024]{3,2,1,0:T(8,128)S(1)}, f32[1,4,64,1024]{3,2,1,0:T(8,128)}, u32[]{:S(2)}) copy-start(f32[1,4,64,1024]{3,2,1,0:T(8,128)} %param.9) | copy-start | bytes 3145732
  0.7 1.7 %copy-start.2 = (bf16[1,1,4,256,1024]{4,3,2,1,0:T(8,128)(2,1)S(1)}, bf16[1,1,4,256,1024]{4,3,2,1,0:T(8,128)(2,1)}, u32[]{:S(2)}) copy-start(bf16[1,1,4,256,1024]{4,3,2,1,0:T(8,128)(2,1)} %param.7) | copy-start | bytes 6291460
  2.3 6.5 %copy-start.6 = (bf16[1,1,4,256]{3,2,1,0:T(4,128)(2,1)S(1)}, bf16[1,1,4,256]{3,2,1,0:T(4,128)(2,1)}, u32[]{:S(2)}) copy-start(bf16[1,1,4,256]{3,2,1,0:T(4,128)(2,1)} %param.8) | copy-start | bytes 6148
  3.1 50.1 %collective-permute-start = (bf16[4,64,1024]{2,1,0:T(8,128)(2,1)S(1)}, bf16[4,64,1024]{2,1,0:T(8,128)(2,1)S(1)}, u32[]{:S(2)}, u32[]{:S(2)}) collective-permute-start(bf16[4,64,1024]{2,1,0:T(8,128)(2,1)S(1)} %get-tuple-element.30), channel_id=1, source_target_pairs={{0,24},{8,16},{16,8},{24,0},{1,25},{9,17},{17,9},{25,1},{2,26},{10... | collective-permute-start | bytes 1572872 | tf_op jit(solution)/shard_map/ppermute | solution.py:288
  8.2 45.0 %collective-permute-start.1 = (bf16[4,64,1024]{2,1,0:T(8,128)(2,1)S(1)}, bf16[4,64,1024]{2,1,0:T(8,128)(2,1)S(1)}, u32[]{:S(2)}, u32[]{:S(2)}) collective-permute-start(bf16[4,64,1024]{2,1,0:T(8,128)(2,1)S(1)} %get-tuple-element.31), channel_id=1, source_target_pairs={{0,16},{8,24},{16,0},{24,8},{1,17},{9,25},{17,1},{25,9},{2,18},{10... | collective-permute-start | bytes 1572872 | tf_op jit(solution)/shard_map/ppermute | solution.py:288
  8.2 45.0 %collective-permute-start.2 = (bf16[4,64,1024]{2,1,0:T(8,128)(2,1)S(1)}, bf16[4,64,1024]{2,1,0:T(8,128)(2,1)S(1)}, u32[]{:S(2)}, u32[]{:S(2)}) collective-permute-start(bf16[4,64,1024]{2,1,0:T(8,128)(2,1)S(1)} %get-tuple-element.32), channel_id=1, source_target_pairs={{0,8},{8,0},{16,24},{24,16},{1,9},{9,1},{17,25},{25,17},{2,10},{10... | collective-permute-start | bytes 1572872 | tf_op jit(solution)/shard_map/ppermute | solution.py:288
  66.2 42.1 %copy-start.1 = (bf16[1,4,64,1024]{3,2,1,0:T(8,128)(2,1)S(1)}, bf16[1,4,64,1024]{3,2,1,0:T(8,128)(2,1)}, u32[]{:S(2)}) copy-start(bf16[1,4,64,1024]{3,2,1,0:T(8,128)(2,1)} %param.10) | copy-start | bytes 1572868
  66.2 43.4 %copy-start.3 = (f32[1,4,64]{2,1,0:T(4,128)S(1)}, f32[1,4,64]{2,1,0:T(4,128)}, u32[]{:S(2)}) copy-start(f32[1,4,64]{2,1,0:T(4,128)} %param.11) | copy-start | bytes 3076
  66.2 43.4 %copy-start.4 = (f32[1,4,64]{2,1,0:T(4,128)S(1)}, f32[1,4,64]{2,1,0:T(4,128)}, u32[]{:S(2)}) copy-start(f32[1,4,64]{2,1,0:T(4,128)} %param.12) | copy-start | bytes 3076
  66.2 43.4 %copy-start.5 = (f32[1,4,64]{2,1,0:T(4,128)S(1)}, f32[1,4,64]{2,1,0:T(4,128)}, u32[]{:S(2)}) copy-start(f32[1,4,64]{2,1,0:T(4,128)} %param.13) | copy-start | bytes 3076
  67.2 6.9 %collective-permute-start.3 = (bf16[64,1024]{1,0:T(8,128)(2,1)S(1)}, bf16[64,1024]{1,0:T(8,128)(2,1)S(1)}, u32[]{:S(2)}, u32[]{:S(2)}) collective-permute-start(bf16[64,1024]{1,0:T(8,128)(2,1)S(1)} %get-tuple-element.38), channel_id=1, source_target_pairs={{0,8},{8,0},{16,24},{24,16},{1,9},{9,1},{17,25},{25,17},{2,10},{10... | collective-permute-start | bytes 393224 | tf_op jit(solution)/shard_map/ppermute | solution.py:288
  67.9 8.6 %collective-permute-start.4 = (bf16[64,1024]{1,0:T(8,128)(2,1)S(1)}, bf16[64,1024]{1,0:T(8,128)(2,1)S(1)}, u32[]{:S(2)}, u32[]{:S(2)}) collective-permute-start(bf16[64,1024]{1,0:T(8,128)(2,1)S(1)} %get-tuple-element.39), channel_id=1, source_target_pairs={{0,16},{8,24},{16,0},{24,8},{1,17},{9,25},{17,1},{25,9},{2,18},{10... | collective-permute-start | bytes 393224 | tf_op jit(solution)/shard_map/ppermute | solution.py:288
  68.4 10.2 %collective-permute-start.10 = (bf16[64,1024]{1,0:T(8,128)(2,1)S(1)}, bf16[64,1024]{1,0:T(8,128)(2,1)S(1)}, u32[]{:S(2)}, u32[]{:S(2)}) collective-permute-start(bf16[64,1024]{1,0:T(8,128)(2,1)S(1)} %get-tuple-element.37.refs_0_), channel_id=1, source_target_pairs={{0,4},{2,6},{4,0},{6,2},{1,5},{3,7},{5,1},{7,3},{8,12},{10,14},{12... | collective-permute-start | bytes 393224 | tf_op jit(solution)/shard_map/ppermute | solution.py:288
  69.0 10.2 %collective-permute-start.6 = (bf16[64,1024]{1,0:T(8,128)(2,1)S(1)}, bf16[64,1024]{1,0:T(8,128)(2,1)S(1)}, u32[]{:S(2)}, u32[]{:S(2)}) collective-permute-start(bf16[64,1024]{1,0:T(8,128)(2,1)S(1)} %get-tuple-element.37.refs_0_), channel_id=1, source_target_pairs={{0,2},{2,0},{4,6},{6,4},{1,3},{3,1},{5,7},{7,5},{8,10},{10,8},{12,... | collective-permute-start | bytes 393224 | tf_op jit(solution)/shard_map/ppermute | solution.py:288
  74.2 6.5 %collective-permute-start.11 = (bf16[64,1024]{1,0:T(8,128)(2,1)S(1)}, bf16[64,1024]{1,0:T(8,128)(2,1)S(1)}, u32[]{:S(2)}, u32[]{:S(2)}) collective-permute-start(bf16[64,1024]{1,0:T(8,128)(2,1)S(1)} %collective-permute-done.3.refs_1_), channel_id=1, source_target_pairs={{0,4},{2,6},{4,0},{6,2},{1,5},{3,7},{5,1},{7,3},{8,12},{10,14},{12... | collective-permute-start | bytes 393224 | tf_op jit(solution)/shard_map/ppermute | solution.py:288
  76.5 6.8 %collective-permute-start.5 = (bf16[64,1024]{1,0:T(8,128)(2,1)S(1)}, bf16[64,1024]{1,0:T(8,128)(2,1)S(1)}, u32[]{:S(2)}, u32[]{:S(2)}) collective-permute-start(bf16[64,1024]{1,0:T(8,128)(2,1)S(1)} %get-tuple-element.41), channel_id=1, source_target_pairs={{0,24},{8,16},{16,8},{24,0},{1,25},{9,17},{17,9},{25,1},{2,26},{10... | collective-permute-start | bytes 393224 | tf_op jit(solution)/shard_map/ppermute | solution.py:288
  78.0 5.9 %collective-permute-start.7 = (bf16[64,1024]{1,0:T(8,128)(2,1)S(1)}, bf16[64,1024]{1,0:T(8,128)(2,1)S(1)}, u32[]{:S(2)}, u32[]{:S(2)}) collective-permute-start(bf16[64,1024]{1,0:T(8,128)(2,1)S(1)} %collective-permute-done.3.refs_1_), channel_id=1, source_target_pairs={{0,2},{2,0},{4,6},{6,4},{1,3},{3,1},{5,7},{7,5},{8,10},{10,8},{12,... | collective-permute-start | bytes 393224 | tf_op jit(solution)/shard_map/ppermute | solution.py:288
  78.6 7.4 %collective-permute-start.12 = (bf16[64,1024]{1,0:T(8,128)(2,1)S(1)}, bf16[64,1024]{1,0:T(8,128)(2,1)S(1)}, u32[]{:S(2)}, u32[]{:S(2)}) collective-permute-start(bf16[64,1024]{1,0:T(8,128)(2,1)S(1)} %collective-permute-done.4.refs_2_), channel_id=1, source_target_pairs={{0,4},{2,6},{4,0},{6,2},{1,5},{3,7},{5,1},{7,3},{8,12},{10,14},{12... | collective-permute-start | bytes 393224 | tf_op jit(solution)/shard_map/ppermute | solution.py:288
  79.2 8.2 %collective-permute-start.8 = (bf16[64,1024]{1,0:T(8,128)(2,1)S(1)}, bf16[64,1024]{1,0:T(8,128)(2,1)S(1)}, u32[]{:S(2)}, u32[]{:S(2)}) collective-permute-start(bf16[64,1024]{1,0:T(8,128)(2,1)S(1)} %collective-permute-done.4.refs_2_), channel_id=1, source_target_pairs={{0,2},{2,0},{4,6},{6,4},{1,3},{3,1},{5,7},{7,5},{8,10},{10,8},{12,... | collective-permute-start | bytes 393224 | tf_op jit(solution)/shard_map/ppermute | solution.py:288
  80.7 9.6 %collective-permute-start.14 = (bf16[64,1024]{1,0:T(8,128)(2,1)S(1)}, bf16[64,1024]{1,0:T(8,128)(2,1)S(1)}, u32[]{:S(2)}, u32[]{:S(2)}) collective-permute-start(bf16[64,1024]{1,0:T(8,128)(2,1)S(1)} %collective-permute-done.6.refs_4_), channel_id=1, source_target_pairs={{0,4},{2,6},{4,0},{6,2},{1,5},{3,7},{5,1},{7,3},{8,12},{10,14},{12... | collective-permute-start | bytes 393224 | tf_op jit(solution)/shard_map/ppermute | solution.py:288
  83.3 8.1 %collective-permute-start.17 = (bf16[64,1024]{1,0:T(8,128)(2,1)S(1)}, bf16[64,1024]{1,0:T(8,128)(2,1)S(1)}, u32[]{:S(2)}, u32[]{:S(2)}) collective-permute-start(bf16[64,1024]{1,0:T(8,128)(2,1)S(1)} %collective-permute-done.5.refs_3_), channel_id=1, source_target_pairs={{0,6},{2,4},{4,2},{6,0},{1,7},{3,5},{5,3},{7,1},{8,14},{10,12},{12... | collective-permute-start | bytes 393224 | tf_op jit(solution)/shard_map/ppermute | solution.py:288
  83.9 8.2 %collective-permute-start.13 = (bf16[64,1024]{1,0:T(8,128)(2,1)S(1)}, bf16[64,1024]{1,0:T(8,128)(2,1)S(1)}, u32[]{:S(2)}, u32[]{:S(2)}) collective-permute-start(bf16[64,1024]{1,0:T(8,128)(2,1)S(1)} %collective-permute-done.5.refs_3_), channel_id=1, source_target_pairs={{0,4},{2,6},{4,0},{6,2},{1,5},{3,7},{5,1},{7,3},{8,12},{10,14},{12... | collective-permute-start | bytes 393224 | tf_op jit(solution)/shard_map/ppermute | solution.py:288
  86.1 5.3 %collective-permute-start.15 = (bf16[64,1024]{1,0:T(8,128)(2,1)S(1)}, bf16[64,1024]{1,0:T(8,128)(2,1)S(1)}, u32[]{:S(2)}, u32[]{:S(2)}) collective-permute-start(bf16[64,1024]{1,0:T(8,128)(2,1)S(1)} %collective-permute-done.11.refs_9_), channel_id=1, source_target_pairs={{0,2},{2,0},{4,6},{6,4},{1,3},{3,1},{5,7},{7,5},{8,10},{10,8},{12,... | collective-permute-start | bytes 393224 | tf_op jit(solution)/shard_map/ppermute | solution.py:288
  87.3 5.4 %collective-permute-start.9 = (bf16[64,1024]{1,0:T(8,128)(2,1)S(1)}, bf16[64,1024]{1,0:T(8,128)(2,1)S(1)}, u32[]{:S(2)}, u32[]{:S(2)}) collective-permute-start(bf16[64,1024]{1,0:T(8,128)(2,1)S(1)} %collective-permute-done.5.refs_3_), channel_id=1, source_target_pairs={{0,2},{2,0},{4,6},{6,4},{1,3},{3,1},{5,7},{7,5},{8,10},{10,8},{12,... | collective-permute-start | bytes 393224 | tf_op jit(solution)/shard_map/ppermute | solution.py:288
  90.3 5.0 %collective-permute-start.16 = (bf16[64,1024]{1,0:T(8,128)(2,1)S(1)}, bf16[64,1024]{1,0:T(8,128)(2,1)S(1)}, u32[]{:S(2)}, u32[]{:S(2)}) collective-permute-start(bf16[64,1024]{1,0:T(8,128)(2,1)S(1)} %collective-permute-done.8.refs_6_), channel_id=1, source_target_pairs={{0,4},{2,6},{4,0},{6,2},{1,5},{3,7},{5,1},{7,3},{8,12},{10,14},{12... | collective-permute-start | bytes 393224 | tf_op jit(solution)/shard_map/ppermute | solution.py:288
  103.8 7.6 %collective-permute-start.18 = (bf16[64,1024]{1,0:T(8,128)(2,1)S(1)}, bf16[64,1024]{1,0:T(8,128)(2,1)S(1)}, u32[]{:S(2)}, u32[]{:S(2)}) collective-permute-start(bf16[64,1024]{1,0:T(8,128)(2,1)S(1)} %get-tuple-element.46), channel_id=1, source_target_pairs={{0,24},{8,16},{16,8},{24,0},{1,25},{9,17},{17,9},{25,1},{2,26},{10... | collective-permute-start | bytes 393224 | tf_op jit(solution)/shard_map/ppermute | solution.py:288
  105.7 8.6 %collective-permute-start.19 = (bf16[64,1024]{1,0:T(8,128)(2,1)S(1)}, bf16[64,1024]{1,0:T(8,128)(2,1)S(1)}, u32[]{:S(2)}, u32[]{:S(2)}) collective-permute-start(bf16[64,1024]{1,0:T(8,128)(2,1)S(1)} %get-tuple-element.47), channel_id=1, source_target_pairs={{0,16},{8,24},{16,0},{24,8},{1,17},{9,25},{17,1},{25,9},{2,18},{10... | collective-permute-start | bytes 393224 | tf_op jit(solution)/shard_map/ppermute | solution.py:288
  105.7 8.6 %collective-permute-start.20 = (bf16[64,1024]{1,0:T(8,128)(2,1)S(1)}, bf16[64,1024]{1,0:T(8,128)(2,1)S(1)}, u32[]{:S(2)}, u32[]{:S(2)}) collective-permute-start(bf16[64,1024]{1,0:T(8,128)(2,1)S(1)} %get-tuple-element.48), channel_id=1, source_target_pairs={{0,8},{8,0},{16,24},{24,16},{1,9},{9,1},{17,25},{25,17},{2,10},{10... | collective-permute-start | bytes 393224 | tf_op jit(solution)/shard_map/ppermute | solution.py:288

commit v2 on v0

--- a/solution.py
+++ b/solution.py
@@ -349,21 +349,22 @@
     )
 
     pieces = [scaled[0]] + [None] * 3
-    for offset in (2, 3, 1):
+    for offset in (2, 1):
         pieces[offset] = swapped(scaled[offset], "shard", offset)
     near, side, far = [None] * 4, [None] * 4, [None] * 4
     near[0] = swapped(pieces[0], "tensor", 1)
     side[0] = swapped(pieces[0], "tensor", 2)
-    far[0] = swapped(near[0], "tensor", 2)
-    near[1] = swapped(pieces[1], "tensor", 1)
-    side[1] = swapped(after(pieces[1], near[0]), "tensor", 2)
+    far[0] = swapped(pieces[0], "tensor", 3)
+    pieces[3] = swapped(after(scaled[3], near[0]), "shard", 3)
+    near[1] = swapped(after(pieces[1], near[0]), "tensor", 1)
+    side[1] = swapped(after(pieces[1], side[0]), "tensor", 2)
     far[1] = swapped(side[1], "tensor", 1)
-    near[2] = swapped(pieces[2], "tensor", 1)
-    side[2] = swapped(after(pieces[2], side[0]), "tensor", 2)
+    near[2] = swapped(after(pieces[2], far[0]), "tensor", 1)
+    side[2] = swapped(after(pieces[2], far[0]), "tensor", 2)
     far[2] = swapped(near[2], "tensor", 2)
-    near[3] = swapped(after(pieces[3], near[1]), "tensor", 1)
-    side[3] = swapped(after(pieces[3], near[1]), "tensor", 2)
-    far[3] = swapped(side[3], "tensor", 1)
+    near[3] = swapped(after(pieces[3], side[1]), "tensor", 1)
+    side[3] = swapped(after(pieces[3], side[1]), "tensor", 2)
+    far[3] = swapped(after(pieces[3], side[1]), "tensor", 3)
     results = orthogonalize([pieces, near, side, far])
 
     returned = {

time: 116 us -> 116 us (level)
  starting transfers between devices: 24.7 us -> 26.6 us
  waiting for transfers between devices: 16.8 us -> 15 us
    ppermute x21, starting transfers between devices: 24.7 us -> 26.6 us  [swapped(): return lax.ppermute(array, axis, pairs)]
    ppermute x21, waiting for transfers between devices: 16.8 us -> 15 us  [swapped(): return lax.ppermute(array, axis, pairs)]
  transfers between devices with their start and end apart: 21 -> 21, of which waited for: 7 -> 10; matrix products, arithmetic and copies ran while one was open for 0% -> 0% of each run, Pallas kernels for 3% -> 3%
where the time goes in v2:
time: 116 us
  blocking collectives  56 us (48%)
  starting transfers between devices  26.6 us (23%)
  Pallas kernels  16.2 us (14%)
  waiting for transfers between devices  15 us (13%)
  local copies, waits for them, and re-layouts  1.7 us (1%)
    all_to_all x1, blocking collectives, per_device(): lax.all_to_all(jnp.broadcast_to(vector_grads[0], (shard_count, vector_cou...  44.3 us
    ppermute x21, starting transfers between devices, swapped(): return lax.ppermute(array, axis, pairs)  26.6 us
    ppermute x21, waiting for transfers between devices, swapped(): return lax.ppermute(array, axis, pairs)  15 us
    all_to_all x1, blocking collectives, per_device(): lax.all_to_all(figures.reshape(others * section_count, 1, LANES), MESH_AX...  11.7 us
    pallas_call x1, Pallas kernels, orthogonalize(): pl.pallas_call(functools.partial(orthogonalize_kernel, count, pieces), ou...  8.55 us
    pallas_call x3, Pallas kernels, on_device(): pl.pallas_call(kernel, out_shape=out_shape, in_specs=[pl.BlockSpec(memory...  4.2 us
    pallas_call x2, Pallas kernels, finished(): pl.pallas_call(functools.partial(end_kernel, offsets), out_shape=[jax.Sha...  2.74 us
  transfers between devices with their start and end apart: 21, of which 10 were waited for; matrix products, arithmetic and copies ran while one was open for 0% of the time, Pallas kernels for 3%

profile of v2, /device:TPU:0, one launch (start us, length us, event | category | flops | bytes accessed | tf_op | source)
XLA Modules:
  0.0 116.3 jit_solution(17590307653965262548)
XLA Ops:
  0.6 0.0 copy-start
  0.7 0.0 copy-start.2
  0.7 1.7 %copy-done.2 = bf16[1,1,4,256,1024]{4,3,2,1,0:T(8,128)(2,1)S(1)} copy-done((bf16[1,1,4,256,1024]{4,3,2,1,0:T(8,128)(2,1)S(1)}, bf16[1,1,4,256,1024]{4,3,2,1,0:T(8,128)(2,1)}, u32[]{:S(2)}) %copy-start.2) | copy-done | bytes 2097176
  2.3 0.0 copy-start.6
  2.3 0.7 shard_map.110
  3.1 5.1 %collective-permute-start = (bf16[4,64,1024]{2,1,0:T(8,128)(2,1)S(1)}, bf16[4,64,1024]{2,1,0:T(8,128)(2,1)S(1)}, u32[]{:S(2)}, u32[]{:S(2)}) collective-permute-start(bf16[4,64,1024]{2,1,0:T(8,128)(2,1)S(1)} %get-tuple-element.34), channel_id=1, source_target_pairs={{0,24},{8,16},{16,8},{24,0},{1,25},{9,17},{17,9},{25,1},{2,26},{10... | collective-permute-start | bytes 1572872 | tf_op jit(solution)/shard_map/ppermute | solution.py:288
  8.2 0.0 collective-permute-start.1
  8.2 0.6 collective-permute-start.2
  8.8 0.0 copy-done.6
  8.8 44.3 %all_to_all.10.refs_4_ = bf16[4,4,256]{2,1,0:T(4,128)(2,1)S(1)} all-to-all(bf16[4,4,256]{2,1,0:T(4,128)(2,1)S(1)} %broadcast_in_dim.28), channel_id=1, replica_groups=mesh['shard'=4,'tensor'=4,'section'=2] {'shard'}, dimensions={0} | all-to-all | bytes 16384 | tf_op jit(solution)/shard_map/all_to_all | solution.py:317
  53.1 0.0 collective-permute-done.refs_0_
  53.2 0.0 collective-permute-done.1.refs_1_
  53.2 0.0 collective-permute-done.2.refs_2_
  53.2 0.0 copy-done
  53.2 1.3 %shard_map.111 = (f32[4,64,1024]{2,1,0:T(8,128)S(1)}, f32[4,256]{1,0:T(4,128)S(1)}, f32[16,2,1,128]{3,2,1,0:T(1,128)S(1)}) custom-call(s32[5]{0:T(128)S(1)} %compare_select_fusion.place_ref, bf16[4,64,1024]{2,1,0:T(8,128)(2,1)S(1)} %collective-permute-done.refs_0_, bf16[4,64,1024]{2,1,0:T(8,128)(2,1)S(1)} %collective-permute-done.1.refs_1_, ...), custom_call_target="tpu_custom_call" | custom-call | tf_op jit(solution)/shard_map/pallas_call | solution.py:277
  54.5 11.7 %all_to_all.11.figures_ref = f32[32,1,128]{2,1,0:T(1,128)S(1)} all-to-all(f32[32,1,128]{2,1,0:T(1,128)S(1)} %bitcast.19), channel_id=1, replica_groups=mesh['shard'=4,'tensor'=4,'section'=2] {'shard','tensor','section'}, dimensions={0} | all-to-all | bytes 32768 | tf_op jit(solution)/shard_map/all_to_all | solution.py:336
  66.2 0.0 copy-start.1
  66.2 0.0 copy-start.3
  66.2 0.0 copy-start.4
  66.2 1.0 shard_map.112
  67.2 0.6 collective-permute-start.3
  67.9 0.5 collective-permute-start.10
  68.4 0.6 collective-permute-start.5
  69.1 0.5 collective-permute-start.4
  69.6 2.4 %collective-permute-start.8 = (bf16[64,1024]{1,0:T(8,128)(2,1)S(1)}, bf16[64,1024]{1,0:T(8,128)(2,1)S(1)}, u32[]{:S(2)}, u32[]{:S(2)}) collective-permute-start(bf16[64,1024]{1,0:T(8,128)(2,1)S(1)} %get-tuple-element.41.refs_0_), channel_id=1, source_target_pairs={{0,6},{2,4},{4,2},{6,0},{1,7},{3,5},{5,3},{7,1},{8,14},{10,12},{12... | collective-permute-start | bytes 393224 | tf_op jit(solution)/shard_map/ppermute | solution.py:288
  71.9 1.7 %collective-permute-done.3.refs_1_ = bf16[64,1024]{1,0:T(8,128)(2,1)S(1)} collective-permute-done((bf16[64,1024]{1,0:T(8,128)(2,1)S(1)}, bf16[64,1024]{1,0:T(8,128)(2,1)S(1)}, u32[]{:S(2)}, u32[]{:S(2)}) %collective-permute-start.3) | collective-permute-done | bytes 131104 | tf_op jit(solution)/shard_map/ppermute | solution.py:288
  73.6 0.0 collective-permute-done.10.refs_8_
  73.6 0.4 collective-permute-start.11
  74.1 0.5 collective-permute-done.5.refs_4_
  74.5 1.2 %collective-permute-start.6 = (bf16[64,1024]{1,0:T(8,128)(2,1)S(1)}, bf16[64,1024]{1,0:T(8,128)(2,1)S(1)}, u32[]{:S(2)}, u32[]{:S(2)}) collective-permute-start(bf16[64,1024]{1,0:T(8,128)(2,1)S(1)} %get-tuple-element.45), channel_id=1, source_target_pairs={{0,24},{8,16},{16,8},{24,0},{1,25},{9,17},{17,9},{25,1},{2,26},{10... | collective-permute-start | bytes 393224 | tf_op jit(solution)/shard_map/ppermute | solution.py:288
  75.7 3.9 %collective-permute-done.4.refs_2_ = bf16[64,1024]{1,0:T(8,128)(2,1)S(1)} collective-permute-done((bf16[64,1024]{1,0:T(8,128)(2,1)S(1)}, bf16[64,1024]{1,0:T(8,128)(2,1)S(1)}, u32[]{:S(2)}, u32[]{:S(2)}) %collective-permute-start.4) | collective-permute-done | bytes 131104 | tf_op jit(solution)/shard_map/ppermute | solution.py:288
  79.7 0.0 collective-permute-done.8.refs_12_
  79.7 1.4 %collective-permute-start.13 = (bf16[64,1024]{1,0:T(8,128)(2,1)S(1)}, bf16[64,1024]{1,0:T(8,128)(2,1)S(1)}, u32[]{:S(2)}, u32[]{:S(2)}) collective-permute-start(bf16[64,1024]{1,0:T(8,128)(2,1)S(1)} %collective-permute-done.4.refs_2_), channel_id=1, source_target_pairs={{0,4},{2,6},{4,0},{6,2},{1,5},{3,7},{5,1},{7,3},{8,12},{10,14},{12... | collective-permute-start | bytes 393224 | tf_op jit(solution)/shard_map/ppermute | solution.py:288
  81.0 2.9 %collective-permute-start.9 = (bf16[64,1024]{1,0:T(8,128)(2,1)S(1)}, bf16[64,1024]{1,0:T(8,128)(2,1)S(1)}, u32[]{:S(2)}, u32[]{:S(2)}) collective-permute-start(bf16[64,1024]{1,0:T(8,128)(2,1)S(1)} %collective-permute-done.4.refs_2_), channel_id=1, source_target_pairs={{0,2},{2,0},{4,6},{6,4},{1,3},{3,1},{5,7},{7,5},{8,10},{10,8},{12,... | collective-permute-start | bytes 393224 | tf_op jit(solution)/shard_map/ppermute | solution.py:288
  83.9 0.0 collective-permute-start.7
  84.0 0.0 collective-permute-done.11.refs_9_
  84.0 0.0 collective-permute-done.6.refs_3_
  84.0 1.9 %collective-permute-start.17 = (bf16[64,1024]{1,0:T(8,128)(2,1)S(1)}, bf16[64,1024]{1,0:T(8,128)(2,1)S(1)}, u32[]{:S(2)}, u32[]{:S(2)}) collective-permute-start(bf16[64,1024]{1,0:T(8,128)(2,1)S(1)} %collective-permute-done.6.refs_3_), channel_id=1, source_target_pairs={{0,6},{2,4},{4,2},{6,0},{1,7},{3,5},{5,3},{7,1},{8,14},{10,12},{12... | collective-permute-start | bytes 393224 | tf_op jit(solution)/shard_map/ppermute | solution.py:288
  85.9 0.1 collective-permute-start.15
  86.0 2.3 %collective-permute-done.9.refs_6_ = bf16[64,1024]{1,0:T(8,128)(2,1)S(1)} collective-permute-done((bf16[64,1024]{1,0:T(8,128)(2,1)S(1)}, bf16[64,1024]{1,0:T(8,128)(2,1)S(1)}, u32[]{:S(2)}, u32[]{:S(2)}) %collective-permute-start.9) | collective-permute-done | bytes 131104 | tf_op jit(solution)/shard_map/ppermute | solution.py:288
  88.4 0.5 collective-permute-start.16
  88.9 0.0 collective-permute-done.13.refs_10_
  88.9 1.5 %collective-permute-start.14 = (bf16[64,1024]{1,0:T(8,128)(2,1)S(1)}, bf16[64,1024]{1,0:T(8,128)(2,1)S(1)}, u32[]{:S(2)}, u32[]{:S(2)}) collective-permute-start(bf16[64,1024]{1,0:T(8,128)(2,1)S(1)} %collective-permute-done.6.refs_3_), channel_id=1, source_target_pairs={{0,4},{2,6},{4,0},{6,2},{1,5},{3,7},{5,1},{7,3},{8,12},{10,14},{12... | collective-permute-start | bytes 393224 | tf_op jit(solution)/shard_map/ppermute | solution.py:288
  90.4 0.4 collective-permute-done.7.refs_5_
  90.8 1.6 %collective-permute-start.12 = (bf16[64,1024]{1,0:T(8,128)(2,1)S(1)}, bf16[64,1024]{1,0:T(8,128)(2,1)S(1)}, u32[]{:S(2)}, u32[]{:S(2)}) collective-permute-start(bf16[64,1024]{1,0:T(8,128)(2,1)S(1)} %collective-permute-done.6.refs_3_), channel_id=1, source_target_pairs={{0,2},{2,0},{4,6},{6,4},{1,3},{3,1},{5,7},{7,5},{8,10},{10,8},{12,... | collective-permute-start | bytes 393224 | tf_op jit(solution)/shard_map/ppermute | solution.py:288
  92.4 1.2 %collective-permute-done.15.refs_13_ = bf16[64,1024]{1,0:T(8,128)(2,1)S(1)} collective-permute-done((bf16[64,1024]{1,0:T(8,128)(2,1)S(1)}, bf16[64,1024]{1,0:T(8,128)(2,1)S(1)}, u32[]{:S(2)}, u32[]{:S(2)}) %collective-permute-start.15) | collective-permute-done | bytes 131104 | tf_op jit(solution)/shard_map/ppermute | solution.py:288
  93.6 0.2 collective-permute-done.16.refs_14_
  93.8 0.0 collective-permute-done.17.refs_15_
  93.8 1.4 %collective-permute-done.14.refs_11_ = bf16[64,1024]{1,0:T(8,128)(2,1)S(1)} collective-permute-done((bf16[64,1024]{1,0:T(8,128)(2,1)S(1)}, bf16[64,1024]{1,0:T(8,128)(2,1)S(1)}, u32[]{:S(2)}, u32[]{:S(2)}) %collective-permute-start.14) | collective-permute-done | bytes 131104 | tf_op jit(solution)/shard_map/ppermute | solution.py:288
  95.2 0.5 collective-permute-done.12.refs_7_
  95.8 8.5 %shard_map.113 = (bf16[64,1024]{1,0:T(8,128)(2,1)S(1)}, bf16[64,1024]{1,0:T(8,128)(2,1)S(1)}, bf16[64,1024]{1,0:T(8,128)(2,1)S(1)}, bf16[64,1024]{1,0:T(8,128)(2,1)S(1)}) custom-call(bf16[64,1024]{1,0:T(8,128)(2,1)S(1)} %get-tuple-element.41.refs_0_, bf16[64,1024]{1,0:T(8,128)(2,1)S(1)} %collective-permute-done.3.refs_1_, ...), custom_call_target="tpu_custom_call" | custom-call | tf_op jit(solution)/shard_map/pallas_call | solution.py:91
  104.3 1.4 %collective-permute-start.18 = (bf16[64,1024]{1,0:T(8,128)(2,1)S(1)}, bf16[64,1024]{1,0:T(8,128)(2,1)S(1)}, u32[]{:S(2)}, u32[]{:S(2)}) collective-permute-start(bf16[64,1024]{1,0:T(8,128)(2,1)S(1)} %get-tuple-element.54), channel_id=1, source_target_pairs={{0,24},{8,16},{16,8},{24,0},{1,25},{9,17},{17,9},{25,1},{2,26},{10... | collective-permute-start | bytes 393224 | tf_op jit(solution)/shard_map/ppermute | solution.py:288
  105.8 0.0 collective-permute-start.19
  105.8 3.0 %collective-permute-start.20 = (bf16[64,1024]{1,0:T(8,128)(2,1)S(1)}, bf16[64,1024]{1,0:T(8,128)(2,1)S(1)}, u32[]{:S(2)}, u32[]{:S(2)}) collective-permute-start(bf16[64,1024]{1,0:T(8,128)(2,1)S(1)} %get-tuple-element.56), channel_id=1, source_target_pairs={{0,8},{8,0},{16,24},{24,16},{1,9},{9,1},{17,25},{25,17},{2,10},{10... | collective-permute-start | bytes 393224 | tf_op jit(solution)/shard_map/ppermute | solution.py:288
  108.8 0.0 copy-done.1
  108.8 1.3 %shard_map.115 = (bf16[4,64,1024]{2,1,0:T(8,128)(2,1)}, bf16[4,64,1024]{2,1,0:T(8,128)(2,1)}) custom-call(s32[5]{0:T(128)S(1)} %compare_select_fusion.place_ref, bf16[64,1024]{1,0:T(8,128)(2,1)S(1)} %get-tuple-element.50.refs_0_, bf16[4,64,1024]{2,1,0:T(8,128)(2,1)S(1)} %bitcast.16), custom_call_target="tpu_custom_call" | custom-call | tf_op jit(solution)/shard_map/pallas_call | solution.py:231
  110.1 0.0 copy-done.3
  110.1 0.0 copy-done.4
  110.1 0.0 copy-done.5
  110.1 1.8 %shard_map.114 = (f32[4,64,1024]{2,1,0:T(8,128)}, f32[4,64]{1,0:T(4,128)}, f32[4,64]{1,0:T(4,128)}) custom-call(s32[5]{0:T(128)S(1)} %compare_select_fusion.place_ref, f32[8,128]{1,0:T(8,128)S(1)} %get-tuple-element.51.clip_ref, f32[4,64,1024]{2,1,0:T(8,128)S(1)} %get-tuple-element.39.grad_ref, f32[4,64,1024]{2,1,0:T(8,128)S(1)} %bitcast.15, ...), custom_call_target="tpu_custom_call" | custom-call | tf_op jit(solution)/shard_map/pallas_call | solution.py:277
  111.9 0.0 collective-permute-done.18.refs_0_
  111.9 2.9 %collective-permute-done.19.refs_1_ = bf16[64,1024]{1,0:T(8,128)(2,1)S(1)} collective-permute-done((bf16[64,1024]{1,0:T(8,128)(2,1)S(1)}, bf16[64,1024]{1,0:T(8,128)(2,1)S(1)}, u32[]{:S(2)}, u32[]{:S(2)}) %collective-permute-start.19) | collective-permute-done | bytes 131104 | tf_op jit(solution)/shard_map/ppermute | solution.py:288
  114.8 0.0 collective-permute-done.20.refs_2_
  114.8 1.5 %shard_map.116 = (bf16[4,64,1024]{2,1,0:T(8,128)(2,1)}, bf16[4,64,1024]{2,1,0:T(8,128)(2,1)}) custom-call(s32[5]{0:T(128)S(1)} %compare_select_fusion.place_ref, bf16[64,1024]{1,0:T(8,128)(2,1)S(1)} %collective-permute-done.18.refs_0_, bf16[64,1024]{1,0:T(8,128)(2,1)S(1)} %collective-permute-done.19.refs_1_, ...), custom_call_target="tpu_custom_call", output_to_operand_aliasing={{0}: (5, {}), {1}: (6, {})} | custom-call | tf_op jit(solution)/shard_map/pallas_call | solution.py:231
  (3 shorter events, 0.0 us)
Async XLA Ops:
  0.6 52.5 %copy-start = (f32[1,4,64,1024]{3,2,1,0:T(8,128)S(1)}, f32[1,4,64,1024]{3,2,1,0:T(8,128)}, u32[]{:S(2)}) copy-start(f32[1,4,64,1024]{3,2,1,0:T(8,128)} %param.9) | copy-start | bytes 3145732
  0.7 1.7 %copy-start.2 = (bf16[1,1,4,256,1024]{4,3,2,1,0:T(8,128)(2,1)S(1)}, bf16[1,1,4,256,1024]{4,3,2,1,0:T(8,128)(2,1)}, u32[]{:S(2)}) copy-start(bf16[1,1,4,256,1024]{4,3,2,1,0:T(8,128)(2,1)} %param.7) | copy-start | bytes 6291460
  2.3 6.5 %copy-start.6 = (bf16[1,1,4,256]{3,2,1,0:T(4,128)(2,1)S(1)}, bf16[1,1,4,256]{3,2,1,0:T(4,128)(2,1)}, u32[]{:S(2)}) copy-start(bf16[1,1,4,256]{3,2,1,0:T(4,128)(2,1)} %param.8) | copy-start | bytes 6148
  3.1 50.1 %collective-permute-start = (bf16[4,64,1024]{2,1,0:T(8,128)(2,1)S(1)}, bf16[4,64,1024]{2,1,0:T(8,128)(2,1)S(1)}, u32[]{:S(2)}, u32[]{:S(2)}) collective-permute-start(bf16[4,64,1024]{2,1,0:T(8,128)(2,1)S(1)} %get-tuple-element.34), channel_id=1, source_target_pairs={{0,24},{8,16},{16,8},{24,0},{1,25},{9,17},{17,9},{25,1},{2,26},{10... | collective-permute-start | bytes 1572872 | tf_op jit(solution)/shard_map/ppermute | solution.py:288
  8.2 45.0 %collective-permute-start.1 = (bf16[4,64,1024]{2,1,0:T(8,128)(2,1)S(1)}, bf16[4,64,1024]{2,1,0:T(8,128)(2,1)S(1)}, u32[]{:S(2)}, u32[]{:S(2)}) collective-permute-start(bf16[4,64,1024]{2,1,0:T(8,128)(2,1)S(1)} %get-tuple-element.35), channel_id=1, source_target_pairs={{0,16},{8,24},{16,0},{24,8},{1,17},{9,25},{17,1},{25,9},{2,18},{10... | collective-permute-start | bytes 1572872 | tf_op jit(solution)/shard_map/ppermute | solution.py:288
  8.2 45.0 %collective-permute-start.2 = (bf16[4,64,1024]{2,1,0:T(8,128)(2,1)S(1)}, bf16[4,64,1024]{2,1,0:T(8,128)(2,1)S(1)}, u32[]{:S(2)}, u32[]{:S(2)}) collective-permute-start(bf16[4,64,1024]{2,1,0:T(8,128)(2,1)S(1)} %get-tuple-element.36), channel_id=1, source_target_pairs={{0,8},{8,0},{16,24},{24,16},{1,9},{9,1},{17,25},{25,17},{2,10},{10... | collective-permute-start | bytes 1572872 | tf_op jit(solution)/shard_map/ppermute | solution.py:288
  66.2 42.6 %copy-start.1 = (bf16[1,4,64,1024]{3,2,1,0:T(8,128)(2,1)S(1)}, bf16[1,4,64,1024]{3,2,1,0:T(8,128)(2,1)}, u32[]{:S(2)}) copy-start(bf16[1,4,64,1024]{3,2,1,0:T(8,128)(2,1)} %param.10) | copy-start | bytes 1572868
  66.2 43.9 %copy-start.3 = (f32[1,4,64]{2,1,0:T(4,128)S(1)}, f32[1,4,64]{2,1,0:T(4,128)}, u32[]{:S(2)}) copy-start(f32[1,4,64]{2,1,0:T(4,128)} %param.11) | copy-start | bytes 3076
  66.2 43.9 %copy-start.4 = (f32[1,4,64]{2,1,0:T(4,128)S(1)}, f32[1,4,64]{2,1,0:T(4,128)}, u32[]{:S(2)}) copy-start(f32[1,4,64]{2,1,0:T(4,128)} %param.12) | copy-start | bytes 3076
  66.2 43.9 %copy-start.5 = (f32[1,4,64]{2,1,0:T(4,128)S(1)}, f32[1,4,64]{2,1,0:T(4,128)}, u32[]{:S(2)}) copy-start(f32[1,4,64]{2,1,0:T(4,128)} %param.13) | copy-start | bytes 3076
  67.2 6.4 %collective-permute-start.3 = (bf16[64,1024]{1,0:T(8,128)(2,1)S(1)}, bf16[64,1024]{1,0:T(8,128)(2,1)S(1)}, u32[]{:S(2)}, u32[]{:S(2)}) collective-permute-start(bf16[64,1024]{1,0:T(8,128)(2,1)S(1)} %get-tuple-element.42), channel_id=1, source_target_pairs={{0,8},{8,0},{16,24},{24,16},{1,9},{9,1},{17,25},{25,17},{2,10},{10... | collective-permute-start | bytes 393224 | tf_op jit(solution)/shard_map/ppermute | solution.py:288
  67.9 5.8 %collective-permute-start.10 = (bf16[64,1024]{1,0:T(8,128)(2,1)S(1)}, bf16[64,1024]{1,0:T(8,128)(2,1)S(1)}, u32[]{:S(2)}, u32[]{:S(2)}) collective-permute-start(bf16[64,1024]{1,0:T(8,128)(2,1)S(1)} %get-tuple-element.41.refs_0_), channel_id=1, source_target_pairs={{0,4},{2,6},{4,0},{6,2},{1,5},{3,7},{5,1},{7,3},{8,12},{10,14},{12... | collective-permute-start | bytes 393224 | tf_op jit(solution)/shard_map/ppermute | solution.py:288
  68.4 6.1 %collective-permute-start.5 = (bf16[64,1024]{1,0:T(8,128)(2,1)S(1)}, bf16[64,1024]{1,0:T(8,128)(2,1)S(1)}, u32[]{:S(2)}, u32[]{:S(2)}) collective-permute-start(bf16[64,1024]{1,0:T(8,128)(2,1)S(1)} %get-tuple-element.41.refs_0_), channel_id=1, source_target_pairs={{0,2},{2,0},{4,6},{6,4},{1,3},{3,1},{5,7},{7,5},{8,10},{10,8},{12,... | collective-permute-start | bytes 393224 | tf_op jit(solution)/shard_map/ppermute | solution.py:288
  69.1 10.6 %collective-permute-start.4 = (bf16[64,1024]{1,0:T(8,128)(2,1)S(1)}, bf16[64,1024]{1,0:T(8,128)(2,1)S(1)}, u32[]{:S(2)}, u32[]{:S(2)}) collective-permute-start(bf16[64,1024]{1,0:T(8,128)(2,1)S(1)} %get-tuple-element.43), channel_id=1, source_target_pairs={{0,16},{8,24},{16,0},{24,8},{1,17},{9,25},{17,1},{25,9},{2,18},{10... | collective-permute-start | bytes 393224 | tf_op jit(solution)/shard_map/ppermute | solution.py:288
  69.6 10.1 %collective-permute-start.8 = (bf16[64,1024]{1,0:T(8,128)(2,1)S(1)}, bf16[64,1024]{1,0:T(8,128)(2,1)S(1)}, u32[]{:S(2)}, u32[]{:S(2)}) collective-permute-start(bf16[64,1024]{1,0:T(8,128)(2,1)S(1)} %get-tuple-element.41.refs_0_), channel_id=1, source_target_pairs={{0,6},{2,4},{4,2},{6,0},{1,7},{3,5},{5,3},{7,1},{8,14},{10,12},{12... | collective-permute-start | bytes 393224 | tf_op jit(solution)/shard_map/ppermute | solution.py:288
  73.6 10.3 %collective-permute-start.11 = (bf16[64,1024]{1,0:T(8,128)(2,1)S(1)}, bf16[64,1024]{1,0:T(8,128)(2,1)S(1)}, u32[]{:S(2)}, u32[]{:S(2)}) collective-permute-start(bf16[64,1024]{1,0:T(8,128)(2,1)S(1)} %collective-permute-done.3.refs_1_), channel_id=1, source_target_pairs={{0,4},{2,6},{4,0},{6,2},{1,5},{3,7},{5,1},{7,3},{8,12},{10,14},{12... | collective-permute-start | bytes 393224 | tf_op jit(solution)/shard_map/ppermute | solution.py:288
  74.5 9.4 %collective-permute-start.6 = (bf16[64,1024]{1,0:T(8,128)(2,1)S(1)}, bf16[64,1024]{1,0:T(8,128)(2,1)S(1)}, u32[]{:S(2)}, u32[]{:S(2)}) collective-permute-start(bf16[64,1024]{1,0:T(8,128)(2,1)S(1)} %get-tuple-element.45), channel_id=1, source_target_pairs={{0,24},{8,16},{16,8},{24,0},{1,25},{9,17},{17,9},{25,1},{2,26},{10... | collective-permute-start | bytes 393224 | tf_op jit(solution)/shard_map/ppermute | solution.py:288
  79.7 9.2 %collective-permute-start.13 = (bf16[64,1024]{1,0:T(8,128)(2,1)S(1)}, bf16[64,1024]{1,0:T(8,128)(2,1)S(1)}, u32[]{:S(2)}, u32[]{:S(2)}) collective-permute-start(bf16[64,1024]{1,0:T(8,128)(2,1)S(1)} %collective-permute-done.4.refs_2_), channel_id=1, source_target_pairs={{0,4},{2,6},{4,0},{6,2},{1,5},{3,7},{5,1},{7,3},{8,12},{10,14},{12... | collective-permute-start | bytes 393224 | tf_op jit(solution)/shard_map/ppermute | solution.py:288
  81.0 7.3 %collective-permute-start.9 = (bf16[64,1024]{1,0:T(8,128)(2,1)S(1)}, bf16[64,1024]{1,0:T(8,128)(2,1)S(1)}, u32[]{:S(2)}, u32[]{:S(2)}) collective-permute-start(bf16[64,1024]{1,0:T(8,128)(2,1)S(1)} %collective-permute-done.4.refs_2_), channel_id=1, source_target_pairs={{0,2},{2,0},{4,6},{6,4},{1,3},{3,1},{5,7},{7,5},{8,10},{10,8},{12,... | collective-permute-start | bytes 393224 | tf_op jit(solution)/shard_map/ppermute | solution.py:288
  83.9 6.9 %collective-permute-start.7 = (bf16[64,1024]{1,0:T(8,128)(2,1)S(1)}, bf16[64,1024]{1,0:T(8,128)(2,1)S(1)}, u32[]{:S(2)}, u32[]{:S(2)}) collective-permute-start(bf16[64,1024]{1,0:T(8,128)(2,1)S(1)} %collective-permute-done.3.refs_1_), channel_id=1, source_target_pairs={{0,2},{2,0},{4,6},{6,4},{1,3},{3,1},{5,7},{7,5},{8,10},{10,8},{12,... | collective-permute-start | bytes 393224 | tf_op jit(solution)/shard_map/ppermute | solution.py:288
  84.0 9.8 %collective-permute-start.17 = (bf16[64,1024]{1,0:T(8,128)(2,1)S(1)}, bf16[64,1024]{1,0:T(8,128)(2,1)S(1)}, u32[]{:S(2)}, u32[]{:S(2)}) collective-permute-start(bf16[64,1024]{1,0:T(8,128)(2,1)S(1)} %collective-permute-done.6.refs_3_), channel_id=1, source_target_pairs={{0,6},{2,4},{4,2},{6,0},{1,7},{3,5},{5,3},{7,1},{8,14},{10,12},{12... | collective-permute-start | bytes 393224 | tf_op jit(solution)/shard_map/ppermute | solution.py:288
  85.9 7.7 %collective-permute-start.15 = (bf16[64,1024]{1,0:T(8,128)(2,1)S(1)}, bf16[64,1024]{1,0:T(8,128)(2,1)S(1)}, u32[]{:S(2)}, u32[]{:S(2)}) collective-permute-start(bf16[64,1024]{1,0:T(8,128)(2,1)S(1)} %collective-permute-done.11.refs_9_), channel_id=1, source_target_pairs={{0,2},{2,0},{4,6},{6,4},{1,3},{3,1},{5,7},{7,5},{8,10},{10,8},{12,... | collective-permute-start | bytes 393224 | tf_op jit(solution)/shard_map/ppermute | solution.py:288
  88.4 5.5 %collective-permute-start.16 = (bf16[64,1024]{1,0:T(8,128)(2,1)S(1)}, bf16[64,1024]{1,0:T(8,128)(2,1)S(1)}, u32[]{:S(2)}, u32[]{:S(2)}) collective-permute-start(bf16[64,1024]{1,0:T(8,128)(2,1)S(1)} %collective-permute-done.9.refs_6_), channel_id=1, source_target_pairs={{0,4},{2,6},{4,0},{6,2},{1,5},{3,7},{5,1},{7,3},{8,12},{10,14},{12... | collective-permute-start | bytes 393224 | tf_op jit(solution)/shard_map/ppermute | solution.py:288
  88.9 6.4 %collective-permute-start.14 = (bf16[64,1024]{1,0:T(8,128)(2,1)S(1)}, bf16[64,1024]{1,0:T(8,128)(2,1)S(1)}, u32[]{:S(2)}, u32[]{:S(2)}) collective-permute-start(bf16[64,1024]{1,0:T(8,128)(2,1)S(1)} %collective-permute-done.6.refs_3_), channel_id=1, source_target_pairs={{0,4},{2,6},{4,0},{6,2},{1,5},{3,7},{5,1},{7,3},{8,12},{10,14},{12... | collective-permute-start | bytes 393224 | tf_op jit(solution)/shard_map/ppermute | solution.py:288
  90.8 5.0 %collective-permute-start.12 = (bf16[64,1024]{1,0:T(8,128)(2,1)S(1)}, bf16[64,1024]{1,0:T(8,128)(2,1)S(1)}, u32[]{:S(2)}, u32[]{:S(2)}) collective-permute-start(bf16[64,1024]{1,0:T(8,128)(2,1)S(1)} %collective-permute-done.6.refs_3_), channel_id=1, source_target_pairs={{0,2},{2,0},{4,6},{6,4},{1,3},{3,1},{5,7},{7,5},{8,10},{10,8},{12,... | collective-permute-start | bytes 393224 | tf_op jit(solution)/shard_map/ppermute | solution.py:288
  104.3 7.6 %collective-permute-start.18 = (bf16[64,1024]{1,0:T(8,128)(2,1)S(1)}, bf16[64,1024]{1,0:T(8,128)(2,1)S(1)}, u32[]{:S(2)}, u32[]{:S(2)}) collective-permute-start(bf16[64,1024]{1,0:T(8,128)(2,1)S(1)} %get-tuple-element.54), channel_id=1, source_target_pairs={{0,24},{8,16},{16,8},{24,0},{1,25},{9,17},{17,9},{25,1},{2,26},{10... | collective-permute-start | bytes 393224 | tf_op jit(solution)/shard_map/ppermute | solution.py:288
  105.8 9.0 %collective-permute-start.19 = (bf16[64,1024]{1,0:T(8,128)(2,1)S(1)}, bf16[64,1024]{1,0:T(8,128)(2,1)S(1)}, u32[]{:S(2)}, u32[]{:S(2)}) collective-permute-start(bf16[64,1024]{1,0:T(8,128)(2,1)S(1)} %get-tuple-element.55), channel_id=1, source_target_pairs={{0,16},{8,24},{16,0},{24,8},{1,17},{9,25},{17,1},{25,9},{2,18},{10... | collective-permute-start | bytes 393224 | tf_op jit(solution)/shard_map/ppermute | solution.py:288
  105.8 9.0 %collective-permute-start.20 = (bf16[64,1024]{1,0:T(8,128)(2,1)S(1)}, bf16[64,1024]{1,0:T(8,128)(2,1)S(1)}, u32[]{:S(2)}, u32[]{:S(2)}) collective-permute-start(bf16[64,1024]{1,0:T(8,128)(2,1)S(1)} %get-tuple-element.56), channel_id=1, source_target_pairs={{0,8},{8,0},{16,24},{24,16},{1,9},{9,1},{17,25},{25,17},{2,10},{10... | collective-permute-start | bytes 393224 | tf_op jit(solution)/shard_map/ppermute | solution.py:288

commit v3 on v2

--- a/solution.py
+++ b/solution.py
@@ -27,6 +27,7 @@
 MIB = 2**20
 LANES = 128
 MESH_AXES = ("shard", "tensor", "section")
+TURNS = ((0, 2, 1, 3), (0, 1, 2, 3))
 
 
 def gram_of(blocks, gram_ref):
@@ -190,7 +191,7 @@
     inverse = 1.0 / (jnp.sqrt(jnp.maximum(update_norm, 0.0)) + 1e-07)
     position = lax.broadcasted_iota(jnp.int32, inverse.shape, 0)
     for place in range(matrix_count):
-        matrix = place_ref[place]
+        matrix = place_ref[matrix_count + 1 + place]
         factor = jnp.sum(jnp.where(position == matrix, inverse, 0.0), axis=0, keepdims=True)
         clipped = clip * grad_ref[matrix]
         new_momentum = mom_beta * momentum_ref[matrix] + clipped
@@ -205,7 +206,7 @@
     step_size = muon_rate * (0.2 * math.sqrt(D))
     copies = []
     for slot, offset in enumerate(offsets):
-        matrix = place_ref[offset]
+        matrix = place_ref[weights_ref.shape[0] + 1 + offset]
         update = arrived[slot][...]
         update_rows[slot] = update
         weight_rows[slot] = (
@@ -288,6 +289,16 @@
     return lax.ppermute(array, axis, pairs)
 
 
+def traded(array, slot):
+    sections = lax.axis_size("section")
+    pairs = [
+        (shard * sections + section, (shard ^ TURNS[section % 2][slot]) * sections + section)
+        for shard in range(lax.axis_size("shard"))
+        for section in range(sections)
+    ]
+    return lax.ppermute(array, ("shard", "section"), pairs)
+
+
 def after(array, earlier):
     return lax.optimization_barrier((array, earlier))[0]
 
@@ -303,11 +314,16 @@
         )
     vector_count, vector_width = vectors.shape[1:]
     own_momentum = momentum[0]
-    position = jnp.arange(shard_count + 1, dtype=jnp.int32)
+    position = jnp.arange(2 * shard_count + 1, dtype=jnp.int32)
+    section_index = lax.axis_index("section").astype(jnp.int32)
+    slot = position - shard_count - 1
+    swap = (slot == 1) | (slot == 2)
+    offset = jnp.where(swap & (section_index % 2 == 0), 3 - slot, slot)
     place = jnp.where(
         position == shard_count,
-        lax.axis_index("section").astype(jnp.int32),
-        lax.axis_index("shard").astype(jnp.int32) ^ position,
+        section_index,
+        lax.axis_index("shard").astype(jnp.int32)
+        ^ jnp.where(position < shard_count, position, offset),
     )
 
     by_rows = grad_parts.reshape(matrix_count, shard_count, local_height, width)
@@ -349,26 +365,26 @@
     )
 
     pieces = [scaled[0]] + [None] * 3
-    for offset in (2, 1):
-        pieces[offset] = swapped(scaled[offset], "shard", offset)
+    pieces[1] = traded(scaled[1], 1)
     near, side, far = [None] * 4, [None] * 4, [None] * 4
     near[0] = swapped(pieces[0], "tensor", 1)
     side[0] = swapped(pieces[0], "tensor", 2)
     far[0] = swapped(pieces[0], "tensor", 3)
-    pieces[3] = swapped(after(scaled[3], near[0]), "shard", 3)
+    pieces[2] = traded(after(scaled[2], pieces[1]), 2)
+    pieces[3] = traded(after(scaled[3], side[0]), 3)
     near[1] = swapped(after(pieces[1], near[0]), "tensor", 1)
     side[1] = swapped(after(pieces[1], side[0]), "tensor", 2)
     far[1] = swapped(side[1], "tensor", 1)
-    near[2] = swapped(after(pieces[2], far[0]), "tensor", 1)
-    side[2] = swapped(after(pieces[2], far[0]), "tensor", 2)
+    near[2] = swapped(pieces[2], "tensor", 1)
+    side[2] = swapped(after(pieces[2], near[1]), "tensor", 2)
     far[2] = swapped(near[2], "tensor", 2)
-    near[3] = swapped(after(pieces[3], side[1]), "tensor", 1)
-    side[3] = swapped(after(pieces[3], side[1]), "tensor", 2)
-    far[3] = swapped(after(pieces[3], side[1]), "tensor", 3)
+    near[3] = swapped(after(pieces[3], (side[1], near[1])), "tensor", 1)
+    side[3] = swapped(after(pieces[3], (side[1], near[1])), "tensor", 2)
+    far[3] = swapped(after(pieces[3], (side[1], near[1])), "tensor", 3)
     results = orthogonalize([pieces, near, side, far])
 
     returned = {
-        offset: swapped(results[offset], "shard", offset)
+        offset: traded(results[offset], offset)
         for offset in reversed(range(1, shard_count))
     }
     early = finished((0,), place, [results[0]], weights[0])

time: 116 us -> 117 us (level)
  waiting for transfers between devices: 15 us -> 20 us
  starting transfers between devices: 26.6 us -> 22.4 us
    ppermute x0 -> x6, waiting for transfers between devices: none -> 13.1 us  [traded(): return lax.ppermute(array, ('shard', 'section'), pairs)]
    ppermute x21 -> x15, starting transfers between devices: 26.6 us -> 16.8 us  [swapped(): return lax.ppermute(array, axis, pairs)]
    ppermute x21 -> x15, waiting for transfers between devices: 15 us -> 6.86 us  [swapped(): return lax.ppermute(array, axis, pairs)]
    ppermute x0 -> x6, starting transfers between devices: none -> 5.6 us  [traded(): return lax.ppermute(array, ('shard', 'section'), pairs)]
where the time goes in v3:
time: 117 us
  blocking collectives  56 us (48%)
  starting transfers between devices  22.4 us (19%)
  waiting for transfers between devices  20 us (17%)
  Pallas kernels  16.2 us (14%)
  local copies, waits for them, and re-layouts  1.7 us (1%)
    all_to_all x1, blocking collectives, per_device(): lax.all_to_all(jnp.broadcast_to(vector_grads[0], (shard_count, vector_cou...  44.3 us
    ppermute x15, starting transfers between devices, swapped(): return lax.ppermute(array, axis, pairs)  16.8 us
    ppermute x6, waiting for transfers between devices, traded(): return lax.ppermute(array, ('shard', 'section'), pairs)  13.1 us
    all_to_all x1, blocking collectives, per_device(): lax.all_to_all(figures.reshape(others * section_count, 1, LANES), MESH_AX...  11.7 us
    pallas_call x1, Pallas kernels, orthogonalize(): pl.pallas_call(functools.partial(orthogonalize_kernel, count, pieces), ou...  8.55 us
    ppermute x15, waiting for transfers between devices, swapped(): return lax.ppermute(array, axis, pairs)  6.86 us
    ppermute x6, starting transfers between devices, traded(): return lax.ppermute(array, ('shard', 'section'), pairs)  5.6 us
    pallas_call x3, Pallas kernels, on_device(): pl.pallas_call(kernel, out_shape=out_shape, in_specs=[pl.BlockSpec(memory...  4.2 us
  transfers between devices with their start and end apart: 21, of which 10 were waited for; matrix products, arithmetic and copies ran while one was open for 0% of the time, Pallas kernels for 3%

profile of v3, /device:TPU:0, one launch (start us, length us, event | category | flops | bytes accessed | tf_op | source)
XLA Modules:
  0.0 117.1 jit_solution(10743756028282277926)
XLA Ops:
  0.6 0.0 copy-start
  0.7 0.0 copy-start.2
  0.7 1.7 %copy-done.2 = bf16[1,1,4,256,1024]{4,3,2,1,0:T(8,128)(2,1)S(1)} copy-done((bf16[1,1,4,256,1024]{4,3,2,1,0:T(8,128)(2,1)S(1)}, bf16[1,1,4,256,1024]{4,3,2,1,0:T(8,128)(2,1)}, u32[]{:S(2)}) %copy-start.2) | copy-done | bytes 2097176
  2.3 0.0 copy-start.6
  2.3 0.7 shard_map.110
  3.1 5.1 %collective-permute-start = (bf16[4,64,1024]{2,1,0:T(8,128)(2,1)S(1)}, bf16[4,64,1024]{2,1,0:T(8,128)(2,1)S(1)}, u32[]{:S(2)}, u32[]{:S(2)}) collective-permute-start(bf16[4,64,1024]{2,1,0:T(8,128)(2,1)S(1)} %get-tuple-element.35), channel_id=1, source_target_pairs={{0,24},{8,16},{16,8},{24,0},{1,25},{9,17},{17,9},{25,1},{2,26},{10... | collective-permute-start | bytes 1572872 | tf_op jit(solution)/shard_map/ppermute | solution.py:289
  8.2 0.0 collective-permute-start.1
  8.2 0.6 collective-permute-start.2
  8.8 0.0 copy-done.6
  8.9 44.3 %all_to_all.10.refs_4_ = bf16[4,4,256]{2,1,0:T(4,128)(2,1)S(1)} all-to-all(bf16[4,4,256]{2,1,0:T(4,128)(2,1)S(1)} %broadcast_in_dim.28), channel_id=1, replica_groups=mesh['shard'=4,'tensor'=4,'section'=2] {'shard'}, dimensions={0} | all-to-all | bytes 16384 | tf_op jit(solution)/shard_map/all_to_all | solution.py:333
  53.2 0.0 collective-permute-done.refs_0_
  53.2 0.0 collective-permute-done.1.refs_1_
  53.2 0.0 collective-permute-done.2.refs_2_
  53.2 0.0 copy-done
  53.2 1.3 %shard_map.111 = (f32[4,64,1024]{2,1,0:T(8,128)S(1)}, f32[4,256]{1,0:T(4,128)S(1)}, f32[16,2,1,128]{3,2,1,0:T(1,128)S(1)}) custom-call(s32[9]{0:T(128)S(1)} %compare_select_fusion.1.place_ref, bf16[4,64,1024]{2,1,0:T(8,128)(2,1)S(1)} %collective-permute-done.refs_0_, bf16[4,64,1024]{2,1,0:T(8,128)(2,1)S(1)} %collective-permute-done.1.refs_1_, ...), custom_call_target="tpu_custom_call" | custom-call | tf_op jit(solution)/shard_map/pallas_call | solution.py:278
  54.5 11.7 %all_to_all.11.figures_ref = f32[32,1,128]{2,1,0:T(1,128)S(1)} all-to-all(f32[32,1,128]{2,1,0:T(1,128)S(1)} %bitcast.19), channel_id=1, replica_groups=mesh['shard'=4,'tensor'=4,'section'=2] {'shard','tensor','section'}, dimensions={0} | all-to-all | bytes 32768 | tf_op jit(solution)/shard_map/all_to_all | solution.py:352
  66.2 0.0 copy-start.1
  66.2 0.0 copy-start.3
  66.2 0.0 copy-start.4
  66.2 1.0 shard_map.112
  67.3 0.7 collective-permute-start.3
  67.9 0.5 collective-permute-start.7
  68.4 0.6 collective-permute-start.5
  69.0 7.0 %collective-permute-done.3.refs_1_ = bf16[64,1024]{1,0:T(8,128)(2,1)S(1)} collective-permute-done((bf16[64,1024]{1,0:T(8,128)(2,1)S(1)}, bf16[64,1024]{1,0:T(8,128)(2,1)S(1)}, u32[]{:S(2)}, u32[]{:S(2)}) %collective-permute-start.3) | collective-permute-done | bytes 131104 | tf_op jit(solution)/shard_map/ppermute | solution.py:299
  76.0 0.0 collective-permute-start.4
  76.0 0.0 collective-permute-done.7.refs_4_
  76.0 0.0 collective-permute-start.8
  76.0 0.0 collective-permute-done.5.refs_8_
  76.0 0.1 collective-permute-start.6
  76.2 0.7 collective-permute-start.10
  76.9 2.6 %collective-permute-start.14 = (bf16[64,1024]{1,0:T(8,128)(2,1)S(1)}, bf16[64,1024]{1,0:T(8,128)(2,1)S(1)}, u32[]{:S(2)}, u32[]{:S(2)}) collective-permute-start(bf16[64,1024]{1,0:T(8,128)(2,1)S(1)} %get-tuple-element.42.refs_0_), channel_id=1, source_target_pairs={{0,6},{2,4},{4,2},{6,0},{1,7},{3,5},{5,3},{7,1},{8,14},{10,12},{12... | collective-permute-start | bytes 393224 | tf_op jit(solution)/shard_map/ppermute | solution.py:289
  79.5 1.5 %collective-permute-done.4.refs_2_ = bf16[64,1024]{1,0:T(8,128)(2,1)S(1)} collective-permute-done((bf16[64,1024]{1,0:T(8,128)(2,1)S(1)}, bf16[64,1024]{1,0:T(8,128)(2,1)S(1)}, u32[]{:S(2)}, u32[]{:S(2)}) %collective-permute-start.4) | collective-permute-done | bytes 131104 | tf_op jit(solution)/shard_map/ppermute | solution.py:299
  81.0 0.0 collective-permute-done.8.refs_5_
  81.0 0.9 collective-permute-start.9
  81.8 0.2 collective-permute-start.12
  82.0 0.9 collective-permute-done.6.refs_3_
  83.0 0.0 collective-permute-done.10.refs_9_
  83.0 1.5 %collective-permute-start.17 = (bf16[64,1024]{1,0:T(8,128)(2,1)S(1)}, bf16[64,1024]{1,0:T(8,128)(2,1)S(1)}, u32[]{:S(2)}, u32[]{:S(2)}) collective-permute-start(bf16[64,1024]{1,0:T(8,128)(2,1)S(1)} %collective-permute-done.6.refs_3_), channel_id=1, source_target_pairs={{0,6},{2,4},{4,2},{6,0},{1,7},{3,5},{5,3},{7,1},{8,14},{10,12},{12... | collective-permute-start | bytes 393224 | tf_op jit(solution)/shard_map/ppermute | solution.py:289
  84.5 2.3 %collective-permute-start.13 = (bf16[64,1024]{1,0:T(8,128)(2,1)S(1)}, bf16[64,1024]{1,0:T(8,128)(2,1)S(1)}, u32[]{:S(2)}, u32[]{:S(2)}) collective-permute-start(bf16[64,1024]{1,0:T(8,128)(2,1)S(1)} %collective-permute-done.6.refs_3_), channel_id=1, source_target_pairs={{0,4},{2,6},{4,0},{6,2},{1,5},{3,7},{5,1},{7,3},{8,12},{10,14},{12... | collective-permute-start | bytes 393224 | tf_op jit(solution)/shard_map/ppermute | solution.py:289
  86.8 0.0 collective-permute-done.14.refs_12_
  86.8 0.0 collective-permute-start.11
  86.8 0.6 collective-permute-done.9.refs_6_
  87.4 1.4 %collective-permute-start.15 = (bf16[64,1024]{1,0:T(8,128)(2,1)S(1)}, bf16[64,1024]{1,0:T(8,128)(2,1)S(1)}, u32[]{:S(2)}, u32[]{:S(2)}) collective-permute-start(bf16[64,1024]{1,0:T(8,128)(2,1)S(1)} %collective-permute-done.10.refs_9_), channel_id=1, source_target_pairs={{0,2},{2,0},{4,6},{6,4},{1,3},{3,1},{5,7},{7,5},{8,10},{10,8},{12,... | collective-permute-start | bytes 393224 | tf_op jit(solution)/shard_map/ppermute | solution.py:289
  88.9 1.5 %collective-permute-done.12.refs_10_ = bf16[64,1024]{1,0:T(8,128)(2,1)S(1)} collective-permute-done((bf16[64,1024]{1,0:T(8,128)(2,1)S(1)}, bf16[64,1024]{1,0:T(8,128)(2,1)S(1)}, u32[]{:S(2)}, u32[]{:S(2)}) %collective-permute-start.12) | collective-permute-done | bytes 131104 | tf_op jit(solution)/shard_map/ppermute | solution.py:289
  90.4 0.3 collective-permute-start.16
  90.6 0.0 collective-permute-done.17.refs_15_
  90.6 1.9 %collective-permute-done.13.refs_11_ = bf16[64,1024]{1,0:T(8,128)(2,1)S(1)} collective-permute-done((bf16[64,1024]{1,0:T(8,128)(2,1)S(1)}, bf16[64,1024]{1,0:T(8,128)(2,1)S(1)}, u32[]{:S(2)}, u32[]{:S(2)}) %collective-permute-start.13) | collective-permute-done | bytes 131104 | tf_op jit(solution)/shard_map/ppermute | solution.py:289
  92.6 0.0 collective-permute-done.11.refs_7_
  92.6 1.3 %collective-permute-done.15.refs_13_ = bf16[64,1024]{1,0:T(8,128)(2,1)S(1)} collective-permute-done((bf16[64,1024]{1,0:T(8,128)(2,1)S(1)}, bf16[64,1024]{1,0:T(8,128)(2,1)S(1)}, u32[]{:S(2)}, u32[]{:S(2)}) %collective-permute-start.15) | collective-permute-done | bytes 131104 | tf_op jit(solution)/shard_map/ppermute | solution.py:289
  93.9 1.5 %collective-permute-done.16.refs_14_ = bf16[64,1024]{1,0:T(8,128)(2,1)S(1)} collective-permute-done((bf16[64,1024]{1,0:T(8,128)(2,1)S(1)}, bf16[64,1024]{1,0:T(8,128)(2,1)S(1)}, u32[]{:S(2)}, u32[]{:S(2)}) %collective-permute-start.16) | collective-permute-done | bytes 131104 | tf_op jit(solution)/shard_map/ppermute | solution.py:289
  95.4 8.5 %shard_map.113 = (bf16[64,1024]{1,0:T(8,128)(2,1)S(1)}, bf16[64,1024]{1,0:T(8,128)(2,1)S(1)}, bf16[64,1024]{1,0:T(8,128)(2,1)S(1)}, bf16[64,1024]{1,0:T(8,128)(2,1)S(1)}) custom-call(bf16[64,1024]{1,0:T(8,128)(2,1)S(1)} %get-tuple-element.42.refs_0_, bf16[64,1024]{1,0:T(8,128)(2,1)S(1)} %collective-permute-done.3.refs_1_, ...), custom_call_target="tpu_custom_call" | custom-call | tf_op jit(solution)/shard_map/pallas_call | solution.py:92
  103.9 4.2 %collective-permute-start.18 = (bf16[64,1024]{1,0:T(8,128)(2,1)S(1)}, bf16[64,1024]{1,0:T(8,128)(2,1)S(1)}, u32[]{:S(2)}, u32[]{:S(2)}) collective-permute-start(bf16[64,1024]{1,0:T(8,128)(2,1)S(1)} %get-tuple-element.56), channel_id=1, source_target_pairs={{0,24},{1,25},{8,16},{9,17},{16,8},{17,9},{24,0},{25,1},{2,26},{3,... | collective-permute-start | bytes 393224 | tf_op jit(solution)/shard_map/ppermute | solution.py:299
  108.1 0.2 collective-permute-start.19
  108.3 0.5 collective-permute-start.20
  108.7 0.0 copy-done.1
  108.7 1.3 %shard_map.115 = (bf16[4,64,1024]{2,1,0:T(8,128)(2,1)}, bf16[4,64,1024]{2,1,0:T(8,128)(2,1)}) custom-call(s32[9]{0:T(128)S(1)} %compare_select_fusion.1.place_ref, bf16[64,1024]{1,0:T(8,128)(2,1)S(1)} %get-tuple-element.52.refs_0_, bf16[4,64,1024]{2,1,0:T(8,128)(2,1)S(1)} %bitcast.16), custom_call_target="tpu_custom_call" | custom-call | tf_op jit(solution)/shard_map/pallas_call | solution.py:232
  110.0 0.0 copy-done.3
  110.0 0.0 copy-done.4
  110.0 0.0 copy-done.5
  110.0 1.8 %shard_map.114 = (f32[4,64,1024]{2,1,0:T(8,128)}, f32[4,64]{1,0:T(4,128)}, f32[4,64]{1,0:T(4,128)}) custom-call(s32[9]{0:T(128)S(1)} %compare_select_fusion.1.place_ref, f32[8,128]{1,0:T(8,128)S(1)} %get-tuple-element.53.clip_ref, f32[4,64,1024]{2,1,0:T(8,128)S(1)} %get-tuple-element.40.grad_ref, f32[4,64,1024]{2,1,0:T(8,128)S(1)} %bitcast.15, ...), custom_call_target="tpu_custom_call" | custom-call | tf_op jit(solution)/shard_map/pallas_call | solution.py:278
  111.9 0.0 collective-permute-done.18.refs_0_
  111.9 2.5 %collective-permute-done.19.refs_1_ = bf16[64,1024]{1,0:T(8,128)(2,1)S(1)} collective-permute-done((bf16[64,1024]{1,0:T(8,128)(2,1)S(1)}, bf16[64,1024]{1,0:T(8,128)(2,1)S(1)}, u32[]{:S(2)}, u32[]{:S(2)}) %collective-permute-start.19) | collective-permute-done | bytes 131104 | tf_op jit(solution)/shard_map/ppermute | solution.py:299
  114.4 1.2 %collective-permute-done.20.refs_2_ = bf16[64,1024]{1,0:T(8,128)(2,1)S(1)} collective-permute-done((bf16[64,1024]{1,0:T(8,128)(2,1)S(1)}, bf16[64,1024]{1,0:T(8,128)(2,1)S(1)}, u32[]{:S(2)}, u32[]{:S(2)}) %collective-permute-start.20) | collective-permute-done | bytes 131104 | tf_op jit(solution)/shard_map/ppermute | solution.py:299
  115.6 1.5 %shard_map.116 = (bf16[4,64,1024]{2,1,0:T(8,128)(2,1)}, bf16[4,64,1024]{2,1,0:T(8,128)(2,1)}) custom-call(s32[9]{0:T(128)S(1)} %compare_select_fusion.1.place_ref, bf16[64,1024]{1,0:T(8,128)(2,1)S(1)} %collective-permute-done.18.refs_0_, bf16[64,1024]{1,0:T(8,128)(2,1)S(1)} %collective-permute-done.19.refs_1_, ...), custom_call_target="tpu_custom_call", output_to_operand_aliasing={{0}: (5, {}), {1}: (6, {})} | custom-call | tf_op jit(solution)/shard_map/pallas_call | solution.py:232
  (3 shorter events, 0.0 us)
Async XLA Ops:
  0.6 52.5 %copy-start = (f32[1,4,64,1024]{3,2,1,0:T(8,128)S(1)}, f32[1,4,64,1024]{3,2,1,0:T(8,128)}, u32[]{:S(2)}) copy-start(f32[1,4,64,1024]{3,2,1,0:T(8,128)} %param.9) | copy-start | bytes 3145732
  0.7 1.7 %copy-start.2 = (bf16[1,1,4,256,1024]{4,3,2,1,0:T(8,128)(2,1)S(1)}, bf16[1,1,4,256,1024]{4,3,2,1,0:T(8,128)(2,1)}, u32[]{:S(2)}) copy-start(bf16[1,1,4,256,1024]{4,3,2,1,0:T(8,128)(2,1)} %param.7) | copy-start | bytes 6291460
  2.3 6.5 %copy-start.6 = (bf16[1,1,4,256]{3,2,1,0:T(4,128)(2,1)S(1)}, bf16[1,1,4,256]{3,2,1,0:T(4,128)(2,1)}, u32[]{:S(2)}) copy-start(bf16[1,1,4,256]{3,2,1,0:T(4,128)(2,1)} %param.8) | copy-start | bytes 6148
  3.1 50.1 %collective-permute-start = (bf16[4,64,1024]{2,1,0:T(8,128)(2,1)S(1)}, bf16[4,64,1024]{2,1,0:T(8,128)(2,1)S(1)}, u32[]{:S(2)}, u32[]{:S(2)}) collective-permute-start(bf16[4,64,1024]{2,1,0:T(8,128)(2,1)S(1)} %get-tuple-element.35), channel_id=1, source_target_pairs={{0,24},{8,16},{16,8},{24,0},{1,25},{9,17},{17,9},{25,1},{2,26},{10... | collective-permute-start | bytes 1572872 | tf_op jit(solution)/shard_map/ppermute | solution.py:289
  8.2 45.0 %collective-permute-start.1 = (bf16[4,64,1024]{2,1,0:T(8,128)(2,1)S(1)}, bf16[4,64,1024]{2,1,0:T(8,128)(2,1)S(1)}, u32[]{:S(2)}, u32[]{:S(2)}) collective-permute-start(bf16[4,64,1024]{2,1,0:T(8,128)(2,1)S(1)} %get-tuple-element.36), channel_id=1, source_target_pairs={{0,16},{8,24},{16,0},{24,8},{1,17},{9,25},{17,1},{25,9},{2,18},{10... | collective-permute-start | bytes 1572872 | tf_op jit(solution)/shard_map/ppermute | solution.py:289
  8.2 45.0 %collective-permute-start.2 = (bf16[4,64,1024]{2,1,0:T(8,128)(2,1)S(1)}, bf16[4,64,1024]{2,1,0:T(8,128)(2,1)S(1)}, u32[]{:S(2)}, u32[]{:S(2)}) collective-permute-start(bf16[4,64,1024]{2,1,0:T(8,128)(2,1)S(1)} %get-tuple-element.37), channel_id=1, source_target_pairs={{0,8},{8,0},{16,24},{24,16},{1,9},{9,1},{17,25},{25,17},{2,10},{10... | collective-permute-start | bytes 1572872 | tf_op jit(solution)/shard_map/ppermute | solution.py:289
  66.2 42.5 %copy-start.1 = (bf16[1,4,64,1024]{3,2,1,0:T(8,128)(2,1)S(1)}, bf16[1,4,64,1024]{3,2,1,0:T(8,128)(2,1)}, u32[]{:S(2)}) copy-start(bf16[1,4,64,1024]{3,2,1,0:T(8,128)(2,1)} %param.10) | copy-start | bytes 1572868
  66.2 43.8 %copy-start.3 = (f32[1,4,64]{2,1,0:T(4,128)S(1)}, f32[1,4,64]{2,1,0:T(4,128)}, u32[]{:S(2)}) copy-start(f32[1,4,64]{2,1,0:T(4,128)} %param.11) | copy-start | bytes 3076
  66.2 43.8 %copy-start.4 = (f32[1,4,64]{2,1,0:T(4,128)S(1)}, f32[1,4,64]{2,1,0:T(4,128)}, u32[]{:S(2)}) copy-start(f32[1,4,64]{2,1,0:T(4,128)} %param.12) | copy-start | bytes 3076
  66.2 43.8 %copy-start.5 = (f32[1,4,64]{2,1,0:T(4,128)S(1)}, f32[1,4,64]{2,1,0:T(4,128)}, u32[]{:S(2)}) copy-start(f32[1,4,64]{2,1,0:T(4,128)} %param.13) | copy-start | bytes 3076
  67.3 8.8 %collective-permute-start.3 = (bf16[64,1024]{1,0:T(8,128)(2,1)S(1)}, bf16[64,1024]{1,0:T(8,128)(2,1)S(1)}, u32[]{:S(2)}, u32[]{:S(2)}) collective-permute-start(bf16[64,1024]{1,0:T(8,128)(2,1)S(1)} %get-tuple-element.43), channel_id=1, source_target_pairs={{0,16},{1,9},{8,24},{9,1},{16,0},{17,25},{24,8},{25,17},{2,18},{3,... | collective-permute-start | bytes 393224 | tf_op jit(solution)/shard_map/ppermute | solution.py:299
  67.9 8.1 %collective-permute-start.7 = (bf16[64,1024]{1,0:T(8,128)(2,1)S(1)}, bf16[64,1024]{1,0:T(8,128)(2,1)S(1)}, u32[]{:S(2)}, u32[]{:S(2)}) collective-permute-start(bf16[64,1024]{1,0:T(8,128)(2,1)S(1)} %get-tuple-element.42.refs_0_), channel_id=1, source_target_pairs={{0,2},{2,0},{4,6},{6,4},{1,3},{3,1},{5,7},{7,5},{8,10},{10,8},{12,... | collective-permute-start | bytes 393224 | tf_op jit(solution)/shard_map/ppermute | solution.py:289
  68.4 7.6 %collective-permute-start.5 = (bf16[64,1024]{1,0:T(8,128)(2,1)S(1)}, bf16[64,1024]{1,0:T(8,128)(2,1)S(1)}, u32[]{:S(2)}, u32[]{:S(2)}) collective-permute-start(bf16[64,1024]{1,0:T(8,128)(2,1)S(1)} %get-tuple-element.42.refs_0_), channel_id=1, source_target_pairs={{0,4},{2,6},{4,0},{6,2},{1,5},{3,7},{5,1},{7,3},{8,12},{10,14},{12... | collective-permute-start | bytes 393224 | tf_op jit(solution)/shard_map/ppermute | solution.py:289
  76.0 5.0 %collective-permute-start.4 = (bf16[64,1024]{1,0:T(8,128)(2,1)S(1)}, bf16[64,1024]{1,0:T(8,128)(2,1)S(1)}, u32[]{:S(2)}, u32[]{:S(2)}) collective-permute-start(bf16[64,1024]{1,0:T(8,128)(2,1)S(1)} %get-tuple-element.45), channel_id=1, source_target_pairs={{0,8},{1,17},{8,0},{9,25},{16,24},{17,1},{24,16},{25,9},{2,10},{3,... | collective-permute-start | bytes 393224 | tf_op jit(solution)/shard_map/ppermute | solution.py:299
  76.0 5.0 %collective-permute-start.8 = (bf16[64,1024]{1,0:T(8,128)(2,1)S(1)}, bf16[64,1024]{1,0:T(8,128)(2,1)S(1)}, u32[]{:S(2)}, u32[]{:S(2)}) collective-permute-start(bf16[64,1024]{1,0:T(8,128)(2,1)S(1)} %collective-permute-done.3.refs_1_), channel_id=1, source_target_pairs={{0,2},{2,0},{4,6},{6,4},{1,3},{3,1},{5,7},{7,5},{8,10},{10,8},{12,... | collective-permute-start | bytes 393224 | tf_op jit(solution)/shard_map/ppermute | solution.py:289
  76.0 6.9 %collective-permute-start.6 = (bf16[64,1024]{1,0:T(8,128)(2,1)S(1)}, bf16[64,1024]{1,0:T(8,128)(2,1)S(1)}, u32[]{:S(2)}, u32[]{:S(2)}) collective-permute-start(bf16[64,1024]{1,0:T(8,128)(2,1)S(1)} %get-tuple-element.47), channel_id=1, source_target_pairs={{0,24},{1,25},{8,16},{9,17},{16,8},{17,9},{24,0},{25,1},{2,26},{3,... | collective-permute-start | bytes 393224 | tf_op jit(solution)/shard_map/ppermute | solution.py:299
  76.2 6.8 %collective-permute-start.10 = (bf16[64,1024]{1,0:T(8,128)(2,1)S(1)}, bf16[64,1024]{1,0:T(8,128)(2,1)S(1)}, u32[]{:S(2)}, u32[]{:S(2)}) collective-permute-start(bf16[64,1024]{1,0:T(8,128)(2,1)S(1)} %collective-permute-done.3.refs_1_), channel_id=1, source_target_pairs={{0,4},{2,6},{4,0},{6,2},{1,5},{3,7},{5,1},{7,3},{8,12},{10,14},{12... | collective-permute-start | bytes 393224 | tf_op jit(solution)/shard_map/ppermute | solution.py:289
  76.9 9.9 %collective-permute-start.14 = (bf16[64,1024]{1,0:T(8,128)(2,1)S(1)}, bf16[64,1024]{1,0:T(8,128)(2,1)S(1)}, u32[]{:S(2)}, u32[]{:S(2)}) collective-permute-start(bf16[64,1024]{1,0:T(8,128)(2,1)S(1)} %get-tuple-element.42.refs_0_), channel_id=1, source_target_pairs={{0,6},{2,4},{4,2},{6,0},{1,7},{3,5},{5,3},{7,1},{8,14},{10,12},{12... | collective-permute-start | bytes 393224 | tf_op jit(solution)/shard_map/ppermute | solution.py:289
  81.0 6.4 %collective-permute-start.9 = (bf16[64,1024]{1,0:T(8,128)(2,1)S(1)}, bf16[64,1024]{1,0:T(8,128)(2,1)S(1)}, u32[]{:S(2)}, u32[]{:S(2)}) collective-permute-start(bf16[64,1024]{1,0:T(8,128)(2,1)S(1)} %collective-permute-done.4.refs_2_), channel_id=1, source_target_pairs={{0,2},{2,0},{4,6},{6,4},{1,3},{3,1},{5,7},{7,5},{8,10},{10,8},{12,... | collective-permute-start | bytes 393224 | tf_op jit(solution)/shard_map/ppermute | solution.py:289
  81.8 8.5 %collective-permute-start.12 = (bf16[64,1024]{1,0:T(8,128)(2,1)S(1)}, bf16[64,1024]{1,0:T(8,128)(2,1)S(1)}, u32[]{:S(2)}, u32[]{:S(2)}) collective-permute-start(bf16[64,1024]{1,0:T(8,128)(2,1)S(1)} %collective-permute-done.4.refs_2_), channel_id=1, source_target_pairs={{0,4},{2,6},{4,0},{6,2},{1,5},{3,7},{5,1},{7,3},{8,12},{10,14},{12... | collective-permute-start | bytes 393224 | tf_op jit(solution)/shard_map/ppermute | solution.py:289
  83.0 7.7 %collective-permute-start.17 = (bf16[64,1024]{1,0:T(8,128)(2,1)S(1)}, bf16[64,1024]{1,0:T(8,128)(2,1)S(1)}, u32[]{:S(2)}, u32[]{:S(2)}) collective-permute-start(bf16[64,1024]{1,0:T(8,128)(2,1)S(1)} %collective-permute-done.6.refs_3_), channel_id=1, source_target_pairs={{0,6},{2,4},{4,2},{6,0},{1,7},{3,5},{5,3},{7,1},{8,14},{10,12},{12... | collective-permute-start | bytes 393224 | tf_op jit(solution)/shard_map/ppermute | solution.py:289
  84.5 8.1 %collective-permute-start.13 = (bf16[64,1024]{1,0:T(8,128)(2,1)S(1)}, bf16[64,1024]{1,0:T(8,128)(2,1)S(1)}, u32[]{:S(2)}, u32[]{:S(2)}) collective-permute-start(bf16[64,1024]{1,0:T(8,128)(2,1)S(1)} %collective-permute-done.6.refs_3_), channel_id=1, source_target_pairs={{0,4},{2,6},{4,0},{6,2},{1,5},{3,7},{5,1},{7,3},{8,12},{10,14},{12... | collective-permute-start | bytes 393224 | tf_op jit(solution)/shard_map/ppermute | solution.py:289
  86.8 5.7 %collective-permute-start.11 = (bf16[64,1024]{1,0:T(8,128)(2,1)S(1)}, bf16[64,1024]{1,0:T(8,128)(2,1)S(1)}, u32[]{:S(2)}, u32[]{:S(2)}) collective-permute-start(bf16[64,1024]{1,0:T(8,128)(2,1)S(1)} %collective-permute-done.6.refs_3_), channel_id=1, source_target_pairs={{0,2},{2,0},{4,6},{6,4},{1,3},{3,1},{5,7},{7,5},{8,10},{10,8},{12,... | collective-permute-start | bytes 393224 | tf_op jit(solution)/shard_map/ppermute | solution.py:289
  87.4 6.4 %collective-permute-start.15 = (bf16[64,1024]{1,0:T(8,128)(2,1)S(1)}, bf16[64,1024]{1,0:T(8,128)(2,1)S(1)}, u32[]{:S(2)}, u32[]{:S(2)}) collective-permute-start(bf16[64,1024]{1,0:T(8,128)(2,1)S(1)} %collective-permute-done.10.refs_9_), channel_id=1, source_target_pairs={{0,2},{2,0},{4,6},{6,4},{1,3},{3,1},{5,7},{7,5},{8,10},{10,8},{12,... | collective-permute-start | bytes 393224 | tf_op jit(solution)/shard_map/ppermute | solution.py:289
  90.4 5.0 %collective-permute-start.16 = (bf16[64,1024]{1,0:T(8,128)(2,1)S(1)}, bf16[64,1024]{1,0:T(8,128)(2,1)S(1)}, u32[]{:S(2)}, u32[]{:S(2)}) collective-permute-start(bf16[64,1024]{1,0:T(8,128)(2,1)S(1)} %collective-permute-done.9.refs_6_), channel_id=1, source_target_pairs={{0,4},{2,6},{4,0},{6,2},{1,5},{3,7},{5,1},{7,3},{8,12},{10,14},{12... | collective-permute-start | bytes 393224 | tf_op jit(solution)/shard_map/ppermute | solution.py:289
  103.9 8.0 %collective-permute-start.18 = (bf16[64,1024]{1,0:T(8,128)(2,1)S(1)}, bf16[64,1024]{1,0:T(8,128)(2,1)S(1)}, u32[]{:S(2)}, u32[]{:S(2)}) collective-permute-start(bf16[64,1024]{1,0:T(8,128)(2,1)S(1)} %get-tuple-element.56), channel_id=1, source_target_pairs={{0,24},{1,25},{8,16},{9,17},{16,8},{17,9},{24,0},{25,1},{2,26},{3,... | collective-permute-start | bytes 393224 | tf_op jit(solution)/shard_map/ppermute | solution.py:299
  108.1 6.3 %collective-permute-start.19 = (bf16[64,1024]{1,0:T(8,128)(2,1)S(1)}, bf16[64,1024]{1,0:T(8,128)(2,1)S(1)}, u32[]{:S(2)}, u32[]{:S(2)}) collective-permute-start(bf16[64,1024]{1,0:T(8,128)(2,1)S(1)} %get-tuple-element.57), channel_id=1, source_target_pairs={{0,8},{1,17},{8,0},{9,25},{16,24},{17,1},{24,16},{25,9},{2,10},{3,... | collective-permute-start | bytes 393224 | tf_op jit(solution)/shard_map/ppermute | solution.py:299
  108.3 7.3 %collective-permute-start.20 = (bf16[64,1024]{1,0:T(8,128)(2,1)S(1)}, bf16[64,1024]{1,0:T(8,128)(2,1)S(1)}, u32[]{:S(2)}, u32[]{:S(2)}) collective-permute-start(bf16[64,1024]{1,0:T(8,128)(2,1)S(1)} %get-tuple-element.58), channel_id=1, source_target_pairs={{0,16},{1,9},{8,24},{9,1},{16,0},{17,25},{24,8},{25,17},{2,18},{3,... | collective-permute-start | bytes 393224 | tf_op jit(solution)/shard_map/ppermute | solution.py:299

commit v4 on v1

--- a/solution.py
+++ b/solution.py
@@ -68,19 +68,21 @@
     inputs = refs[: count * pieces]
     outputs = refs[count * pieces : count * pieces + pieces]
     gram_ref, start_ref, next_ref = refs[count * pieces + pieces :]
-    for position in range(count):
-        for piece in range(pieces):
-            start_ref[position, piece * height : (piece + 1) * height, :] = inputs[
-                position * pieces + piece
-            ][...]
+    block = pieces * height
+    rows = count * block
+    chunk = 2 * block if count % 2 == 0 else block
+    for position, piece_ref in enumerate(inputs):
+        start_ref[position * height : (position + 1) * height, :] = piece_ref[...]
     current, other = start_ref, next_ref
-    for iteration in range(NS_STEPS - 1):
-        gram_of([current.at[position] for position in range(count)], gram_ref)
-        for position in range(count):
-            other[position] = polynomial(current[position], gram_ref)
-        current, other = other, current
-    gram_of([current.at[position] for position in range(count)], gram_ref)
-    result = polynomial(current[0], gram_ref)
+    for iteration in range(NS_STEPS):
+        gram_of([current.at[start : start + block] for start in range(0, rows, block)], gram_ref)
+        if iteration + 1 < NS_STEPS:
+            for start in range(0, rows, chunk):
+                other[start : start + chunk, :] = polynomial(
+                    current[start : start + chunk, :], gram_ref
+                )
+            current, other = other, current
+    result = polynomial(current[:block, :], gram_ref)
     for piece in range(pieces):
         outputs[piece][...] = result[piece * height : (piece + 1) * height, :]
 
@@ -93,8 +95,8 @@
         out_shape=[jax.ShapeDtypeStruct((height, width), jnp.bfloat16)] * pieces,
         scratch_shapes=[
             pltpu.VMEM((width, width), jnp.bfloat16),
-            pltpu.VMEM((count, pieces * height, width), jnp.bfloat16),
-            pltpu.VMEM((count, pieces * height, width), jnp.bfloat16),
+            pltpu.VMEM((count * pieces * height, width), jnp.bfloat16),
+            pltpu.VMEM((count * pieces * height, width), jnp.bfloat16),
         ],
         compiler_params=pltpu.CompilerParams(vmem_limit_bytes=32 * MIB),
     )(*[piece for block in blocks for piece in block])
@@ -126,15 +128,14 @@
     matrix_count, shard_count, height, width = by_rows.shape
     return pl.pallas_call(
         functools.partial(slices_kernel, shard_count),
-        out_shape=[jax.ShapeDtypeStruct((matrix_count, height, width), by_rows.dtype)]
-        * shard_count,
+        out_shape=[pltpu.VMEM((matrix_count, height, width), by_rows.dtype)] * shard_count,
         in_specs=[
             pl.BlockSpec(memory_space=pltpu.SMEM),
             pl.BlockSpec(memory_space=pltpu.HBM),
         ],
         out_specs=[pl.BlockSpec(memory_space=pltpu.VMEM)] * shard_count,
         scratch_shapes=[pltpu.SemaphoreType.DMA((shard_count,))],
-        compiler_params=pltpu.CompilerParams(vmem_limit_bytes=4 * MIB),
+        compiler_params=pltpu.CompilerParams(vmem_limit_bytes=60 * MIB),
     )(place, by_rows)
 
 

time: 116 us -> 116 us (level)
  local copies, waits for them, and re-layouts: 1.7 us -> 0.03 us
  Pallas kernels: 16.2 us -> 17.8 us
    unnamed x14, local copies, waits for them, and re-layouts: 1.69 us -> 0.03 us
    pallas_call x1, Pallas kernels: 0.73 us -> 2.35 us  [row_slices(): pl.pallas_call(functools.partial(slices_kernel, shard_count), out_shape=[...]
where the time goes in v4:
time: 116 us
  blocking collectives  56 us (48%)
  starting transfers between devices  22.7 us (20%)
  waiting for transfers between devices  18.3 us (16%)
  Pallas kernels  17.8 us (15%)
    all_to_all x1, blocking collectives, per_device(): lax.all_to_all(jnp.broadcast_to(vector_grads[0], (shard_count, vector_cou...  44.3 us
    ppermute x21, starting transfers between devices, swapped(): return lax.ppermute(array, axis, pairs)  22.7 us
    ppermute x21, waiting for transfers between devices, swapped(): return lax.ppermute(array, axis, pairs)  18.3 us
    all_to_all x1, blocking collectives, per_device(): lax.all_to_all(figures.reshape(others * section_count, 1, LANES), MESH_AX...  11.7 us
    pallas_call x1, Pallas kernels, orthogonalize(): pl.pallas_call(functools.partial(orthogonalize_kernel, count, pieces), ou...  8.54 us
    pallas_call x3, Pallas kernels, on_device(): pl.pallas_call(kernel, out_shape=out_shape, in_specs=[pl.BlockSpec(memory...  4.18 us
    pallas_call x2, Pallas kernels, finished(): pl.pallas_call(functools.partial(end_kernel, offsets), out_shape=[jax.Sha...  2.74 us
    pallas_call x1, Pallas kernels, row_slices(): pl.pallas_call(functools.partial(slices_kernel, shard_count), out_shape=[...  2.35 us
  transfers between devices with their start and end apart: 21, of which 10 were waited for; matrix products, arithmetic and copies ran while one was open for 0% of the time, Pallas kernels for 3%

profile of v4, /device:TPU:0, one launch (start us, length us, event | category | flops | bytes accessed | tf_op | source)
XLA Modules:
  0.0 116.2 jit_solution(10753491073226183061)
XLA Ops:
  0.6 0.0 copy-start.6
  0.6 0.0 copy-start
  0.7 0.5 compare_select_fusion.place_ref
  1.2 2.3 %shard_map.110 = (bf16[4,64,1024]{2,1,0:T(8,128)(2,1)S(1)}, bf16[4,64,1024]{2,1,0:T(8,128)(2,1)S(1)}, bf16[4,64,1024]{2,1,0:T(8,128)(2,1)S(1)}, bf16[4,64,1024]{2,1,0:T(8,128)(2,1)S(1)}) custom-call(s32[5]{0:T(128)} %compare_select_fusion.place_ref, bf16[4,4,64,1024]{3,2,1,0:T(8,128)(2,1)} %bitcast.22), custom_call_target="tpu_custom_call" | custom-call | tf_op jit(solution)/shard_map/pallas_call | solution.py:129
  3.5 5.1 %collective-permute-start = (bf16[4,64,1024]{2,1,0:T(8,128)(2,1)S(1)}, bf16[4,64,1024]{2,1,0:T(8,128)(2,1)S(1)}, u32[]{:S(2)}, u32[]{:S(2)}) collective-permute-start(bf16[4,64,1024]{2,1,0:T(8,128)(2,1)S(1)} %get-tuple-element.30), channel_id=1, source_target_pairs={{0,24},{8,16},{16,8},{24,0},{1,25},{9,17},{17,9},{25,1},{2,26},{10... | collective-permute-start | bytes 1572872 | tf_op jit(solution)/shard_map/ppermute | solution.py:289
  8.6 0.0 collective-permute-start.1
  8.6 0.6 collective-permute-start.2
  9.3 0.0 copy-done.6
  9.3 44.3 %all_to_all.10.refs_4_ = bf16[4,4,256]{2,1,0:T(4,128)(2,1)S(1)} all-to-all(bf16[4,4,256]{2,1,0:T(4,128)(2,1)S(1)} %broadcast_in_dim.28), channel_id=1, replica_groups=mesh['shard'=4,'tensor'=4,'section'=2] {'shard'}, dimensions={0} | all-to-all | bytes 16384 | tf_op jit(solution)/shard_map/all_to_all | solution.py:318
  53.6 0.0 collective-permute-done.refs_0_
  53.6 0.0 collective-permute-done.1.refs_1_
  53.6 0.0 collective-permute-done.2.refs_2_
  53.6 0.0 copy-done
  53.6 0.0 copy-done.2
  53.6 1.3 %shard_map.111 = (f32[4,64,1024]{2,1,0:T(8,128)S(1)}, f32[4,256]{1,0:T(4,128)S(1)}, f32[16,2,1,128]{3,2,1,0:T(1,128)S(1)}) custom-call(s32[5]{0:T(128)S(1)} %copy-done.2, bf16[4,64,1024]{2,1,0:T(8,128)(2,1)S(1)} %collective-permute-done.refs_0_, bf16[4,64,1024]{2,1,0:T(8,128)(2,1)S(1)} %collective-permute-done.1.refs_1_, ...), custom_call_target="tpu_custom_call" | custom-call | tf_op jit(solution)/shard_map/pallas_call | solution.py:278
  55.0 11.7 %all_to_all.11.figures_ref = f32[32,1,128]{2,1,0:T(1,128)S(1)} all-to-all(f32[32,1,128]{2,1,0:T(1,128)S(1)} %bitcast.18), channel_id=1, replica_groups=mesh['shard'=4,'tensor'=4,'section'=2] {'shard','tensor','section'}, dimensions={0} | all-to-all | bytes 32768 | tf_op jit(solution)/shard_map/all_to_all | solution.py:337
  66.6 0.0 copy-start.1
  66.6 0.0 copy-start.3
  66.6 0.0 copy-start.4
  66.7 1.0 shard_map.112
  67.7 0.6 collective-permute-start.3
  68.3 0.6 collective-permute-start.4
  68.9 0.5 collective-permute-start.10
  69.4 0.6 collective-permute-start.6
  70.0 4.6 %collective-permute-done.3.refs_1_ = bf16[64,1024]{1,0:T(8,128)(2,1)S(1)} collective-permute-done((bf16[64,1024]{1,0:T(8,128)(2,1)S(1)}, bf16[64,1024]{1,0:T(8,128)(2,1)S(1)}, u32[]{:S(2)}, u32[]{:S(2)}) %collective-permute-start.3) | collective-permute-done | bytes 131104 | tf_op jit(solution)/shard_map/ppermute | solution.py:289
  74.6 0.5 collective-permute-start.11
  75.2 1.8 %collective-permute-done.4.refs_2_ = bf16[64,1024]{1,0:T(8,128)(2,1)S(1)} collective-permute-done((bf16[64,1024]{1,0:T(8,128)(2,1)S(1)}, bf16[64,1024]{1,0:T(8,128)(2,1)S(1)}, u32[]{:S(2)}, u32[]{:S(2)}) %collective-permute-start.4) | collective-permute-done | bytes 131104 | tf_op jit(solution)/shard_map/ppermute | solution.py:289
  76.9 1.5 %collective-permute-start.5 = (bf16[64,1024]{1,0:T(8,128)(2,1)S(1)}, bf16[64,1024]{1,0:T(8,128)(2,1)S(1)}, u32[]{:S(2)}, u32[]{:S(2)}) collective-permute-start(bf16[64,1024]{1,0:T(8,128)(2,1)S(1)} %get-tuple-element.41), channel_id=1, source_target_pairs={{0,24},{8,16},{16,8},{24,0},{1,25},{9,17},{17,9},{25,1},{2,26},{10... | collective-permute-start | bytes 393224 | tf_op jit(solution)/shard_map/ppermute | solution.py:289
  78.4 0.7 collective-permute-start.7
  79.1 0.0 collective-permute-done.10.refs_8_
  79.1 0.5 collective-permute-start.12
  79.6 0.0 collective-permute-done.6.refs_4_
  79.6 1.5 %collective-permute-start.8 = (bf16[64,1024]{1,0:T(8,128)(2,1)S(1)}, bf16[64,1024]{1,0:T(8,128)(2,1)S(1)}, u32[]{:S(2)}, u32[]{:S(2)}) collective-permute-start(bf16[64,1024]{1,0:T(8,128)(2,1)S(1)} %collective-permute-done.4.refs_2_), channel_id=1, source_target_pairs={{0,2},{2,0},{4,6},{6,4},{1,3},{3,1},{5,7},{7,5},{8,10},{10,8},{12,... | collective-permute-start | bytes 393224 | tf_op jit(solution)/shard_map/ppermute | solution.py:289
  81.1 0.0 collective-permute-done.11.refs_9_
  81.1 1.4 %collective-permute-start.14 = (bf16[64,1024]{1,0:T(8,128)(2,1)S(1)}, bf16[64,1024]{1,0:T(8,128)(2,1)S(1)}, u32[]{:S(2)}, u32[]{:S(2)}) collective-permute-start(bf16[64,1024]{1,0:T(8,128)(2,1)S(1)} %collective-permute-done.6.refs_4_), channel_id=1, source_target_pairs={{0,4},{2,6},{4,0},{6,2},{1,5},{3,7},{5,1},{7,3},{8,12},{10,14},{12... | collective-permute-start | bytes 393224 | tf_op jit(solution)/shard_map/ppermute | solution.py:289
  82.5 1.2 %collective-permute-done.5.refs_3_ = bf16[64,1024]{1,0:T(8,128)(2,1)S(1)} collective-permute-done((bf16[64,1024]{1,0:T(8,128)(2,1)S(1)}, bf16[64,1024]{1,0:T(8,128)(2,1)S(1)}, u32[]{:S(2)}, u32[]{:S(2)}) %collective-permute-start.5) | collective-permute-done | bytes 131104 | tf_op jit(solution)/shard_map/ppermute | solution.py:289
  83.7 0.6 collective-permute-start.17
  84.3 0.0 collective-permute-done.7.refs_5_
  84.3 1.5 %collective-permute-start.13 = (bf16[64,1024]{1,0:T(8,128)(2,1)S(1)}, bf16[64,1024]{1,0:T(8,128)(2,1)S(1)}, u32[]{:S(2)}, u32[]{:S(2)}) collective-permute-start(bf16[64,1024]{1,0:T(8,128)(2,1)S(1)} %collective-permute-done.5.refs_3_), channel_id=1, source_target_pairs={{0,4},{2,6},{4,0},{6,2},{1,5},{3,7},{5,1},{7,3},{8,12},{10,14},{12... | collective-permute-start | bytes 393224 | tf_op jit(solution)/shard_map/ppermute | solution.py:289
  85.8 0.7 collective-permute-done.12.refs_10_
  86.5 1.3 %collective-permute-start.15 = (bf16[64,1024]{1,0:T(8,128)(2,1)S(1)}, bf16[64,1024]{1,0:T(8,128)(2,1)S(1)}, u32[]{:S(2)}, u32[]{:S(2)}) collective-permute-start(bf16[64,1024]{1,0:T(8,128)(2,1)S(1)} %collective-permute-done.11.refs_9_), channel_id=1, source_target_pairs={{0,2},{2,0},{4,6},{6,4},{1,3},{3,1},{5,7},{7,5},{8,10},{10,8},{12,... | collective-permute-start | bytes 393224 | tf_op jit(solution)/shard_map/ppermute | solution.py:289
  87.8 0.0 collective-permute-done.8.refs_6_
  87.8 0.8 collective-permute-start.9
  88.6 2.2 %collective-permute-done.14.refs_12_ = bf16[64,1024]{1,0:T(8,128)(2,1)S(1)} collective-permute-done((bf16[64,1024]{1,0:T(8,128)(2,1)S(1)}, bf16[64,1024]{1,0:T(8,128)(2,1)S(1)}, u32[]{:S(2)}, u32[]{:S(2)}) %collective-permute-start.14) | collective-permute-done | bytes 131104 | tf_op jit(solution)/shard_map/ppermute | solution.py:289
  90.7 0.0 collective-permute-start.16
  90.7 1.1 collective-permute-done.15.refs_13_
  91.8 0.0 collective-permute-done.17.refs_15_
  91.8 0.7 collective-permute-done.13.refs_11_
  92.5 0.7 collective-permute-done.9.refs_7_
  93.2 2.5 %collective-permute-done.16.refs_14_ = bf16[64,1024]{1,0:T(8,128)(2,1)S(1)} collective-permute-done((bf16[64,1024]{1,0:T(8,128)(2,1)S(1)}, bf16[64,1024]{1,0:T(8,128)(2,1)S(1)}, u32[]{:S(2)}, u32[]{:S(2)}) %collective-permute-start.16) | collective-permute-done | bytes 131104 | tf_op jit(solution)/shard_map/ppermute | solution.py:289
  95.7 8.5 %shard_map.113 = (bf16[64,1024]{1,0:T(8,128)(2,1)S(1)}, bf16[64,1024]{1,0:T(8,128)(2,1)S(1)}, bf16[64,1024]{1,0:T(8,128)(2,1)S(1)}, bf16[64,1024]{1,0:T(8,128)(2,1)S(1)}) custom-call(bf16[64,1024]{1,0:T(8,128)(2,1)S(1)} %get-tuple-element.37.refs_0_, bf16[64,1024]{1,0:T(8,128)(2,1)S(1)} %collective-permute-done.3.refs_1_, ...), custom_call_target="tpu_custom_call" | custom-call | tf_op jit(solution)/shard_map/pallas_call | solution.py:93
  104.3 1.8 %collective-permute-start.18 = (bf16[64,1024]{1,0:T(8,128)(2,1)S(1)}, bf16[64,1024]{1,0:T(8,128)(2,1)S(1)}, u32[]{:S(2)}, u32[]{:S(2)}) collective-permute-start(bf16[64,1024]{1,0:T(8,128)(2,1)S(1)} %get-tuple-element.46), channel_id=1, source_target_pairs={{0,24},{8,16},{16,8},{24,0},{1,25},{9,17},{17,9},{25,1},{2,26},{10... | collective-permute-start | bytes 393224 | tf_op jit(solution)/shard_map/ppermute | solution.py:289
  106.1 0.0 collective-permute-start.19
  106.1 2.6 %collective-permute-start.20 = (bf16[64,1024]{1,0:T(8,128)(2,1)S(1)}, bf16[64,1024]{1,0:T(8,128)(2,1)S(1)}, u32[]{:S(2)}, u32[]{:S(2)}) collective-permute-start(bf16[64,1024]{1,0:T(8,128)(2,1)S(1)} %get-tuple-element.48), channel_id=1, source_target_pairs={{0,8},{8,0},{16,24},{24,16},{1,9},{9,1},{17,25},{25,17},{2,10},{10... | collective-permute-start | bytes 393224 | tf_op jit(solution)/shard_map/ppermute | solution.py:289
  108.7 0.0 copy-done.1
  108.7 1.3 %shard_map.115 = (bf16[4,64,1024]{2,1,0:T(8,128)(2,1)}, bf16[4,64,1024]{2,1,0:T(8,128)(2,1)}) custom-call(s32[5]{0:T(128)S(1)} %copy-done.2, bf16[64,1024]{1,0:T(8,128)(2,1)S(1)} %get-tuple-element.42.refs_0_, bf16[4,64,1024]{2,1,0:T(8,128)(2,1)S(1)} %bitcast.16), custom_call_target="tpu_custom_call" | custom-call | tf_op jit(solution)/shard_map/pallas_call | solution.py:232
  110.0 0.0 copy-done.3
  110.0 0.0 copy-done.4
  110.0 0.0 copy-done.5
  110.0 1.8 %shard_map.114 = (f32[4,64,1024]{2,1,0:T(8,128)}, f32[4,64]{1,0:T(4,128)}, f32[4,64]{1,0:T(4,128)}) custom-call(s32[5]{0:T(128)S(1)} %copy-done.2, f32[8,128]{1,0:T(8,128)S(1)} %get-tuple-element.43.clip_ref, f32[4,64,1024]{2,1,0:T(8,128)S(1)} %get-tuple-element.35.grad_ref, f32[4,64,1024]{2,1,0:T(8,128)S(1)} %bitcast.15, ...), custom_call_target="tpu_custom_call" | custom-call | tf_op jit(solution)/shard_map/pallas_call | solution.py:278
  111.9 0.0 collective-permute-done.18.refs_0_
  111.9 2.8 %collective-permute-done.19.refs_1_ = bf16[64,1024]{1,0:T(8,128)(2,1)S(1)} collective-permute-done((bf16[64,1024]{1,0:T(8,128)(2,1)S(1)}, bf16[64,1024]{1,0:T(8,128)(2,1)S(1)}, u32[]{:S(2)}, u32[]{:S(2)}) %collective-permute-start.19) | collective-permute-done | bytes 131104 | tf_op jit(solution)/shard_map/ppermute | solution.py:289
  114.7 0.0 collective-permute-done.20.refs_2_
  114.7 1.5 %shard_map.116 = (bf16[4,64,1024]{2,1,0:T(8,128)(2,1)}, bf16[4,64,1024]{2,1,0:T(8,128)(2,1)}) custom-call(s32[5]{0:T(128)S(1)} %copy-done.2, bf16[64,1024]{1,0:T(8,128)(2,1)S(1)} %collective-permute-done.18.refs_0_, bf16[64,1024]{1,0:T(8,128)(2,1)S(1)} %collective-permute-done.19.refs_1_, ...), custom_call_target="tpu_custom_call", output_to_operand_aliasing={{0}: (5, {}), {1}: (6, {})} | custom-call | tf_op jit(solution)/shard_map/pallas_call | solution.py:232
  (3 shorter events, 0.0 us)
Async XLA Ops:
  0.6 8.7 %copy-start.6 = (bf16[1,1,4,256]{3,2,1,0:T(4,128)(2,1)S(1)}, bf16[1,1,4,256]{3,2,1,0:T(4,128)(2,1)}, u32[]{:S(2)}) copy-start(bf16[1,1,4,256]{3,2,1,0:T(4,128)(2,1)} %param.8) | copy-start | bytes 6148
  0.6 53.0 %copy-start = (f32[1,4,64,1024]{3,2,1,0:T(8,128)S(1)}, f32[1,4,64,1024]{3,2,1,0:T(8,128)}, u32[]{:S(2)}) copy-start(f32[1,4,64,1024]{3,2,1,0:T(8,128)} %param.9) | copy-start | bytes 3145732
  1.2 52.5 %copy-start.2 = (s32[5]{0:T(128)S(1)}, s32[5]{0:T(128)}, u32[]{:S(2)}) copy-start(s32[5]{0:T(128)} %compare_select_fusion.place_ref) | copy-start | bytes 64
  3.5 50.1 %collective-permute-start = (bf16[4,64,1024]{2,1,0:T(8,128)(2,1)S(1)}, bf16[4,64,1024]{2,1,0:T(8,128)(2,1)S(1)}, u32[]{:S(2)}, u32[]{:S(2)}) collective-permute-start(bf16[4,64,1024]{2,1,0:T(8,128)(2,1)S(1)} %get-tuple-element.30), channel_id=1, source_target_pairs={{0,24},{8,16},{16,8},{24,0},{1,25},{9,17},{17,9},{25,1},{2,26},{10... | collective-permute-start | bytes 1572872 | tf_op jit(solution)/shard_map/ppermute | solution.py:289
  8.6 45.0 %collective-permute-start.1 = (bf16[4,64,1024]{2,1,0:T(8,128)(2,1)S(1)}, bf16[4,64,1024]{2,1,0:T(8,128)(2,1)S(1)}, u32[]{:S(2)}, u32[]{:S(2)}) collective-permute-start(bf16[4,64,1024]{2,1,0:T(8,128)(2,1)S(1)} %get-tuple-element.31), channel_id=1, source_target_pairs={{0,16},{8,24},{16,0},{24,8},{1,17},{9,25},{17,1},{25,9},{2,18},{10... | collective-permute-start | bytes 1572872 | tf_op jit(solution)/shard_map/ppermute | solution.py:289
  8.6 45.0 %collective-permute-start.2 = (bf16[4,64,1024]{2,1,0:T(8,128)(2,1)S(1)}, bf16[4,64,1024]{2,1,0:T(8,128)(2,1)S(1)}, u32[]{:S(2)}, u32[]{:S(2)}) collective-permute-start(bf16[4,64,1024]{2,1,0:T(8,128)(2,1)S(1)} %get-tuple-element.32), channel_id=1, source_target_pairs={{0,8},{8,0},{16,24},{24,16},{1,9},{9,1},{17,25},{25,17},{2,10},{10... | collective-permute-start | bytes 1572872 | tf_op jit(solution)/shard_map/ppermute | solution.py:289
  66.6 42.1 %copy-start.1 = (bf16[1,4,64,1024]{3,2,1,0:T(8,128)(2,1)S(1)}, bf16[1,4,64,1024]{3,2,1,0:T(8,128)(2,1)}, u32[]{:S(2)}) copy-start(bf16[1,4,64,1024]{3,2,1,0:T(8,128)(2,1)} %param.10) | copy-start | bytes 1572868
  66.6 43.3 %copy-start.3 = (f32[1,4,64]{2,1,0:T(4,128)S(1)}, f32[1,4,64]{2,1,0:T(4,128)}, u32[]{:S(2)}) copy-start(f32[1,4,64]{2,1,0:T(4,128)} %param.11) | copy-start | bytes 3076
  66.6 43.4 %copy-start.4 = (f32[1,4,64]{2,1,0:T(4,128)S(1)}, f32[1,4,64]{2,1,0:T(4,128)}, u32[]{:S(2)}) copy-start(f32[1,4,64]{2,1,0:T(4,128)} %param.12) | copy-start | bytes 3076
  66.6 43.4 %copy-start.5 = (f32[1,4,64]{2,1,0:T(4,128)S(1)}, f32[1,4,64]{2,1,0:T(4,128)}, u32[]{:S(2)}) copy-start(f32[1,4,64]{2,1,0:T(4,128)} %param.13) | copy-start | bytes 3076
  67.7 6.9 %collective-permute-start.3 = (bf16[64,1024]{1,0:T(8,128)(2,1)S(1)}, bf16[64,1024]{1,0:T(8,128)(2,1)S(1)}, u32[]{:S(2)}, u32[]{:S(2)}) collective-permute-start(bf16[64,1024]{1,0:T(8,128)(2,1)S(1)} %get-tuple-element.38), channel_id=1, source_target_pairs={{0,8},{8,0},{16,24},{24,16},{1,9},{9,1},{17,25},{25,17},{2,10},{10... | collective-permute-start | bytes 393224 | tf_op jit(solution)/shard_map/ppermute | solution.py:289
  68.3 8.6 %collective-permute-start.4 = (bf16[64,1024]{1,0:T(8,128)(2,1)S(1)}, bf16[64,1024]{1,0:T(8,128)(2,1)S(1)}, u32[]{:S(2)}, u32[]{:S(2)}) collective-permute-start(bf16[64,1024]{1,0:T(8,128)(2,1)S(1)} %get-tuple-element.39), channel_id=1, source_target_pairs={{0,16},{8,24},{16,0},{24,8},{1,17},{9,25},{17,1},{25,9},{2,18},{10... | collective-permute-start | bytes 393224 | tf_op jit(solution)/shard_map/ppermute | solution.py:289
  68.9 10.2 %collective-permute-start.10 = (bf16[64,1024]{1,0:T(8,128)(2,1)S(1)}, bf16[64,1024]{1,0:T(8,128)(2,1)S(1)}, u32[]{:S(2)}, u32[]{:S(2)}) collective-permute-start(bf16[64,1024]{1,0:T(8,128)(2,1)S(1)} %get-tuple-element.37.refs_0_), channel_id=1, source_target_pairs={{0,4},{2,6},{4,0},{6,2},{1,5},{3,7},{5,1},{7,3},{8,12},{10,14},{12... | collective-permute-start | bytes 393224 | tf_op jit(solution)/shard_map/ppermute | solution.py:289
  69.4 10.2 %collective-permute-start.6 = (bf16[64,1024]{1,0:T(8,128)(2,1)S(1)}, bf16[64,1024]{1,0:T(8,128)(2,1)S(1)}, u32[]{:S(2)}, u32[]{:S(2)}) collective-permute-start(bf16[64,1024]{1,0:T(8,128)(2,1)S(1)} %get-tuple-element.37.refs_0_), channel_id=1, source_target_pairs={{0,2},{2,0},{4,6},{6,4},{1,3},{3,1},{5,7},{7,5},{8,10},{10,8},{12,... | collective-permute-start | bytes 393224 | tf_op jit(solution)/shard_map/ppermute | solution.py:289
  74.6 6.5 %collective-permute-start.11 = (bf16[64,1024]{1,0:T(8,128)(2,1)S(1)}, bf16[64,1024]{1,0:T(8,128)(2,1)S(1)}, u32[]{:S(2)}, u32[]{:S(2)}) collective-permute-start(bf16[64,1024]{1,0:T(8,128)(2,1)S(1)} %collective-permute-done.3.refs_1_), channel_id=1, source_target_pairs={{0,4},{2,6},{4,0},{6,2},{1,5},{3,7},{5,1},{7,3},{8,12},{10,14},{12... | collective-permute-start | bytes 393224 | tf_op jit(solution)/shard_map/ppermute | solution.py:289
  76.9 6.8 %collective-permute-start.5 = (bf16[64,1024]{1,0:T(8,128)(2,1)S(1)}, bf16[64,1024]{1,0:T(8,128)(2,1)S(1)}, u32[]{:S(2)}, u32[]{:S(2)}) collective-permute-start(bf16[64,1024]{1,0:T(8,128)(2,1)S(1)} %get-tuple-element.41), channel_id=1, source_target_pairs={{0,24},{8,16},{16,8},{24,0},{1,25},{9,17},{17,9},{25,1},{2,26},{10... | collective-permute-start | bytes 393224 | tf_op jit(solution)/shard_map/ppermute | solution.py:289
  78.4 5.9 %collective-permute-start.7 = (bf16[64,1024]{1,0:T(8,128)(2,1)S(1)}, bf16[64,1024]{1,0:T(8,128)(2,1)S(1)}, u32[]{:S(2)}, u32[]{:S(2)}) collective-permute-start(bf16[64,1024]{1,0:T(8,128)(2,1)S(1)} %collective-permute-done.3.refs_1_), channel_id=1, source_target_pairs={{0,2},{2,0},{4,6},{6,4},{1,3},{3,1},{5,7},{7,5},{8,10},{10,8},{12,... | collective-permute-start | bytes 393224 | tf_op jit(solution)/shard_map/ppermute | solution.py:289
  79.1 7.4 %collective-permute-start.12 = (bf16[64,1024]{1,0:T(8,128)(2,1)S(1)}, bf16[64,1024]{1,0:T(8,128)(2,1)S(1)}, u32[]{:S(2)}, u32[]{:S(2)}) collective-permute-start(bf16[64,1024]{1,0:T(8,128)(2,1)S(1)} %collective-permute-done.4.refs_2_), channel_id=1, source_target_pairs={{0,4},{2,6},{4,0},{6,2},{1,5},{3,7},{5,1},{7,3},{8,12},{10,14},{12... | collective-permute-start | bytes 393224 | tf_op jit(solution)/shard_map/ppermute | solution.py:289
  79.6 8.2 %collective-permute-start.8 = (bf16[64,1024]{1,0:T(8,128)(2,1)S(1)}, bf16[64,1024]{1,0:T(8,128)(2,1)S(1)}, u32[]{:S(2)}, u32[]{:S(2)}) collective-permute-start(bf16[64,1024]{1,0:T(8,128)(2,1)S(1)} %collective-permute-done.4.refs_2_), channel_id=1, source_target_pairs={{0,2},{2,0},{4,6},{6,4},{1,3},{3,1},{5,7},{7,5},{8,10},{10,8},{12,... | collective-permute-start | bytes 393224 | tf_op jit(solution)/shard_map/ppermute | solution.py:289
  81.1 9.6 %collective-permute-start.14 = (bf16[64,1024]{1,0:T(8,128)(2,1)S(1)}, bf16[64,1024]{1,0:T(8,128)(2,1)S(1)}, u32[]{:S(2)}, u32[]{:S(2)}) collective-permute-start(bf16[64,1024]{1,0:T(8,128)(2,1)S(1)} %collective-permute-done.6.refs_4_), channel_id=1, source_target_pairs={{0,4},{2,6},{4,0},{6,2},{1,5},{3,7},{5,1},{7,3},{8,12},{10,14},{12... | collective-permute-start | bytes 393224 | tf_op jit(solution)/shard_map/ppermute | solution.py:289
  83.7 8.1 %collective-permute-start.17 = (bf16[64,1024]{1,0:T(8,128)(2,1)S(1)}, bf16[64,1024]{1,0:T(8,128)(2,1)S(1)}, u32[]{:S(2)}, u32[]{:S(2)}) collective-permute-start(bf16[64,1024]{1,0:T(8,128)(2,1)S(1)} %collective-permute-done.5.refs_3_), channel_id=1, source_target_pairs={{0,6},{2,4},{4,2},{6,0},{1,7},{3,5},{5,3},{7,1},{8,14},{10,12},{12... | collective-permute-start | bytes 393224 | tf_op jit(solution)/shard_map/ppermute | solution.py:289
  84.3 8.2 %collective-permute-start.13 = (bf16[64,1024]{1,0:T(8,128)(2,1)S(1)}, bf16[64,1024]{1,0:T(8,128)(2,1)S(1)}, u32[]{:S(2)}, u32[]{:S(2)}) collective-permute-start(bf16[64,1024]{1,0:T(8,128)(2,1)S(1)} %collective-permute-done.5.refs_3_), channel_id=1, source_target_pairs={{0,4},{2,6},{4,0},{6,2},{1,5},{3,7},{5,1},{7,3},{8,12},{10,14},{12... | collective-permute-start | bytes 393224 | tf_op jit(solution)/shard_map/ppermute | solution.py:289
  86.5 5.3 %collective-permute-start.15 = (bf16[64,1024]{1,0:T(8,128)(2,1)S(1)}, bf16[64,1024]{1,0:T(8,128)(2,1)S(1)}, u32[]{:S(2)}, u32[]{:S(2)}) collective-permute-start(bf16[64,1024]{1,0:T(8,128)(2,1)S(1)} %collective-permute-done.11.refs_9_), channel_id=1, source_target_pairs={{0,2},{2,0},{4,6},{6,4},{1,3},{3,1},{5,7},{7,5},{8,10},{10,8},{12,... | collective-permute-start | bytes 393224 | tf_op jit(solution)/shard_map/ppermute | solution.py:289
  87.8 5.4 %collective-permute-start.9 = (bf16[64,1024]{1,0:T(8,128)(2,1)S(1)}, bf16[64,1024]{1,0:T(8,128)(2,1)S(1)}, u32[]{:S(2)}, u32[]{:S(2)}) collective-permute-start(bf16[64,1024]{1,0:T(8,128)(2,1)S(1)} %collective-permute-done.5.refs_3_), channel_id=1, source_target_pairs={{0,2},{2,0},{4,6},{6,4},{1,3},{3,1},{5,7},{7,5},{8,10},{10,8},{12,... | collective-permute-start | bytes 393224 | tf_op jit(solution)/shard_map/ppermute | solution.py:289
  90.7 5.0 %collective-permute-start.16 = (bf16[64,1024]{1,0:T(8,128)(2,1)S(1)}, bf16[64,1024]{1,0:T(8,128)(2,1)S(1)}, u32[]{:S(2)}, u32[]{:S(2)}) collective-permute-start(bf16[64,1024]{1,0:T(8,128)(2,1)S(1)} %collective-permute-done.8.refs_6_), channel_id=1, source_target_pairs={{0,4},{2,6},{4,0},{6,2},{1,5},{3,7},{5,1},{7,3},{8,12},{10,14},{12... | collective-permute-start | bytes 393224 | tf_op jit(solution)/shard_map/ppermute | solution.py:289
  104.3 7.6 %collective-permute-start.18 = (bf16[64,1024]{1,0:T(8,128)(2,1)S(1)}, bf16[64,1024]{1,0:T(8,128)(2,1)S(1)}, u32[]{:S(2)}, u32[]{:S(2)}) collective-permute-start(bf16[64,1024]{1,0:T(8,128)(2,1)S(1)} %get-tuple-element.46), channel_id=1, source_target_pairs={{0,24},{8,16},{16,8},{24,0},{1,25},{9,17},{17,9},{25,1},{2,26},{10... | collective-permute-start | bytes 393224 | tf_op jit(solution)/shard_map/ppermute | solution.py:289
  106.1 8.6 %collective-permute-start.19 = (bf16[64,1024]{1,0:T(8,128)(2,1)S(1)}, bf16[64,1024]{1,0:T(8,128)(2,1)S(1)}, u32[]{:S(2)}, u32[]{:S(2)}) collective-permute-start(bf16[64,1024]{1,0:T(8,128)(2,1)S(1)} %get-tuple-element.47), channel_id=1, source_target_pairs={{0,16},{8,24},{16,0},{24,8},{1,17},{9,25},{17,1},{25,9},{2,18},{10... | collective-permute-start | bytes 393224 | tf_op jit(solution)/shard_map/ppermute | solution.py:289
  106.1 8.6 %collective-permute-start.20 = (bf16[64,1024]{1,0:T(8,128)(2,1)S(1)}, bf16[64,1024]{1,0:T(8,128)(2,1)S(1)}, u32[]{:S(2)}, u32[]{:S(2)}) collective-permute-start(bf16[64,1024]{1,0:T(8,128)(2,1)S(1)} %get-tuple-element.48), channel_id=1, source_target_pairs={{0,8},{8,0},{16,24},{24,16},{1,9},{9,1},{17,25},{25,17},{2,10},{10... | collective-permute-start | bytes 393224 | tf_op jit(solution)/shard_map/ppermute | solution.py:289

commit v5 on v4

--- a/solution.py
+++ b/solution.py
@@ -110,33 +110,32 @@
     return total
 
 
-def slices_kernel(count, place_ref, grad_ref, *refs):
-    outputs, semaphores = refs[:count], refs[count]
+def slices_kernel(offsets, place_ref, grad_ref, *refs):
+    outputs, semaphores = refs[: len(offsets)], refs[len(offsets)]
     copies = [
-        pltpu.make_async_copy(
-            grad_ref.at[:, place_ref[offset]], outputs[offset], semaphores.at[offset]
-        )
-        for offset in range(count)
+        pltpu.make_async_copy(grad_ref.at[:, place_ref[offset]], output, semaphores.at[slot])
+        for slot, (offset, output) in enumerate(zip(offsets, outputs))
     ]
-    for copy in reversed(copies):
+    for copy in copies:
         copy.start()
-    for copy in reversed(copies):
+    for copy in copies:
         copy.wait()
 
 
-def row_slices(place, by_rows):
+def row_slices(offsets, place, by_rows):
     matrix_count, shard_count, height, width = by_rows.shape
-    return pl.pallas_call(
-        functools.partial(slices_kernel, shard_count),
-        out_shape=[pltpu.VMEM((matrix_count, height, width), by_rows.dtype)] * shard_count,
+    slices = pl.pallas_call(
+        functools.partial(slices_kernel, offsets),
+        out_shape=[pltpu.VMEM((matrix_count, height, width), by_rows.dtype)] * len(offsets),
         in_specs=[
             pl.BlockSpec(memory_space=pltpu.SMEM),
             pl.BlockSpec(memory_space=pltpu.HBM),
         ],
-        out_specs=[pl.BlockSpec(memory_space=pltpu.VMEM)] * shard_count,
-        scratch_shapes=[pltpu.SemaphoreType.DMA((shard_count,))],
+        out_specs=[pl.BlockSpec(memory_space=pltpu.VMEM)] * len(offsets),
+        scratch_shapes=[pltpu.SemaphoreType.DMA((len(offsets),))],
         compiler_params=pltpu.CompilerParams(vmem_limit_bytes=60 * MIB),
     )(place, by_rows)
+    return dict(zip(offsets, slices))
 
 
 def sum_kernel(shard_count, place_ref, *refs):
@@ -171,6 +170,11 @@
         )
 
 
+def spread_kernel(place_ref, figures_ref, out_ref):
+    line = jnp.sum(figures_ref[...], axis=0)
+    out_ref[...] = jnp.broadcast_to(line[None], out_ref.shape)
+
+
 def scale_kernel(matrix_count, place_ref, figures_ref, grad_ref, momentum_ref, *refs):
     outputs = refs[:matrix_count]
     clip_ref = refs[matrix_count]
@@ -312,7 +316,8 @@
     )
 
     by_rows = grad_parts.reshape(matrix_count, shard_count, local_height, width)
-    parts = list(row_slices(place, by_rows))
+    parts = row_slices((3, 2), place, by_rows)
+    parts.update(row_slices((1, 0), after(place, parts[3]), by_rows))
     for offset in reversed(range(1, shard_count)):
         parts[offset] = swapped(parts[offset], "shard", offset)
     vector_parts = lax.all_to_all(
@@ -323,24 +328,30 @@
         tiled=True,
     )
 
-    others = shard_count * tensor_count
     grad_rows, vector_whole, figures = on_device(
         functools.partial(sum_kernel, shard_count),
         place,
-        parts[::-1] + [vector_parts, own_momentum],
+        [parts[offset] for offset in (3, 2, 1, 0)] + [vector_parts, own_momentum],
         [
             jax.ShapeDtypeStruct(own_momentum.shape, jnp.float32),
             jax.ShapeDtypeStruct(vector_parts.shape[1:], jnp.float32),
-            jax.ShapeDtypeStruct((others, section_count, 1, LANES), jnp.float32),
+            jax.ShapeDtypeStruct((tensor_count, section_count, 1, LANES), jnp.float32),
         ],
     )
     figures = lax.all_to_all(
-        figures.reshape(others * section_count, 1, LANES),
-        MESH_AXES,
+        figures.reshape(tensor_count * section_count, 1, LANES),
+        ("tensor", "section"),
         split_axis=0,
         concat_axis=0,
         tiled=True,
     )
+    figures = on_device(
+        spread_kernel,
+        place,
+        [figures],
+        jax.ShapeDtypeStruct((shard_count, 1, LANES), jnp.float32),
+    )
+    figures = lax.all_to_all(figures, "shard", split_axis=0, concat_axis=0, tiled=True)
     *scaled, clip_tile = on_device(
         functools.partial(scale_kernel, matrix_count),
         place,

time: 116 us -> 121 us (1.043)
  blocking collectives: 56 us -> 60.8 us
  waiting for transfers between devices: 18.3 us -> 15 us
  Pallas kernels: 17.8 us -> 20.7 us
    all_to_all x1 -> x2, blocking collectives: 11.7 us -> 18.3 us  [the longest x1 10.1 us: per_device(): lax.all_to_all(figures, 'shard', split_axis=0, concat_axis=0, tiled=True)]
    ppermute x21, waiting for transfers between devices: 18.3 us -> 15 us  [swapped(): return lax.ppermute(array, axis, pairs)]
    pallas_call x1 -> x2, Pallas kernels: 2.35 us -> 4.69 us  [row_slices(): pl.pallas_call(functools.partial(slices_kernel, offsets), out_shape=[pltp...]
    all_to_all x1, blocking collectives: 44.3 us -> 42.5 us  [per_device(): lax.all_to_all(jnp.broadcast_to(vector_grads[0], (shard_count, vector_cou...]
    pallas_call x3 -> x4, Pallas kernels: 4.18 us -> 4.71 us  [on_device(): pl.pallas_call(kernel, out_shape=out_shape, in_specs=[pl.BlockSpec(memory...]
  transfers between devices with their start and end apart: 21 -> 21, of which waited for: 10 -> 12; matrix products, arithmetic and copies ran while one was open for 0% -> 0% of each run, Pallas kernels for 3% -> 4%
where the time goes in v5:
time: 121 us
  blocking collectives  60.8 us (50%)
  starting transfers between devices  23 us (19%)
  Pallas kernels  20.7 us (17%)
  waiting for transfers between devices  15 us (12%)
    all_to_all x1, blocking collectives, per_device(): lax.all_to_all(jnp.broadcast_to(vector_grads[0], (shard_count, vector_cou...  42.5 us
    ppermute x21, starting transfers between devices, swapped(): return lax.ppermute(array, axis, pairs)  23 us
    ppermute x21, waiting for transfers between devices, swapped(): return lax.ppermute(array, axis, pairs)  15 us
    all_to_all x1, blocking collectives, per_device(): lax.all_to_all(figures, 'shard', split_axis=0, concat_axis=0, tiled=True)  10.1 us
    pallas_call x1, Pallas kernels, orthogonalize(): pl.pallas_call(functools.partial(orthogonalize_kernel, count, pieces), ou...  8.54 us
    all_to_all x1, blocking collectives, per_device(): lax.all_to_all(figures.reshape(tensor_count * section_count, 1, LANES), (...  8.23 us
    pallas_call x4, Pallas kernels, on_device(): pl.pallas_call(kernel, out_shape=out_shape, in_specs=[pl.BlockSpec(memory...  4.71 us
    pallas_call x2, Pallas kernels, row_slices(): pl.pallas_call(functools.partial(slices_kernel, offsets), out_shape=[pltp...  4.69 us
  transfers between devices with their start and end apart: 21, of which 12 were waited for; matrix products, arithmetic and copies ran while one was open for 0% of the time, Pallas kernels for 4%

profile of v5, /device:TPU:0, one launch (start us, length us, event | category | flops | bytes accessed | tf_op | source)
XLA Modules:
  0.0 120.8 jit_solution(7092017722484733605)
XLA Ops:
  0.6 0.5 compare_select_fusion.place_ref
  1.1 0.0 copy-start.6
  1.2 0.0 copy-start
  1.2 2.8 %shard_map.110 = (bf16[4,64,1024]{2,1,0:T(8,128)(2,1)S(1)}, bf16[4,64,1024]{2,1,0:T(8,128)(2,1)}) custom-call(s32[5]{0:T(128)} %compare_select_fusion.place_ref, bf16[4,4,64,1024]{3,2,1,0:T(8,128)(2,1)} %bitcast.22), custom_call_target="tpu_custom_call" | custom-call | tf_op jit(solution)/shard_map/pallas_call | solution.py:127
  4.0 4.1 %collective-permute-start.1 = (bf16[4,64,1024]{2,1,0:T(8,128)(2,1)}, bf16[4,64,1024]{2,1,0:T(8,128)(2,1)S(1)}, u32[]{:S(2)}, u32[]{:S(2)}) collective-permute-start(bf16[4,64,1024]{2,1,0:T(8,128)(2,1)} %get-tuple-element.32), channel_id=1, source_target_pairs={{0,16},{8,24},{16,0},{24,8},{1,17},{9,25},{17,1},{25,9},{2,18},{10... | collective-permute-start | bytes 1572872 | tf_op jit(solution)/shard_map/ppermute | solution.py:293
  8.1 1.3 %collective-permute-start = (bf16[4,64,1024]{2,1,0:T(8,128)(2,1)S(1)}, bf16[4,64,1024]{2,1,0:T(8,128)(2,1)S(1)}, u32[]{:S(2)}, u32[]{:S(2)}) collective-permute-start(bf16[4,64,1024]{2,1,0:T(8,128)(2,1)S(1)} %get-tuple-element.31), channel_id=1, source_target_pairs={{0,24},{8,16},{16,8},{24,0},{1,25},{9,17},{17,9},{25,1},{2,26},{10... | collective-permute-start | bytes 1572872 | tf_op jit(solution)/shard_map/ppermute | solution.py:293
  9.4 1.9 %shard_map.111 = (bf16[4,64,1024]{2,1,0:T(8,128)(2,1)S(1)}, bf16[4,64,1024]{2,1,0:T(8,128)(2,1)S(1)}) custom-call(s32[5]{0:T(128)} %compare_select_fusion.place_ref, bf16[4,4,64,1024]{3,2,1,0:T(8,128)(2,1)} %bitcast.23), custom_call_target="tpu_custom_call" | custom-call | tf_op jit(solution)/shard_map/pallas_call | solution.py:127
  11.3 0.3 collective-permute-start.2
  11.6 0.0 copy-done.6
  11.6 42.5 %all_to_all.15.refs_4_ = bf16[4,4,256]{2,1,0:T(4,128)(2,1)S(1)} all-to-all(bf16[4,4,256]{2,1,0:T(4,128)(2,1)S(1)} %broadcast_in_dim.28), channel_id=1, replica_groups=mesh['shard'=4,'tensor'=4,'section'=2] {'shard'}, dimensions={0} | all-to-all | bytes 16384 | tf_op jit(solution)/shard_map/all_to_all | solution.py:323
  54.1 0.0 collective-permute-done.1.refs_1_
  54.1 0.0 collective-permute-done.refs_0_
  54.1 0.0 collective-permute-done.2.refs_2_
  54.1 0.0 copy-done
  54.2 0.0 copy-done.2
  54.2 1.3 %shard_map.112 = (f32[4,64,1024]{2,1,0:T(8,128)S(1)}, f32[4,256]{1,0:T(4,128)S(1)}, f32[4,2,1,128]{3,2,1,0:T(1,128)S(1)}) custom-call(s32[5]{0:T(128)S(1)} %copy-done.2, bf16[4,64,1024]{2,1,0:T(8,128)(2,1)S(1)} %collective-permute-done.refs_0_, bf16[4,64,1024]{2,1,0:T(8,128)(2,1)S(1)} %collective-permute-done.1.refs_1_, ...), custom_call_target="tpu_custom_call" | custom-call | tf_op jit(solution)/shard_map/pallas_call | solution.py:282
  55.5 8.2 %all_to_all.16.figures_ref = f32[8,1,128]{2,1,0:T(1,128)S(1)} all-to-all(f32[8,1,128]{2,1,0:T(1,128)S(1)} %bitcast.18), channel_id=1, replica_groups=mesh['shard'=4,'tensor'=4,'section'=2] {'tensor','section'}, dimensions={0} | all-to-all | bytes 8192 | tf_op jit(solution)/shard_map/all_to_all | solution.py:341
  63.7 0.6 shard_map.113
  64.3 10.1 %all_to_all.17.figures_ref = f32[4,1,128]{2,1,0:T(1,128)S(1)} all-to-all(f32[4,1,128]{2,1,0:T(1,128)S(1)} %shard_map.113), channel_id=1, replica_groups=mesh['shard'=4,'tensor'=4,'section'=2] {'shard'}, dimensions={0} | all-to-all | bytes 4096 | tf_op jit(solution)/shard_map/all_to_all | solution.py:354
  74.4 1.0 shard_map.114
  75.4 0.6 collective-permute-start.3
  76.0 0.6 collective-permute-start.4
  76.6 0.6 collective-permute-start.10
  77.1 0.6 collective-permute-start.6
  77.7 3.9 %collective-permute-done.3.refs_1_ = bf16[64,1024]{1,0:T(8,128)(2,1)S(1)} collective-permute-done((bf16[64,1024]{1,0:T(8,128)(2,1)S(1)}, bf16[64,1024]{1,0:T(8,128)(2,1)S(1)}, u32[]{:S(2)}, u32[]{:S(2)}) %collective-permute-start.3) | collective-permute-done | bytes 131104 | tf_op jit(solution)/shard_map/ppermute | solution.py:293
  81.6 0.6 collective-permute-start.11
  82.2 1.4 %collective-permute-done.4.refs_2_ = bf16[64,1024]{1,0:T(8,128)(2,1)S(1)} collective-permute-done((bf16[64,1024]{1,0:T(8,128)(2,1)S(1)}, bf16[64,1024]{1,0:T(8,128)(2,1)S(1)}, u32[]{:S(2)}, u32[]{:S(2)}) %collective-permute-start.4) | collective-permute-done | bytes 131104 | tf_op jit(solution)/shard_map/ppermute | solution.py:293
  83.6 1.3 %collective-permute-start.5 = (bf16[64,1024]{1,0:T(8,128)(2,1)S(1)}, bf16[64,1024]{1,0:T(8,128)(2,1)S(1)}, u32[]{:S(2)}, u32[]{:S(2)}) collective-permute-start(bf16[64,1024]{1,0:T(8,128)(2,1)S(1)} %get-tuple-element.43), channel_id=1, source_target_pairs={{0,24},{8,16},{16,8},{24,0},{1,25},{9,17},{17,9},{25,1},{2,26},{10... | collective-permute-start | bytes 393224 | tf_op jit(solution)/shard_map/ppermute | solution.py:293
  84.9 0.6 collective-permute-start.7
  85.4 0.0 collective-permute-done.10.refs_8_
  85.5 0.6 collective-permute-start.12
  86.0 0.0 collective-permute-done.6.refs_4_
  86.0 1.5 %collective-permute-start.8 = (bf16[64,1024]{1,0:T(8,128)(2,1)S(1)}, bf16[64,1024]{1,0:T(8,128)(2,1)S(1)}, u32[]{:S(2)}, u32[]{:S(2)}) collective-permute-start(bf16[64,1024]{1,0:T(8,128)(2,1)S(1)} %collective-permute-done.4.refs_2_), channel_id=1, source_target_pairs={{0,2},{2,0},{4,6},{6,4},{1,3},{3,1},{5,7},{7,5},{8,10},{10,8},{12,... | collective-permute-start | bytes 393224 | tf_op jit(solution)/shard_map/ppermute | solution.py:293
  87.5 0.5 collective-permute-done.11.refs_9_
  88.0 1.0 collective-permute-start.14
  89.0 1.4 %collective-permute-done.5.refs_3_ = bf16[64,1024]{1,0:T(8,128)(2,1)S(1)} collective-permute-done((bf16[64,1024]{1,0:T(8,128)(2,1)S(1)}, bf16[64,1024]{1,0:T(8,128)(2,1)S(1)}, u32[]{:S(2)}, u32[]{:S(2)}) %collective-permute-start.5) | collective-permute-done | bytes 131104 | tf_op jit(solution)/shard_map/ppermute | solution.py:293
  90.4 0.6 collective-permute-start.17
  91.0 0.3 collective-permute-done.7.refs_5_
  91.3 1.2 collective-permute-start.13
  92.4 0.9 collective-permute-done.12.refs_10_
  93.3 1.0 collective-permute-start.15
  94.3 0.0 collective-permute-done.8.refs_6_
  94.3 1.0 collective-permute-start.9
  95.3 0.8 collective-permute-done.14.refs_12_
  96.1 1.3 %collective-permute-start.16 = (bf16[64,1024]{1,0:T(8,128)(2,1)S(1)}, bf16[64,1024]{1,0:T(8,128)(2,1)S(1)}, u32[]{:S(2)}, u32[]{:S(2)}) collective-permute-start(bf16[64,1024]{1,0:T(8,128)(2,1)S(1)} %collective-permute-done.8.refs_6_), channel_id=1, source_target_pairs={{0,4},{2,6},{4,0},{6,2},{1,5},{3,7},{5,1},{7,3},{8,12},{10,14},{12... | collective-permute-start | bytes 393224 | tf_op jit(solution)/shard_map/ppermute | solution.py:293
  97.4 0.9 collective-permute-done.15.refs_13_
  98.3 0.0 collective-permute-done.17.refs_15_
  98.3 0.1 collective-permute-done.13.refs_11_
  98.4 1.3 %collective-permute-done.9.refs_7_ = bf16[64,1024]{1,0:T(8,128)(2,1)S(1)} collective-permute-done((bf16[64,1024]{1,0:T(8,128)(2,1)S(1)}, bf16[64,1024]{1,0:T(8,128)(2,1)S(1)}, u32[]{:S(2)}, u32[]{:S(2)}) %collective-permute-start.9) | collective-permute-done | bytes 131104 | tf_op jit(solution)/shard_map/ppermute | solution.py:293
  99.7 1.4 %collective-permute-done.16.refs_14_ = bf16[64,1024]{1,0:T(8,128)(2,1)S(1)} collective-permute-done((bf16[64,1024]{1,0:T(8,128)(2,1)S(1)}, bf16[64,1024]{1,0:T(8,128)(2,1)S(1)}, u32[]{:S(2)}, u32[]{:S(2)}) %collective-permute-start.16) | collective-permute-done | bytes 131104 | tf_op jit(solution)/shard_map/ppermute | solution.py:293
  101.1 8.5 %shard_map.115 = (bf16[64,1024]{1,0:T(8,128)(2,1)S(1)}, bf16[64,1024]{1,0:T(8,128)(2,1)S(1)}, bf16[64,1024]{1,0:T(8,128)(2,1)S(1)}, bf16[64,1024]{1,0:T(8,128)(2,1)S(1)}) custom-call(bf16[64,1024]{1,0:T(8,128)(2,1)S(1)} %get-tuple-element.39.refs_0_, bf16[64,1024]{1,0:T(8,128)(2,1)S(1)} %collective-permute-done.3.refs_1_, ...), custom_call_target="tpu_custom_call" | custom-call | tf_op jit(solution)/shard_map/pallas_call | solution.py:93
  109.6 1.9 %collective-permute-start.18 = (bf16[64,1024]{1,0:T(8,128)(2,1)S(1)}, bf16[64,1024]{1,0:T(8,128)(2,1)S(1)}, u32[]{:S(2)}, u32[]{:S(2)}) collective-permute-start(bf16[64,1024]{1,0:T(8,128)(2,1)S(1)} %get-tuple-element.48), channel_id=1, source_target_pairs={{0,24},{8,16},{16,8},{24,0},{1,25},{9,17},{17,9},{25,1},{2,26},{10... | collective-permute-start | bytes 393224 | tf_op jit(solution)/shard_map/ppermute | solution.py:293
  111.5 0.0 collective-permute-start.19
  111.5 2.5 %collective-permute-start.20 = (bf16[64,1024]{1,0:T(8,128)(2,1)S(1)}, bf16[64,1024]{1,0:T(8,128)(2,1)S(1)}, u32[]{:S(2)}, u32[]{:S(2)}) collective-permute-start(bf16[64,1024]{1,0:T(8,128)(2,1)S(1)} %get-tuple-element.50), channel_id=1, source_target_pairs={{0,8},{8,0},{16,24},{24,16},{1,9},{9,1},{17,25},{25,17},{2,10},{10... | collective-permute-start | bytes 393224 | tf_op jit(solution)/shard_map/ppermute | solution.py:293
  114.1 0.0 copy-done.1
  114.1 1.3 %shard_map.117 = (bf16[4,64,1024]{2,1,0:T(8,128)(2,1)}, bf16[4,64,1024]{2,1,0:T(8,128)(2,1)}) custom-call(s32[5]{0:T(128)S(1)} %copy-done.2, bf16[64,1024]{1,0:T(8,128)(2,1)S(1)} %get-tuple-element.44.refs_0_, bf16[4,64,1024]{2,1,0:T(8,128)(2,1)S(1)} %bitcast.16), custom_call_target="tpu_custom_call" | custom-call | tf_op jit(solution)/shard_map/pallas_call | solution.py:236
  115.3 0.0 copy-done.3
  115.4 0.0 copy-done.4
  115.4 0.0 copy-done.5
  115.4 1.8 %shard_map.116 = (f32[4,64,1024]{2,1,0:T(8,128)}, f32[4,64]{1,0:T(4,128)}, f32[4,64]{1,0:T(4,128)}) custom-call(s32[5]{0:T(128)S(1)} %copy-done.2, f32[8,128]{1,0:T(8,128)S(1)} %get-tuple-element.45.clip_ref, f32[4,64,1024]{2,1,0:T(8,128)S(1)} %get-tuple-element.37.grad_ref, f32[4,64,1024]{2,1,0:T(8,128)S(1)} %bitcast.15, ...), custom_call_target="tpu_custom_call" | custom-call | tf_op jit(solution)/shard_map/pallas_call | solution.py:282
  117.2 0.0 collective-permute-done.18.refs_0_
  117.2 2.1 %collective-permute-done.19.refs_1_ = bf16[64,1024]{1,0:T(8,128)(2,1)S(1)} collective-permute-done((bf16[64,1024]{1,0:T(8,128)(2,1)S(1)}, bf16[64,1024]{1,0:T(8,128)(2,1)S(1)}, u32[]{:S(2)}, u32[]{:S(2)}) %collective-permute-start.19) | collective-permute-done | bytes 131104 | tf_op jit(solution)/shard_map/ppermute | solution.py:293
  119.3 0.0 collective-permute-done.20.refs_2_
  119.3 1.5 %shard_map.118 = (bf16[4,64,1024]{2,1,0:T(8,128)(2,1)}, bf16[4,64,1024]{2,1,0:T(8,128)(2,1)}) custom-call(s32[5]{0:T(128)S(1)} %copy-done.2, bf16[64,1024]{1,0:T(8,128)(2,1)S(1)} %collective-permute-done.18.refs_0_, bf16[64,1024]{1,0:T(8,128)(2,1)S(1)} %collective-permute-done.19.refs_1_, ...), custom_call_target="tpu_custom_call", output_to_operand_aliasing={{0}: (5, {}), {1}: (6, {})} | custom-call | tf_op jit(solution)/shard_map/pallas_call | solution.py:236
  (6 shorter events, 0.0 us)
Async XLA Ops:
  1.1 10.5 %copy-start.6 = (bf16[1,1,4,256]{3,2,1,0:T(4,128)(2,1)S(1)}, bf16[1,1,4,256]{3,2,1,0:T(4,128)(2,1)}, u32[]{:S(2)}) copy-start(bf16[1,1,4,256]{3,2,1,0:T(4,128)(2,1)} %param.8) | copy-start | bytes 6148
  1.2 53.0 %copy-start = (f32[1,4,64,1024]{3,2,1,0:T(8,128)S(1)}, f32[1,4,64,1024]{3,2,1,0:T(8,128)}, u32[]{:S(2)}) copy-start(f32[1,4,64,1024]{3,2,1,0:T(8,128)} %param.9) | copy-start | bytes 3145732
  1.2 53.0 %copy-start.2 = (s32[5]{0:T(128)S(1)}, s32[5]{0:T(128)}, u32[]{:S(2)}) copy-start(s32[5]{0:T(128)} %compare_select_fusion.place_ref) | copy-start | bytes 64
  4.0 50.2 %collective-permute-start.1 = (bf16[4,64,1024]{2,1,0:T(8,128)(2,1)}, bf16[4,64,1024]{2,1,0:T(8,128)(2,1)S(1)}, u32[]{:S(2)}, u32[]{:S(2)}) collective-permute-start(bf16[4,64,1024]{2,1,0:T(8,128)(2,1)} %get-tuple-element.32), channel_id=1, source_target_pairs={{0,16},{8,24},{16,0},{24,8},{1,17},{9,25},{17,1},{25,9},{2,18},{10... | collective-permute-start | bytes 1572872 | tf_op jit(solution)/shard_map/ppermute | solution.py:293
  8.1 46.1 %collective-permute-start = (bf16[4,64,1024]{2,1,0:T(8,128)(2,1)S(1)}, bf16[4,64,1024]{2,1,0:T(8,128)(2,1)S(1)}, u32[]{:S(2)}, u32[]{:S(2)}) collective-permute-start(bf16[4,64,1024]{2,1,0:T(8,128)(2,1)S(1)} %get-tuple-element.31), channel_id=1, source_target_pairs={{0,24},{8,16},{16,8},{24,0},{1,25},{9,17},{17,9},{25,1},{2,26},{10... | collective-permute-start | bytes 1572872 | tf_op jit(solution)/shard_map/ppermute | solution.py:293
  11.3 42.8 %collective-permute-start.2 = (bf16[4,64,1024]{2,1,0:T(8,128)(2,1)S(1)}, bf16[4,64,1024]{2,1,0:T(8,128)(2,1)S(1)}, u32[]{:S(2)}, u32[]{:S(2)}) collective-permute-start(bf16[4,64,1024]{2,1,0:T(8,128)(2,1)S(1)} %get-tuple-element.34), channel_id=1, source_target_pairs={{0,8},{8,0},{16,24},{24,16},{1,9},{9,1},{17,25},{25,17},{2,10},{10... | collective-permute-start | bytes 1572872 | tf_op jit(solution)/shard_map/ppermute | solution.py:293
  74.4 39.7 %copy-start.1 = (bf16[1,4,64,1024]{3,2,1,0:T(8,128)(2,1)S(1)}, bf16[1,4,64,1024]{3,2,1,0:T(8,128)(2,1)}, u32[]{:S(2)}) copy-start(bf16[1,4,64,1024]{3,2,1,0:T(8,128)(2,1)} %param.10) | copy-start | bytes 1572868
  74.4 41.0 %copy-start.3 = (f32[1,4,64]{2,1,0:T(4,128)S(1)}, f32[1,4,64]{2,1,0:T(4,128)}, u32[]{:S(2)}) copy-start(f32[1,4,64]{2,1,0:T(4,128)} %param.11) | copy-start | bytes 3076
  74.4 41.0 %copy-start.4 = (f32[1,4,64]{2,1,0:T(4,128)S(1)}, f32[1,4,64]{2,1,0:T(4,128)}, u32[]{:S(2)}) copy-start(f32[1,4,64]{2,1,0:T(4,128)} %param.12) | copy-start | bytes 3076
  74.4 41.0 %copy-start.5 = (f32[1,4,64]{2,1,0:T(4,128)S(1)}, f32[1,4,64]{2,1,0:T(4,128)}, u32[]{:S(2)}) copy-start(f32[1,4,64]{2,1,0:T(4,128)} %param.13) | copy-start | bytes 3076
  75.4 6.2 %collective-permute-start.3 = (bf16[64,1024]{1,0:T(8,128)(2,1)S(1)}, bf16[64,1024]{1,0:T(8,128)(2,1)S(1)}, u32[]{:S(2)}, u32[]{:S(2)}) collective-permute-start(bf16[64,1024]{1,0:T(8,128)(2,1)S(1)} %get-tuple-element.40), channel_id=1, source_target_pairs={{0,8},{8,0},{16,24},{24,16},{1,9},{9,1},{17,25},{25,17},{2,10},{10... | collective-permute-start | bytes 393224 | tf_op jit(solution)/shard_map/ppermute | solution.py:293
  76.0 7.6 %collective-permute-start.4 = (bf16[64,1024]{1,0:T(8,128)(2,1)S(1)}, bf16[64,1024]{1,0:T(8,128)(2,1)S(1)}, u32[]{:S(2)}, u32[]{:S(2)}) collective-permute-start(bf16[64,1024]{1,0:T(8,128)(2,1)S(1)} %get-tuple-element.41), channel_id=1, source_target_pairs={{0,16},{8,24},{16,0},{24,8},{1,17},{9,25},{17,1},{25,9},{2,18},{10... | collective-permute-start | bytes 393224 | tf_op jit(solution)/shard_map/ppermute | solution.py:293
  76.6 8.9 %collective-permute-start.10 = (bf16[64,1024]{1,0:T(8,128)(2,1)S(1)}, bf16[64,1024]{1,0:T(8,128)(2,1)S(1)}, u32[]{:S(2)}, u32[]{:S(2)}) collective-permute-start(bf16[64,1024]{1,0:T(8,128)(2,1)S(1)} %get-tuple-element.39.refs_0_), channel_id=1, source_target_pairs={{0,4},{2,6},{4,0},{6,2},{1,5},{3,7},{5,1},{7,3},{8,12},{10,14},{12... | collective-permute-start | bytes 393224 | tf_op jit(solution)/shard_map/ppermute | solution.py:293
  77.1 8.9 %collective-permute-start.6 = (bf16[64,1024]{1,0:T(8,128)(2,1)S(1)}, bf16[64,1024]{1,0:T(8,128)(2,1)S(1)}, u32[]{:S(2)}, u32[]{:S(2)}) collective-permute-start(bf16[64,1024]{1,0:T(8,128)(2,1)S(1)} %get-tuple-element.39.refs_0_), channel_id=1, source_target_pairs={{0,2},{2,0},{4,6},{6,4},{1,3},{3,1},{5,7},{7,5},{8,10},{10,8},{12,... | collective-permute-start | bytes 393224 | tf_op jit(solution)/shard_map/ppermute | solution.py:293
  81.6 6.4 %collective-permute-start.11 = (bf16[64,1024]{1,0:T(8,128)(2,1)S(1)}, bf16[64,1024]{1,0:T(8,128)(2,1)S(1)}, u32[]{:S(2)}, u32[]{:S(2)}) collective-permute-start(bf16[64,1024]{1,0:T(8,128)(2,1)S(1)} %collective-permute-done.3.refs_1_), channel_id=1, source_target_pairs={{0,4},{2,6},{4,0},{6,2},{1,5},{3,7},{5,1},{7,3},{8,12},{10,14},{12... | collective-permute-start | bytes 393224 | tf_op jit(solution)/shard_map/ppermute | solution.py:293
  83.6 6.8 %collective-permute-start.5 = (bf16[64,1024]{1,0:T(8,128)(2,1)S(1)}, bf16[64,1024]{1,0:T(8,128)(2,1)S(1)}, u32[]{:S(2)}, u32[]{:S(2)}) collective-permute-start(bf16[64,1024]{1,0:T(8,128)(2,1)S(1)} %get-tuple-element.43), channel_id=1, source_target_pairs={{0,24},{8,16},{16,8},{24,0},{1,25},{9,17},{17,9},{25,1},{2,26},{10... | collective-permute-start | bytes 393224 | tf_op jit(solution)/shard_map/ppermute | solution.py:293
  84.9 6.4 %collective-permute-start.7 = (bf16[64,1024]{1,0:T(8,128)(2,1)S(1)}, bf16[64,1024]{1,0:T(8,128)(2,1)S(1)}, u32[]{:S(2)}, u32[]{:S(2)}) collective-permute-start(bf16[64,1024]{1,0:T(8,128)(2,1)S(1)} %collective-permute-done.3.refs_1_), channel_id=1, source_target_pairs={{0,2},{2,0},{4,6},{6,4},{1,3},{3,1},{5,7},{7,5},{8,10},{10,8},{12,... | collective-permute-start | bytes 393224 | tf_op jit(solution)/shard_map/ppermute | solution.py:293
  85.5 7.9 %collective-permute-start.12 = (bf16[64,1024]{1,0:T(8,128)(2,1)S(1)}, bf16[64,1024]{1,0:T(8,128)(2,1)S(1)}, u32[]{:S(2)}, u32[]{:S(2)}) collective-permute-start(bf16[64,1024]{1,0:T(8,128)(2,1)S(1)} %collective-permute-done.4.refs_2_), channel_id=1, source_target_pairs={{0,4},{2,6},{4,0},{6,2},{1,5},{3,7},{5,1},{7,3},{8,12},{10,14},{12... | collective-permute-start | bytes 393224 | tf_op jit(solution)/shard_map/ppermute | solution.py:293
  86.0 8.3 %collective-permute-start.8 = (bf16[64,1024]{1,0:T(8,128)(2,1)S(1)}, bf16[64,1024]{1,0:T(8,128)(2,1)S(1)}, u32[]{:S(2)}, u32[]{:S(2)}) collective-permute-start(bf16[64,1024]{1,0:T(8,128)(2,1)S(1)} %collective-permute-done.4.refs_2_), channel_id=1, source_target_pairs={{0,2},{2,0},{4,6},{6,4},{1,3},{3,1},{5,7},{7,5},{8,10},{10,8},{12,... | collective-permute-start | bytes 393224 | tf_op jit(solution)/shard_map/ppermute | solution.py:293
  88.0 8.1 %collective-permute-start.14 = (bf16[64,1024]{1,0:T(8,128)(2,1)S(1)}, bf16[64,1024]{1,0:T(8,128)(2,1)S(1)}, u32[]{:S(2)}, u32[]{:S(2)}) collective-permute-start(bf16[64,1024]{1,0:T(8,128)(2,1)S(1)} %collective-permute-done.6.refs_4_), channel_id=1, source_target_pairs={{0,4},{2,6},{4,0},{6,2},{1,5},{3,7},{5,1},{7,3},{8,12},{10,14},{12... | collective-permute-start | bytes 393224 | tf_op jit(solution)/shard_map/ppermute | solution.py:293
  90.4 7.9 %collective-permute-start.17 = (bf16[64,1024]{1,0:T(8,128)(2,1)S(1)}, bf16[64,1024]{1,0:T(8,128)(2,1)S(1)}, u32[]{:S(2)}, u32[]{:S(2)}) collective-permute-start(bf16[64,1024]{1,0:T(8,128)(2,1)S(1)} %collective-permute-done.5.refs_3_), channel_id=1, source_target_pairs={{0,6},{2,4},{4,2},{6,0},{1,7},{3,5},{5,3},{7,1},{8,14},{10,12},{12... | collective-permute-start | bytes 393224 | tf_op jit(solution)/shard_map/ppermute | solution.py:293
  91.3 7.1 %collective-permute-start.13 = (bf16[64,1024]{1,0:T(8,128)(2,1)S(1)}, bf16[64,1024]{1,0:T(8,128)(2,1)S(1)}, u32[]{:S(2)}, u32[]{:S(2)}) collective-permute-start(bf16[64,1024]{1,0:T(8,128)(2,1)S(1)} %collective-permute-done.5.refs_3_), channel_id=1, source_target_pairs={{0,4},{2,6},{4,0},{6,2},{1,5},{3,7},{5,1},{7,3},{8,12},{10,14},{12... | collective-permute-start | bytes 393224 | tf_op jit(solution)/shard_map/ppermute | solution.py:293
  93.3 5.0 %collective-permute-start.15 = (bf16[64,1024]{1,0:T(8,128)(2,1)S(1)}, bf16[64,1024]{1,0:T(8,128)(2,1)S(1)}, u32[]{:S(2)}, u32[]{:S(2)}) collective-permute-start(bf16[64,1024]{1,0:T(8,128)(2,1)S(1)} %collective-permute-done.11.refs_9_), channel_id=1, source_target_pairs={{0,2},{2,0},{4,6},{6,4},{1,3},{3,1},{5,7},{7,5},{8,10},{10,8},{12,... | collective-permute-start | bytes 393224 | tf_op jit(solution)/shard_map/ppermute | solution.py:293
  94.3 5.4 %collective-permute-start.9 = (bf16[64,1024]{1,0:T(8,128)(2,1)S(1)}, bf16[64,1024]{1,0:T(8,128)(2,1)S(1)}, u32[]{:S(2)}, u32[]{:S(2)}) collective-permute-start(bf16[64,1024]{1,0:T(8,128)(2,1)S(1)} %collective-permute-done.5.refs_3_), channel_id=1, source_target_pairs={{0,2},{2,0},{4,6},{6,4},{1,3},{3,1},{5,7},{7,5},{8,10},{10,8},{12,... | collective-permute-start | bytes 393224 | tf_op jit(solution)/shard_map/ppermute | solution.py:293
  96.1 5.0 %collective-permute-start.16 = (bf16[64,1024]{1,0:T(8,128)(2,1)S(1)}, bf16[64,1024]{1,0:T(8,128)(2,1)S(1)}, u32[]{:S(2)}, u32[]{:S(2)}) collective-permute-start(bf16[64,1024]{1,0:T(8,128)(2,1)S(1)} %collective-permute-done.8.refs_6_), channel_id=1, source_target_pairs={{0,4},{2,6},{4,0},{6,2},{1,5},{3,7},{5,1},{7,3},{8,12},{10,14},{12... | collective-permute-start | bytes 393224 | tf_op jit(solution)/shard_map/ppermute | solution.py:293
  109.6 7.6 %collective-permute-start.18 = (bf16[64,1024]{1,0:T(8,128)(2,1)S(1)}, bf16[64,1024]{1,0:T(8,128)(2,1)S(1)}, u32[]{:S(2)}, u32[]{:S(2)}) collective-permute-start(bf16[64,1024]{1,0:T(8,128)(2,1)S(1)} %get-tuple-element.48), channel_id=1, source_target_pairs={{0,24},{8,16},{16,8},{24,0},{1,25},{9,17},{17,9},{25,1},{2,26},{10... | collective-permute-start | bytes 393224 | tf_op jit(solution)/shard_map/ppermute | solution.py:293
  111.5 7.8 %collective-permute-start.19 = (bf16[64,1024]{1,0:T(8,128)(2,1)S(1)}, bf16[64,1024]{1,0:T(8,128)(2,1)S(1)}, u32[]{:S(2)}, u32[]{:S(2)}) collective-permute-start(bf16[64,1024]{1,0:T(8,128)(2,1)S(1)} %get-tuple-element.49), channel_id=1, source_target_pairs={{0,16},{8,24},{16,0},{24,8},{1,17},{9,25},{17,1},{25,9},{2,18},{10... | collective-permute-start | bytes 393224 | tf_op jit(solution)/shard_map/ppermute | solution.py:293
  111.5 7.8 %collective-permute-start.20 = (bf16[64,1024]{1,0:T(8,128)(2,1)S(1)}, bf16[64,1024]{1,0:T(8,128)(2,1)S(1)}, u32[]{:S(2)}, u32[]{:S(2)}) collective-permute-start(bf16[64,1024]{1,0:T(8,128)(2,1)S(1)} %get-tuple-element.50), channel_id=1, source_target_pairs={{0,8},{8,0},{16,24},{24,16},{1,9},{9,1},{17,25},{25,17},{2,10},{10... | collective-permute-start | bytes 393224 | tf_op jit(solution)/shard_map/ppermute | solution.py:293

commit v6 on v4

--- a/solution.py
+++ b/solution.py
@@ -29,12 +29,12 @@
 MESH_AXES = ("shard", "tensor", "section")
 
 
-def gram_of(blocks, gram_ref):
+def gram_of(blocks, gram_ref, ready_ref=None):
     width = blocks[0].shape[1]
     step = 256
     for start in range(0, width, step):
         stop = start + step
-        total = None
+        total = None if ready_ref is None else ready_ref[:stop, start:stop].astype(jnp.float32)
         for block in blocks:
             whole = block[...]
             product = lax.dot_general(
@@ -63,11 +63,39 @@
     return combined.astype(jnp.bfloat16)
 
 
+def block_gram_kernel(*refs):
+    pieces, (gram_ref, rows_ref) = refs[:-2], refs[-2:]
+    height = pieces[0].shape[0]
+    for position, piece_ref in enumerate(pieces):
+        rows_ref[position * height : (position + 1) * height, :] = piece_ref[...]
+    whole = rows_ref[...]
+    step = 256
+    for start in range(0, whole.shape[1], step):
+        stop = start + step
+        gram_ref[:stop, start:stop] = lax.dot_general(
+            whole[:, :stop],
+            whole[:, start:stop],
+            (((0,), (0,)), ((), ())),
+            preferred_element_type=jnp.float32,
+        ).astype(jnp.bfloat16)
+
+
+def block_gram(pieces):
+    height, width = pieces[0].shape
+    return pl.pallas_call(
+        block_gram_kernel,
+        out_shape=jax.ShapeDtypeStruct((width, width), jnp.bfloat16),
+        scratch_shapes=[pltpu.VMEM((len(pieces) * height, width), jnp.bfloat16)],
+        compiler_params=pltpu.CompilerParams(vmem_limit_bytes=16 * MIB),
+    )(*pieces)
+
+
 def orthogonalize_kernel(count, pieces, *refs):
     height, width = refs[0].shape
     inputs = refs[: count * pieces]
-    outputs = refs[count * pieces : count * pieces + pieces]
-    gram_ref, start_ref, next_ref = refs[count * pieces + pieces :]
+    ready_ref = refs[count * pieces]
+    outputs = refs[count * pieces + 1 : count * pieces + 1 + pieces]
+    gram_ref, start_ref, next_ref = refs[count * pieces + 1 + pieces :]
     block = pieces * height
     rows = count * block
     chunk = 2 * block if count % 2 == 0 else block
@@ -75,7 +103,11 @@
         start_ref[position * height : (position + 1) * height, :] = piece_ref[...]
     current, other = start_ref, next_ref
     for iteration in range(NS_STEPS):
-        gram_of([current.at[start : start + block] for start in range(0, rows, block)], gram_ref)
+        blocks = [current.at[start : start + block] for start in range(0, rows, block)]
+        if iteration == 0:
+            gram_of(blocks[1:], gram_ref, ready_ref)
+        else:
+            gram_of(blocks, gram_ref)
         if iteration + 1 < NS_STEPS:
             for start in range(0, rows, chunk):
                 other[start : start + chunk, :] = polynomial(
@@ -87,7 +119,7 @@
         outputs[piece][...] = result[piece * height : (piece + 1) * height, :]
 
 
-def orthogonalize(blocks):
+def orthogonalize(blocks, own_gram):
     count, pieces = len(blocks), len(blocks[0])
     height, width = blocks[0][0].shape
     return pl.pallas_call(
@@ -99,7 +131,7 @@
             pltpu.VMEM((count * pieces * height, width), jnp.bfloat16),
         ],
         compiler_params=pltpu.CompilerParams(vmem_limit_bytes=32 * MIB),
-    )(*[piece for block in blocks for piece in block])
+    )(*[piece for block in blocks for piece in block], own_gram)
 
 
 def folded(array):
@@ -128,14 +160,14 @@
     matrix_count, shard_count, height, width = by_rows.shape
     return pl.pallas_call(
         functools.partial(slices_kernel, shard_count),
-        out_shape=[pltpu.VMEM((matrix_count, height, width), by_rows.dtype)] * shard_count,
+        out_shape=[jax.ShapeDtypeStruct((matrix_count, height, width), by_rows.dtype)] * shard_count,
         in_specs=[
             pl.BlockSpec(memory_space=pltpu.SMEM),
             pl.BlockSpec(memory_space=pltpu.HBM),
         ],
         out_specs=[pl.BlockSpec(memory_space=pltpu.VMEM)] * shard_count,
         scratch_shapes=[pltpu.SemaphoreType.DMA((shard_count,))],
-        compiler_params=pltpu.CompilerParams(vmem_limit_bytes=60 * MIB),
+        compiler_params=pltpu.CompilerParams(vmem_limit_bytes=4 * MIB),
     )(place, by_rows)
 
 
@@ -366,7 +398,8 @@
     near[3] = swapped(pieces[3], "tensor", 1)
     side[3] = swapped(pieces[3], "tensor", 2)
     far[3] = swapped(pieces[3], "tensor", 3)
-    results = orthogonalize([pieces, near, side, far])
+    own_gram = block_gram(pieces[:3] + [after(pieces[3], far[1])])
+    results = orthogonalize([pieces, near, side, far], own_gram)
 
     returned = {
         offset: swapped(results[offset], "shard", offset)
@@ -481,7 +514,7 @@
     for offset in range(1, tensor_count):
         pairs = [(i, i ^ offset) for i in range(tensor_count)]
         blocks.append(lax.ppermute(row_block, "tensor", pairs))
-    (own_result,) = orthogonalize([[block] for block in blocks])
+    (own_result,) = orthogonalize([[block] for block in blocks], block_gram(blocks[:1]))
 
     if owner_count == 1:
         own_update = lax.all_to_all(

time: 116 us -> 117 us (level)
  local copies, waits for them, and re-layouts: 0.03 us -> 1.71 us
  Pallas kernels: 17.8 us -> 16.4 us
    unnamed x14, local copies, waits for them, and re-layouts: 0.03 us -> 1.7 us
    pallas_call x1, Pallas kernels: 2.35 us -> 0.73 us  [row_slices(): pl.pallas_call(functools.partial(slices_kernel, shard_count), out_shape=[...]
  transfers between devices with their start and end apart: 21 -> 21, of which waited for: 10 -> 11; matrix products, arithmetic and copies ran while one was open for 0% -> 0% of each run, Pallas kernels for 3% -> 3%
where the time goes in v6:
time: 117 us; the launch traced here: 116 us
  blocking collectives  56 us (48%)
  starting transfers between devices  22.8 us (19%)
  waiting for transfers between devices  18.8 us (16%)
  Pallas kernels  16.4 us (14%)
  local copies, waits for them, and re-layouts  1.71 us (1%)
    all_to_all x1, blocking collectives, per_device(): lax.all_to_all(jnp.broadcast_to(vector_grads[0], (shard_count, vector_cou...  44.3 us
    ppermute x21, starting transfers between devices, swapped(): return lax.ppermute(array, axis, pairs)  22.8 us
    ppermute x21, waiting for transfers between devices, swapped(): return lax.ppermute(array, axis, pairs)  18.8 us
    all_to_all x1, blocking collectives, per_device(): lax.all_to_all(figures.reshape(others * section_count, 1, LANES), MESH_AX...  11.7 us
    pallas_call x1, Pallas kernels, orthogonalize(): pl.pallas_call(functools.partial(orthogonalize_kernel, count, pieces), ou...  8.14 us
    pallas_call x3, Pallas kernels, on_device(): pl.pallas_call(kernel, out_shape=out_shape, in_specs=[pl.BlockSpec(memory...  4.2 us
    pallas_call x2, Pallas kernels, finished(): pl.pallas_call(functools.partial(end_kernel, offsets), out_shape=[jax.Sha...  2.74 us
  transfers between devices with their start and end apart: 21, of which 11 were waited for; matrix products, arithmetic and copies ran while one was open for 0% of the time, Pallas kernels for 3%

profile of v6, /device:TPU:0, one launch (start us, length us, event | category | flops | bytes accessed | tf_op | source)
XLA Modules:
  0.0 116.4 jit_solution(6609800870747463527)
XLA Ops:
  0.6 0.0 copy-start
  0.7 0.0 copy-start.2
  0.7 1.7 %copy-done.2 = bf16[1,1,4,256,1024]{4,3,2,1,0:T(8,128)(2,1)S(1)} copy-done((bf16[1,1,4,256,1024]{4,3,2,1,0:T(8,128)(2,1)S(1)}, bf16[1,1,4,256,1024]{4,3,2,1,0:T(8,128)(2,1)}, u32[]{:S(2)}) %copy-start.2) | copy-done | bytes 2097176
  2.3 0.7 shard_map.110
  3.1 5.1 %collective-permute-start = (bf16[4,64,1024]{2,1,0:T(8,128)(2,1)S(1)}, bf16[4,64,1024]{2,1,0:T(8,128)(2,1)S(1)}, u32[]{:S(2)}, u32[]{:S(2)}) collective-permute-start(bf16[4,64,1024]{2,1,0:T(8,128)(2,1)S(1)} %get-tuple-element.31), channel_id=1, source_target_pairs={{0,24},{8,16},{16,8},{24,0},{1,25},{9,17},{17,9},{25,1},{2,26},{10... | collective-permute-start | bytes 1572872 | tf_op jit(solution)/shard_map/ppermute | solution.py:321
  8.2 0.0 collective-permute-start.1
  8.2 0.6 collective-permute-start.2
  8.8 0.0 copy-done.6
  8.8 44.3 %all_to_all.10.refs_4_ = bf16[4,4,256]{2,1,0:T(4,128)(2,1)S(1)} all-to-all(bf16[4,4,256]{2,1,0:T(4,128)(2,1)S(1)} %broadcast_in_dim.28), channel_id=1, replica_groups=mesh['shard'=4,'tensor'=4,'section'=2] {'shard'}, dimensions={0} | all-to-all | bytes 16384 | tf_op jit(solution)/shard_map/all_to_all | solution.py:350
  53.1 0.0 collective-permute-done.refs_0_
  53.2 0.0 collective-permute-done.1.refs_1_
  53.2 0.0 collective-permute-done.2.refs_2_
  53.2 0.0 copy-done
  53.2 1.3 %shard_map.111 = (f32[4,64,1024]{2,1,0:T(8,128)S(1)}, f32[4,256]{1,0:T(4,128)S(1)}, f32[16,2,1,128]{3,2,1,0:T(1,128)S(1)}) custom-call(s32[5]{0:T(128)S(1)} %compare_select_fusion.place_ref, bf16[4,64,1024]{2,1,0:T(8,128)(2,1)S(1)} %collective-permute-done.refs_0_, bf16[4,64,1024]{2,1,0:T(8,128)(2,1)S(1)} %collective-permute-done.1.refs_1_, ...), custom_call_target="tpu_custom_call" | custom-call | tf_op jit(solution)/shard_map/pallas_call | solution.py:310
  54.5 11.7 %all_to_all.11.figures_ref = f32[32,1,128]{2,1,0:T(1,128)S(1)} all-to-all(f32[32,1,128]{2,1,0:T(1,128)S(1)} %bitcast.19), channel_id=1, replica_groups=mesh['shard'=4,'tensor'=4,'section'=2] {'shard','tensor','section'}, dimensions={0} | all-to-all | bytes 32768 | tf_op jit(solution)/shard_map/all_to_all | solution.py:369
  66.2 1.0 shard_map.112
  67.2 0.6 collective-permute-start.3
  67.9 0.6 collective-permute-start.4
  68.4 0.5 collective-permute-start.10
  69.0 0.6 collective-permute-start.6
  69.5 4.6 %collective-permute-done.3.refs_1_ = bf16[64,1024]{1,0:T(8,128)(2,1)S(1)} collective-permute-done((bf16[64,1024]{1,0:T(8,128)(2,1)S(1)}, bf16[64,1024]{1,0:T(8,128)(2,1)S(1)}, u32[]{:S(2)}, u32[]{:S(2)}) %collective-permute-start.3) | collective-permute-done | bytes 131104 | tf_op jit(solution)/shard_map/ppermute | solution.py:321
  74.2 0.5 collective-permute-start.11
  74.7 1.8 %collective-permute-done.4.refs_2_ = bf16[64,1024]{1,0:T(8,128)(2,1)S(1)} collective-permute-done((bf16[64,1024]{1,0:T(8,128)(2,1)S(1)}, bf16[64,1024]{1,0:T(8,128)(2,1)S(1)}, u32[]{:S(2)}, u32[]{:S(2)}) %collective-permute-start.4) | collective-permute-done | bytes 131104 | tf_op jit(solution)/shard_map/ppermute | solution.py:321
  76.5 0.6 collective-permute-start.7
  77.1 1.5 %collective-permute-start.5 = (bf16[64,1024]{1,0:T(8,128)(2,1)S(1)}, bf16[64,1024]{1,0:T(8,128)(2,1)S(1)}, u32[]{:S(2)}, u32[]{:S(2)}) collective-permute-start(bf16[64,1024]{1,0:T(8,128)(2,1)S(1)} %get-tuple-element.42), channel_id=1, source_target_pairs={{0,24},{8,16},{16,8},{24,0},{1,25},{9,17},{17,9},{25,1},{2,26},{10... | collective-permute-start | bytes 393224 | tf_op jit(solution)/shard_map/ppermute | solution.py:321
  78.6 0.0 collective-permute-done.10.refs_8_
  78.6 0.5 collective-permute-start.12
  79.1 0.0 collective-permute-done.6.refs_4_
  79.1 1.5 %collective-permute-start.8 = (bf16[64,1024]{1,0:T(8,128)(2,1)S(1)}, bf16[64,1024]{1,0:T(8,128)(2,1)S(1)}, u32[]{:S(2)}, u32[]{:S(2)}) collective-permute-start(bf16[64,1024]{1,0:T(8,128)(2,1)S(1)} %collective-permute-done.4.refs_2_), channel_id=1, source_target_pairs={{0,2},{2,0},{4,6},{6,4},{1,3},{3,1},{5,7},{7,5},{8,10},{10,8},{12,... | collective-permute-start | bytes 393224 | tf_op jit(solution)/shard_map/ppermute | solution.py:321
  80.6 0.0 collective-permute-done.11.refs_9_
  80.6 0.5 collective-permute-start.15
  81.2 1.2 %collective-permute-done.7.refs_5_ = bf16[64,1024]{1,0:T(8,128)(2,1)S(1)} collective-permute-done((bf16[64,1024]{1,0:T(8,128)(2,1)S(1)}, bf16[64,1024]{1,0:T(8,128)(2,1)S(1)}, u32[]{:S(2)}, u32[]{:S(2)}) %collective-permute-start.7) | collective-permute-done | bytes 131104 | tf_op jit(solution)/shard_map/ppermute | solution.py:321
  82.4 0.7 collective-permute-start.14
  83.1 0.8 collective-permute-done.5.refs_3_
  83.9 1.4 %collective-permute-start.17 = (bf16[64,1024]{1,0:T(8,128)(2,1)S(1)}, bf16[64,1024]{1,0:T(8,128)(2,1)S(1)}, u32[]{:S(2)}, u32[]{:S(2)}) collective-permute-start(bf16[64,1024]{1,0:T(8,128)(2,1)S(1)} %collective-permute-done.5.refs_3_), channel_id=1, source_target_pairs={{0,6},{2,4},{4,2},{6,0},{1,7},{3,5},{5,3},{7,1},{8,14},{10,12},{12... | collective-permute-start | bytes 393224 | tf_op jit(solution)/shard_map/ppermute | solution.py:321
  85.3 0.1 collective-permute-done.12.refs_10_
  85.4 1.4 %collective-permute-start.13 = (bf16[64,1024]{1,0:T(8,128)(2,1)S(1)}, bf16[64,1024]{1,0:T(8,128)(2,1)S(1)}, u32[]{:S(2)}, u32[]{:S(2)}) collective-permute-start(bf16[64,1024]{1,0:T(8,128)(2,1)S(1)} %collective-permute-done.5.refs_3_), channel_id=1, source_target_pairs={{0,4},{2,6},{4,0},{6,2},{1,5},{3,7},{5,1},{7,3},{8,12},{10,14},{12... | collective-permute-start | bytes 393224 | tf_op jit(solution)/shard_map/ppermute | solution.py:321
  86.7 0.0 collective-permute-done.8.refs_6_
  86.7 0.6 collective-permute-start.9
  87.4 0.9 collective-permute-done.15.refs_13_
  88.3 0.9 collective-permute-start.16
  89.2 0.5 shard_map.113.refs_16_
  89.7 0.0 copy-start.1
  89.7 0.0 copy-start.3
  89.7 0.0 copy-start.4
  89.7 0.0 copy-start.5
  89.8 0.4 collective-permute-done.14.refs_12_
  90.2 0.0 collective-permute-done.17.refs_15_
  90.2 1.8 %collective-permute-done.13.refs_11_ = bf16[64,1024]{1,0:T(8,128)(2,1)S(1)} collective-permute-done((bf16[64,1024]{1,0:T(8,128)(2,1)S(1)}, bf16[64,1024]{1,0:T(8,128)(2,1)S(1)}, u32[]{:S(2)}, u32[]{:S(2)}) %collective-permute-start.13) | collective-permute-done | bytes 131104 | tf_op jit(solution)/shard_map/ppermute | solution.py:321
  92.0 0.0 collective-permute-done.9.refs_7_
  92.0 1.4 %collective-permute-done.16.refs_14_ = bf16[64,1024]{1,0:T(8,128)(2,1)S(1)} collective-permute-done((bf16[64,1024]{1,0:T(8,128)(2,1)S(1)}, bf16[64,1024]{1,0:T(8,128)(2,1)S(1)}, u32[]{:S(2)}, u32[]{:S(2)}) %collective-permute-start.16) | collective-permute-done | bytes 131104 | tf_op jit(solution)/shard_map/ppermute | solution.py:321
  93.4 8.1 %shard_map.114 = (bf16[64,1024]{1,0:T(8,128)(2,1)S(1)}, bf16[64,1024]{1,0:T(8,128)(2,1)S(1)}, bf16[64,1024]{1,0:T(8,128)(2,1)S(1)}, bf16[64,1024]{1,0:T(8,128)(2,1)S(1)}) custom-call(bf16[64,1024]{1,0:T(8,128)(2,1)S(1)} %get-tuple-element.38.refs_0_, bf16[64,1024]{1,0:T(8,128)(2,1)S(1)} %collective-permute-done.3.refs_1_, ...), custom_call_target="tpu_custom_call" | custom-call | tf_op jit(solution)/shard_map/pallas_call | solution.py:125
  101.6 2.4 %collective-permute-start.18 = (bf16[64,1024]{1,0:T(8,128)(2,1)S(1)}, bf16[64,1024]{1,0:T(8,128)(2,1)S(1)}, u32[]{:S(2)}, u32[]{:S(2)}) collective-permute-start(bf16[64,1024]{1,0:T(8,128)(2,1)S(1)} %get-tuple-element.48), channel_id=1, source_target_pairs={{0,24},{8,16},{16,8},{24,0},{1,25},{9,17},{17,9},{25,1},{2,26},{10... | collective-permute-start | bytes 393224 | tf_op jit(solution)/shard_map/ppermute | solution.py:321
  103.9 0.8 collective-permute-start.19
  104.7 1.3 %collective-permute-start.20 = (bf16[64,1024]{1,0:T(8,128)(2,1)S(1)}, bf16[64,1024]{1,0:T(8,128)(2,1)S(1)}, u32[]{:S(2)}, u32[]{:S(2)}) collective-permute-start(bf16[64,1024]{1,0:T(8,128)(2,1)S(1)} %get-tuple-element.50), channel_id=1, source_target_pairs={{0,8},{8,0},{16,24},{24,16},{1,9},{9,1},{17,25},{25,17},{2,10},{10... | collective-permute-start | bytes 393224 | tf_op jit(solution)/shard_map/ppermute | solution.py:321
  106.0 0.0 copy-done.1
  106.0 1.3 %shard_map.116 = (bf16[4,64,1024]{2,1,0:T(8,128)(2,1)}, bf16[4,64,1024]{2,1,0:T(8,128)(2,1)}) custom-call(s32[5]{0:T(128)S(1)} %compare_select_fusion.place_ref, bf16[64,1024]{1,0:T(8,128)(2,1)S(1)} %get-tuple-element.44.refs_0_, bf16[4,64,1024]{2,1,0:T(8,128)(2,1)S(1)} %bitcast.16), custom_call_target="tpu_custom_call" | custom-call | tf_op jit(solution)/shard_map/pallas_call | solution.py:264
  107.3 0.0 copy-done.3
  107.3 0.0 copy-done.4
  107.3 1.8 %shard_map.115 = (f32[4,64,1024]{2,1,0:T(8,128)}, f32[4,64]{1,0:T(4,128)}, f32[4,64]{1,0:T(4,128)}) custom-call(s32[5]{0:T(128)S(1)} %compare_select_fusion.place_ref, f32[8,128]{1,0:T(8,128)S(1)} %get-tuple-element.45.clip_ref, f32[4,64,1024]{2,1,0:T(8,128)S(1)} %get-tuple-element.36.grad_ref, f32[4,64,1024]{2,1,0:T(8,128)S(1)} %bitcast.15, ...), custom_call_target="tpu_custom_call" | custom-call | tf_op jit(solution)/shard_map/pallas_call | solution.py:310
  109.2 0.3 collective-permute-done.18.refs_0_
  109.5 5.4 %collective-permute-done.19.refs_1_ = bf16[64,1024]{1,0:T(8,128)(2,1)S(1)} collective-permute-done((bf16[64,1024]{1,0:T(8,128)(2,1)S(1)}, bf16[64,1024]{1,0:T(8,128)(2,1)S(1)}, u32[]{:S(2)}, u32[]{:S(2)}) %collective-permute-start.19) | collective-permute-done | bytes 131104 | tf_op jit(solution)/shard_map/ppermute | solution.py:321
  115.0 0.0 collective-permute-done.20.refs_2_
  115.0 1.5 %shard_map.117 = (bf16[4,64,1024]{2,1,0:T(8,128)(2,1)}, bf16[4,64,1024]{2,1,0:T(8,128)(2,1)}) custom-call(s32[5]{0:T(128)S(1)} %compare_select_fusion.place_ref, bf16[64,1024]{1,0:T(8,128)(2,1)S(1)} %collective-permute-done.18.refs_0_, bf16[64,1024]{1,0:T(8,128)(2,1)S(1)} %collective-permute-done.19.refs_1_, ...), custom_call_target="tpu_custom_call", output_to_operand_aliasing={{0}: (5, {}), {1}: (6, {})} | custom-call | tf_op jit(solution)/shard_map/pallas_call | solution.py:264
  (4 shorter events, 0.0 us)
Async XLA Ops:
  0.6 52.5 %copy-start = (f32[1,4,64,1024]{3,2,1,0:T(8,128)S(1)}, f32[1,4,64,1024]{3,2,1,0:T(8,128)}, u32[]{:S(2)}) copy-start(f32[1,4,64,1024]{3,2,1,0:T(8,128)} %param.9) | copy-start | bytes 3145732
  0.7 1.7 %copy-start.2 = (bf16[1,1,4,256,1024]{4,3,2,1,0:T(8,128)(2,1)S(1)}, bf16[1,1,4,256,1024]{4,3,2,1,0:T(8,128)(2,1)}, u32[]{:S(2)}) copy-start(bf16[1,1,4,256,1024]{4,3,2,1,0:T(8,128)(2,1)} %param.7) | copy-start | bytes 6291460
  2.3 6.5 %copy-start.6 = (bf16[1,1,4,256]{3,2,1,0:T(4,128)(2,1)S(1)}, bf16[1,1,4,256]{3,2,1,0:T(4,128)(2,1)}, u32[]{:S(2)}) copy-start(bf16[1,1,4,256]{3,2,1,0:T(4,128)(2,1)} %param.8) | copy-start | bytes 6148
  3.1 50.1 %collective-permute-start = (bf16[4,64,1024]{2,1,0:T(8,128)(2,1)S(1)}, bf16[4,64,1024]{2,1,0:T(8,128)(2,1)S(1)}, u32[]{:S(2)}, u32[]{:S(2)}) collective-permute-start(bf16[4,64,1024]{2,1,0:T(8,128)(2,1)S(1)} %get-tuple-element.31), channel_id=1, source_target_pairs={{0,24},{8,16},{16,8},{24,0},{1,25},{9,17},{17,9},{25,1},{2,26},{10... | collective-permute-start | bytes 1572872 | tf_op jit(solution)/shard_map/ppermute | solution.py:321
  8.2 45.0 %collective-permute-start.1 = (bf16[4,64,1024]{2,1,0:T(8,128)(2,1)S(1)}, bf16[4,64,1024]{2,1,0:T(8,128)(2,1)S(1)}, u32[]{:S(2)}, u32[]{:S(2)}) collective-permute-start(bf16[4,64,1024]{2,1,0:T(8,128)(2,1)S(1)} %get-tuple-element.32), channel_id=1, source_target_pairs={{0,16},{8,24},{16,0},{24,8},{1,17},{9,25},{17,1},{25,9},{2,18},{10... | collective-permute-start | bytes 1572872 | tf_op jit(solution)/shard_map/ppermute | solution.py:321
  8.2 45.0 %collective-permute-start.2 = (bf16[4,64,1024]{2,1,0:T(8,128)(2,1)S(1)}, bf16[4,64,1024]{2,1,0:T(8,128)(2,1)S(1)}, u32[]{:S(2)}, u32[]{:S(2)}) collective-permute-start(bf16[4,64,1024]{2,1,0:T(8,128)(2,1)S(1)} %get-tuple-element.33), channel_id=1, source_target_pairs={{0,8},{8,0},{16,24},{24,16},{1,9},{9,1},{17,25},{25,17},{2,10},{10... | collective-permute-start | bytes 1572872 | tf_op jit(solution)/shard_map/ppermute | solution.py:321
  67.2 6.9 %collective-permute-start.3 = (bf16[64,1024]{1,0:T(8,128)(2,1)S(1)}, bf16[64,1024]{1,0:T(8,128)(2,1)S(1)}, u32[]{:S(2)}, u32[]{:S(2)}) collective-permute-start(bf16[64,1024]{1,0:T(8,128)(2,1)S(1)} %get-tuple-element.39), channel_id=1, source_target_pairs={{0,8},{8,0},{16,24},{24,16},{1,9},{9,1},{17,25},{25,17},{2,10},{10... | collective-permute-start | bytes 393224 | tf_op jit(solution)/shard_map/ppermute | solution.py:321
  67.9 8.6 %collective-permute-start.4 = (bf16[64,1024]{1,0:T(8,128)(2,1)S(1)}, bf16[64,1024]{1,0:T(8,128)(2,1)S(1)}, u32[]{:S(2)}, u32[]{:S(2)}) collective-permute-start(bf16[64,1024]{1,0:T(8,128)(2,1)S(1)} %get-tuple-element.40), channel_id=1, source_target_pairs={{0,16},{8,24},{16,0},{24,8},{1,17},{9,25},{17,1},{25,9},{2,18},{10... | collective-permute-start | bytes 393224 | tf_op jit(solution)/shard_map/ppermute | solution.py:321
  68.4 10.2 %collective-permute-start.10 = (bf16[64,1024]{1,0:T(8,128)(2,1)S(1)}, bf16[64,1024]{1,0:T(8,128)(2,1)S(1)}, u32[]{:S(2)}, u32[]{:S(2)}) collective-permute-start(bf16[64,1024]{1,0:T(8,128)(2,1)S(1)} %get-tuple-element.38.refs_0_), channel_id=1, source_target_pairs={{0,4},{2,6},{4,0},{6,2},{1,5},{3,7},{5,1},{7,3},{8,12},{10,14},{12... | collective-permute-start | bytes 393224 | tf_op jit(solution)/shard_map/ppermute | solution.py:321
  69.0 10.2 %collective-permute-start.6 = (bf16[64,1024]{1,0:T(8,128)(2,1)S(1)}, bf16[64,1024]{1,0:T(8,128)(2,1)S(1)}, u32[]{:S(2)}, u32[]{:S(2)}) collective-permute-start(bf16[64,1024]{1,0:T(8,128)(2,1)S(1)} %get-tuple-element.38.refs_0_), channel_id=1, source_target_pairs={{0,2},{2,0},{4,6},{6,4},{1,3},{3,1},{5,7},{7,5},{8,10},{10,8},{12,... | collective-permute-start | bytes 393224 | tf_op jit(solution)/shard_map/ppermute | solution.py:321
  74.2 6.5 %collective-permute-start.11 = (bf16[64,1024]{1,0:T(8,128)(2,1)S(1)}, bf16[64,1024]{1,0:T(8,128)(2,1)S(1)}, u32[]{:S(2)}, u32[]{:S(2)}) collective-permute-start(bf16[64,1024]{1,0:T(8,128)(2,1)S(1)} %collective-permute-done.3.refs_1_), channel_id=1, source_target_pairs={{0,4},{2,6},{4,0},{6,2},{1,5},{3,7},{5,1},{7,3},{8,12},{10,14},{12... | collective-permute-start | bytes 393224 | tf_op jit(solution)/shard_map/ppermute | solution.py:321
  76.5 5.9 %collective-permute-start.7 = (bf16[64,1024]{1,0:T(8,128)(2,1)S(1)}, bf16[64,1024]{1,0:T(8,128)(2,1)S(1)}, u32[]{:S(2)}, u32[]{:S(2)}) collective-permute-start(bf16[64,1024]{1,0:T(8,128)(2,1)S(1)} %collective-permute-done.3.refs_1_), channel_id=1, source_target_pairs={{0,2},{2,0},{4,6},{6,4},{1,3},{3,1},{5,7},{7,5},{8,10},{10,8},{12,... | collective-permute-start | bytes 393224 | tf_op jit(solution)/shard_map/ppermute | solution.py:321
  77.1 6.8 %collective-permute-start.5 = (bf16[64,1024]{1,0:T(8,128)(2,1)S(1)}, bf16[64,1024]{1,0:T(8,128)(2,1)S(1)}, u32[]{:S(2)}, u32[]{:S(2)}) collective-permute-start(bf16[64,1024]{1,0:T(8,128)(2,1)S(1)} %get-tuple-element.42), channel_id=1, source_target_pairs={{0,24},{8,16},{16,8},{24,0},{1,25},{9,17},{17,9},{25,1},{2,26},{10... | collective-permute-start | bytes 393224 | tf_op jit(solution)/shard_map/ppermute | solution.py:321
  78.6 6.8 %collective-permute-start.12 = (bf16[64,1024]{1,0:T(8,128)(2,1)S(1)}, bf16[64,1024]{1,0:T(8,128)(2,1)S(1)}, u32[]{:S(2)}, u32[]{:S(2)}) collective-permute-start(bf16[64,1024]{1,0:T(8,128)(2,1)S(1)} %collective-permute-done.4.refs_2_), channel_id=1, source_target_pairs={{0,4},{2,6},{4,0},{6,2},{1,5},{3,7},{5,1},{7,3},{8,12},{10,14},{12... | collective-permute-start | bytes 393224 | tf_op jit(solution)/shard_map/ppermute | solution.py:321
  79.1 7.6 %collective-permute-start.8 = (bf16[64,1024]{1,0:T(8,128)(2,1)S(1)}, bf16[64,1024]{1,0:T(8,128)(2,1)S(1)}, u32[]{:S(2)}, u32[]{:S(2)}) collective-permute-start(bf16[64,1024]{1,0:T(8,128)(2,1)S(1)} %collective-permute-done.4.refs_2_), channel_id=1, source_target_pairs={{0,2},{2,0},{4,6},{6,4},{1,3},{3,1},{5,7},{7,5},{8,10},{10,8},{12,... | collective-permute-start | bytes 393224 | tf_op jit(solution)/shard_map/ppermute | solution.py:321
  80.6 7.7 %collective-permute-start.15 = (bf16[64,1024]{1,0:T(8,128)(2,1)S(1)}, bf16[64,1024]{1,0:T(8,128)(2,1)S(1)}, u32[]{:S(2)}, u32[]{:S(2)}) collective-permute-start(bf16[64,1024]{1,0:T(8,128)(2,1)S(1)} %collective-permute-done.11.refs_9_), channel_id=1, source_target_pairs={{0,2},{2,0},{4,6},{6,4},{1,3},{3,1},{5,7},{7,5},{8,10},{10,8},{12,... | collective-permute-start | bytes 393224 | tf_op jit(solution)/shard_map/ppermute | solution.py:321
  82.4 7.8 %collective-permute-start.14 = (bf16[64,1024]{1,0:T(8,128)(2,1)S(1)}, bf16[64,1024]{1,0:T(8,128)(2,1)S(1)}, u32[]{:S(2)}, u32[]{:S(2)}) collective-permute-start(bf16[64,1024]{1,0:T(8,128)(2,1)S(1)} %collective-permute-done.6.refs_4_), channel_id=1, source_target_pairs={{0,4},{2,6},{4,0},{6,2},{1,5},{3,7},{5,1},{7,3},{8,12},{10,14},{12... | collective-permute-start | bytes 393224 | tf_op jit(solution)/shard_map/ppermute | solution.py:321
  83.9 6.3 %collective-permute-start.17 = (bf16[64,1024]{1,0:T(8,128)(2,1)S(1)}, bf16[64,1024]{1,0:T(8,128)(2,1)S(1)}, u32[]{:S(2)}, u32[]{:S(2)}) collective-permute-start(bf16[64,1024]{1,0:T(8,128)(2,1)S(1)} %collective-permute-done.5.refs_3_), channel_id=1, source_target_pairs={{0,6},{2,4},{4,2},{6,0},{1,7},{3,5},{5,3},{7,1},{8,14},{10,12},{12... | collective-permute-start | bytes 393224 | tf_op jit(solution)/shard_map/ppermute | solution.py:321
  85.4 6.6 %collective-permute-start.13 = (bf16[64,1024]{1,0:T(8,128)(2,1)S(1)}, bf16[64,1024]{1,0:T(8,128)(2,1)S(1)}, u32[]{:S(2)}, u32[]{:S(2)}) collective-permute-start(bf16[64,1024]{1,0:T(8,128)(2,1)S(1)} %collective-permute-done.5.refs_3_), channel_id=1, source_target_pairs={{0,4},{2,6},{4,0},{6,2},{1,5},{3,7},{5,1},{7,3},{8,12},{10,14},{12... | collective-permute-start | bytes 393224 | tf_op jit(solution)/shard_map/ppermute | solution.py:321
  86.7 5.3 %collective-permute-start.9 = (bf16[64,1024]{1,0:T(8,128)(2,1)S(1)}, bf16[64,1024]{1,0:T(8,128)(2,1)S(1)}, u32[]{:S(2)}, u32[]{:S(2)}) collective-permute-start(bf16[64,1024]{1,0:T(8,128)(2,1)S(1)} %collective-permute-done.5.refs_3_), channel_id=1, source_target_pairs={{0,2},{2,0},{4,6},{6,4},{1,3},{3,1},{5,7},{7,5},{8,10},{10,8},{12,... | collective-permute-start | bytes 393224 | tf_op jit(solution)/shard_map/ppermute | solution.py:321
  88.3 5.1 %collective-permute-start.16 = (bf16[64,1024]{1,0:T(8,128)(2,1)S(1)}, bf16[64,1024]{1,0:T(8,128)(2,1)S(1)}, u32[]{:S(2)}, u32[]{:S(2)}) collective-permute-start(bf16[64,1024]{1,0:T(8,128)(2,1)S(1)} %collective-permute-done.8.refs_6_), channel_id=1, source_target_pairs={{0,4},{2,6},{4,0},{6,2},{1,5},{3,7},{5,1},{7,3},{8,12},{10,14},{12... | collective-permute-start | bytes 393224 | tf_op jit(solution)/shard_map/ppermute | solution.py:321
  89.7 16.3 %copy-start.1 = (bf16[1,4,64,1024]{3,2,1,0:T(8,128)(2,1)S(1)}, bf16[1,4,64,1024]{3,2,1,0:T(8,128)(2,1)}, u32[]{:S(2)}) copy-start(bf16[1,4,64,1024]{3,2,1,0:T(8,128)(2,1)} %param.10) | copy-start | bytes 1572868
  89.7 17.6 %copy-start.3 = (f32[1,4,64]{2,1,0:T(4,128)S(1)}, f32[1,4,64]{2,1,0:T(4,128)}, u32[]{:S(2)}) copy-start(f32[1,4,64]{2,1,0:T(4,128)} %param.11) | copy-start | bytes 3076
  89.7 17.6 %copy-start.4 = (f32[1,4,64]{2,1,0:T(4,128)S(1)}, f32[1,4,64]{2,1,0:T(4,128)}, u32[]{:S(2)}) copy-start(f32[1,4,64]{2,1,0:T(4,128)} %param.12) | copy-start | bytes 3076
  89.7 17.6 %copy-start.5 = (f32[1,4,64]{2,1,0:T(4,128)S(1)}, f32[1,4,64]{2,1,0:T(4,128)}, u32[]{:S(2)}) copy-start(f32[1,4,64]{2,1,0:T(4,128)} %param.13) | copy-start | bytes 3076
  101.6 7.9 %collective-permute-start.18 = (bf16[64,1024]{1,0:T(8,128)(2,1)S(1)}, bf16[64,1024]{1,0:T(8,128)(2,1)S(1)}, u32[]{:S(2)}, u32[]{:S(2)}) collective-permute-start(bf16[64,1024]{1,0:T(8,128)(2,1)S(1)} %get-tuple-element.48), channel_id=1, source_target_pairs={{0,24},{8,16},{16,8},{24,0},{1,25},{9,17},{17,9},{25,1},{2,26},{10... | collective-permute-start | bytes 393224 | tf_op jit(solution)/shard_map/ppermute | solution.py:321
  103.9 11.0 %collective-permute-start.19 = (bf16[64,1024]{1,0:T(8,128)(2,1)S(1)}, bf16[64,1024]{1,0:T(8,128)(2,1)S(1)}, u32[]{:S(2)}, u32[]{:S(2)}) collective-permute-start(bf16[64,1024]{1,0:T(8,128)(2,1)S(1)} %get-tuple-element.49), channel_id=1, source_target_pairs={{0,16},{8,24},{16,0},{24,8},{1,17},{9,25},{17,1},{25,9},{2,18},{10... | collective-permute-start | bytes 393224 | tf_op jit(solution)/shard_map/ppermute | solution.py:321
  104.7 10.2 %collective-permute-start.20 = (bf16[64,1024]{1,0:T(8,128)(2,1)S(1)}, bf16[64,1024]{1,0:T(8,128)(2,1)S(1)}, u32[]{:S(2)}, u32[]{:S(2)}) collective-permute-start(bf16[64,1024]{1,0:T(8,128)(2,1)S(1)} %get-tuple-element.50), channel_id=1, source_target_pairs={{0,8},{8,0},{16,24},{24,16},{1,9},{9,1},{17,25},{25,17},{2,10},{10... | collective-permute-start | bytes 393224 | tf_op jit(solution)/shard_map/ppermute | solution.py:321

commit v7 on v6

--- a/solution.py
+++ b/solution.py
@@ -32,16 +32,13 @@
 def gram_of(blocks, gram_ref, ready_ref=None):
     width = blocks[0].shape[1]
     step = 256
+    turned = [block[...].T for block in blocks]
     for start in range(0, width, step):
         stop = start + step
         total = None if ready_ref is None else ready_ref[:stop, start:stop].astype(jnp.float32)
-        for block in blocks:
-            whole = block[...]
-            product = lax.dot_general(
-                whole[:, :stop],
-                whole[:, start:stop],
-                (((0,), (0,)), ((), ())),
-                preferred_element_type=jnp.float32,
+        for block, columns in zip(blocks, turned):
+            product = jnp.dot(
+                columns[:stop], block[:, start:stop], preferred_element_type=jnp.float32
             )
             rounded = product.astype(jnp.bfloat16).astype(jnp.float32)
             total = rounded if total is None else total + rounded

time: 117 us -> 117 us (level)
  no operation moved by 1% of the time
where the time goes in v7:
time: 117 us; the launch traced here: 116 us
  blocking collectives  56 us (48%)
  starting transfers between devices  22.8 us (19%)
  waiting for transfers between devices  18.8 us (16%)
  Pallas kernels  16.3 us (14%)
  local copies, waits for them, and re-layouts  1.71 us (1%)
    all_to_all x1, blocking collectives, per_device(): lax.all_to_all(jnp.broadcast_to(vector_grads[0], (shard_count, vector_cou...  44.3 us
    ppermute x21, starting transfers between devices, swapped(): return lax.ppermute(array, axis, pairs)  22.8 us
    ppermute x21, waiting for transfers between devices, swapped(): return lax.ppermute(array, axis, pairs)  18.8 us
    all_to_all x1, blocking collectives, per_device(): lax.all_to_all(figures.reshape(others * section_count, 1, LANES), MESH_AX...  11.7 us
    pallas_call x1, Pallas kernels, orthogonalize(): pl.pallas_call(functools.partial(orthogonalize_kernel, count, pieces), ou...  8.13 us
    pallas_call x3, Pallas kernels, on_device(): pl.pallas_call(kernel, out_shape=out_shape, in_specs=[pl.BlockSpec(memory...  4.2 us
    pallas_call x2, Pallas kernels, finished(): pl.pallas_call(functools.partial(end_kernel, offsets), out_shape=[jax.Sha...  2.74 us
  transfers between devices with their start and end apart: 21, of which 11 were waited for; matrix products, arithmetic and copies ran while one was open for 0% of the time, Pallas kernels for 3%

profile of v7, /device:TPU:0, one launch (start us, length us, event | category | flops | bytes accessed | tf_op | source)
XLA Modules:
  0.0 116.4 jit_solution(8407958645657490730)
XLA Ops:
  0.6 0.0 copy-start
  0.7 0.0 copy-start.2
  0.7 1.7 %copy-done.2 = bf16[1,1,4,256,1024]{4,3,2,1,0:T(8,128)(2,1)S(1)} copy-done((bf16[1,1,4,256,1024]{4,3,2,1,0:T(8,128)(2,1)S(1)}, bf16[1,1,4,256,1024]{4,3,2,1,0:T(8,128)(2,1)}, u32[]{:S(2)}) %copy-start.2) | copy-done | bytes 2097176
  2.3 0.7 shard_map.110
  3.1 5.1 %collective-permute-start = (bf16[4,64,1024]{2,1,0:T(8,128)(2,1)S(1)}, bf16[4,64,1024]{2,1,0:T(8,128)(2,1)S(1)}, u32[]{:S(2)}, u32[]{:S(2)}) collective-permute-start(bf16[4,64,1024]{2,1,0:T(8,128)(2,1)S(1)} %get-tuple-element.31), channel_id=1, source_target_pairs={{0,24},{8,16},{16,8},{24,0},{1,25},{9,17},{17,9},{25,1},{2,26},{10... | collective-permute-start | bytes 1572872 | tf_op jit(solution)/shard_map/ppermute | solution.py:318
  8.2 0.0 collective-permute-start.1
  8.2 0.6 collective-permute-start.2
  8.8 0.0 copy-done.6
  8.8 44.3 %all_to_all.10.refs_4_ = bf16[4,4,256]{2,1,0:T(4,128)(2,1)S(1)} all-to-all(bf16[4,4,256]{2,1,0:T(4,128)(2,1)S(1)} %broadcast_in_dim.28), channel_id=1, replica_groups=mesh['shard'=4,'tensor'=4,'section'=2] {'shard'}, dimensions={0} | all-to-all | bytes 16384 | tf_op jit(solution)/shard_map/all_to_all | solution.py:347
  53.1 0.0 collective-permute-done.refs_0_
  53.2 0.0 collective-permute-done.1.refs_1_
  53.2 0.0 collective-permute-done.2.refs_2_
  53.2 0.0 copy-done
  53.2 1.3 %shard_map.111 = (f32[4,64,1024]{2,1,0:T(8,128)S(1)}, f32[4,256]{1,0:T(4,128)S(1)}, f32[16,2,1,128]{3,2,1,0:T(1,128)S(1)}) custom-call(s32[5]{0:T(128)S(1)} %compare_select_fusion.place_ref, bf16[4,64,1024]{2,1,0:T(8,128)(2,1)S(1)} %collective-permute-done.refs_0_, bf16[4,64,1024]{2,1,0:T(8,128)(2,1)S(1)} %collective-permute-done.1.refs_1_, ...), custom_call_target="tpu_custom_call" | custom-call | tf_op jit(solution)/shard_map/pallas_call | solution.py:307
  54.5 11.7 %all_to_all.11.figures_ref = f32[32,1,128]{2,1,0:T(1,128)S(1)} all-to-all(f32[32,1,128]{2,1,0:T(1,128)S(1)} %bitcast.19), channel_id=1, replica_groups=mesh['shard'=4,'tensor'=4,'section'=2] {'shard','tensor','section'}, dimensions={0} | all-to-all | bytes 32768 | tf_op jit(solution)/shard_map/all_to_all | solution.py:366
  66.2 1.0 shard_map.112
  67.2 0.6 collective-permute-start.3
  67.9 0.6 collective-permute-start.4
  68.4 0.5 collective-permute-start.10
  69.0 0.6 collective-permute-start.6
  69.5 4.6 %collective-permute-done.3.refs_1_ = bf16[64,1024]{1,0:T(8,128)(2,1)S(1)} collective-permute-done((bf16[64,1024]{1,0:T(8,128)(2,1)S(1)}, bf16[64,1024]{1,0:T(8,128)(2,1)S(1)}, u32[]{:S(2)}, u32[]{:S(2)}) %collective-permute-start.3) | collective-permute-done | bytes 131104 | tf_op jit(solution)/shard_map/ppermute | solution.py:318
  74.2 0.5 collective-permute-start.11
  74.7 1.8 %collective-permute-done.4.refs_2_ = bf16[64,1024]{1,0:T(8,128)(2,1)S(1)} collective-permute-done((bf16[64,1024]{1,0:T(8,128)(2,1)S(1)}, bf16[64,1024]{1,0:T(8,128)(2,1)S(1)}, u32[]{:S(2)}, u32[]{:S(2)}) %collective-permute-start.4) | collective-permute-done | bytes 131104 | tf_op jit(solution)/shard_map/ppermute | solution.py:318
  76.5 0.6 collective-permute-start.7
  77.1 1.5 %collective-permute-start.5 = (bf16[64,1024]{1,0:T(8,128)(2,1)S(1)}, bf16[64,1024]{1,0:T(8,128)(2,1)S(1)}, u32[]{:S(2)}, u32[]{:S(2)}) collective-permute-start(bf16[64,1024]{1,0:T(8,128)(2,1)S(1)} %get-tuple-element.42), channel_id=1, source_target_pairs={{0,24},{8,16},{16,8},{24,0},{1,25},{9,17},{17,9},{25,1},{2,26},{10... | collective-permute-start | bytes 393224 | tf_op jit(solution)/shard_map/ppermute | solution.py:318
  78.6 0.0 collective-permute-done.10.refs_8_
  78.6 0.5 collective-permute-start.12
  79.1 0.0 collective-permute-done.6.refs_4_
  79.1 1.5 %collective-permute-start.8 = (bf16[64,1024]{1,0:T(8,128)(2,1)S(1)}, bf16[64,1024]{1,0:T(8,128)(2,1)S(1)}, u32[]{:S(2)}, u32[]{:S(2)}) collective-permute-start(bf16[64,1024]{1,0:T(8,128)(2,1)S(1)} %collective-permute-done.4.refs_2_), channel_id=1, source_target_pairs={{0,2},{2,0},{4,6},{6,4},{1,3},{3,1},{5,7},{7,5},{8,10},{10,8},{12,... | collective-permute-start | bytes 393224 | tf_op jit(solution)/shard_map/ppermute | solution.py:318
  80.6 0.0 collective-permute-done.11.refs_9_
  80.6 0.5 collective-permute-start.15
  81.2 1.2 %collective-permute-done.7.refs_5_ = bf16[64,1024]{1,0:T(8,128)(2,1)S(1)} collective-permute-done((bf16[64,1024]{1,0:T(8,128)(2,1)S(1)}, bf16[64,1024]{1,0:T(8,128)(2,1)S(1)}, u32[]{:S(2)}, u32[]{:S(2)}) %collective-permute-start.7) | collective-permute-done | bytes 131104 | tf_op jit(solution)/shard_map/ppermute | solution.py:318
  82.4 0.7 collective-permute-start.14
  83.1 0.8 collective-permute-done.5.refs_3_
  83.9 1.4 %collective-permute-start.17 = (bf16[64,1024]{1,0:T(8,128)(2,1)S(1)}, bf16[64,1024]{1,0:T(8,128)(2,1)S(1)}, u32[]{:S(2)}, u32[]{:S(2)}) collective-permute-start(bf16[64,1024]{1,0:T(8,128)(2,1)S(1)} %collective-permute-done.5.refs_3_), channel_id=1, source_target_pairs={{0,6},{2,4},{4,2},{6,0},{1,7},{3,5},{5,3},{7,1},{8,14},{10,12},{12... | collective-permute-start | bytes 393224 | tf_op jit(solution)/shard_map/ppermute | solution.py:318
  85.3 0.1 collective-permute-done.12.refs_10_
  85.4 1.4 %collective-permute-start.13 = (bf16[64,1024]{1,0:T(8,128)(2,1)S(1)}, bf16[64,1024]{1,0:T(8,128)(2,1)S(1)}, u32[]{:S(2)}, u32[]{:S(2)}) collective-permute-start(bf16[64,1024]{1,0:T(8,128)(2,1)S(1)} %collective-permute-done.5.refs_3_), channel_id=1, source_target_pairs={{0,4},{2,6},{4,0},{6,2},{1,5},{3,7},{5,1},{7,3},{8,12},{10,14},{12... | collective-permute-start | bytes 393224 | tf_op jit(solution)/shard_map/ppermute | solution.py:318
  86.7 0.0 collective-permute-done.8.refs_6_
  86.7 0.6 collective-permute-start.9
  87.4 0.9 collective-permute-done.15.refs_13_
  88.3 0.9 collective-permute-start.16
  89.2 0.5 shard_map.113.refs_16_
  89.7 0.0 copy-start.1
  89.7 0.0 copy-start.3
  89.7 0.0 copy-start.4
  89.7 0.0 copy-start.5
  89.8 0.4 collective-permute-done.14.refs_12_
  90.2 0.0 collective-permute-done.17.refs_15_
  90.2 1.8 %collective-permute-done.13.refs_11_ = bf16[64,1024]{1,0:T(8,128)(2,1)S(1)} collective-permute-done((bf16[64,1024]{1,0:T(8,128)(2,1)S(1)}, bf16[64,1024]{1,0:T(8,128)(2,1)S(1)}, u32[]{:S(2)}, u32[]{:S(2)}) %collective-permute-start.13) | collective-permute-done | bytes 131104 | tf_op jit(solution)/shard_map/ppermute | solution.py:318
  92.0 0.0 collective-permute-done.9.refs_7_
  92.0 1.4 %collective-permute-done.16.refs_14_ = bf16[64,1024]{1,0:T(8,128)(2,1)S(1)} collective-permute-done((bf16[64,1024]{1,0:T(8,128)(2,1)S(1)}, bf16[64,1024]{1,0:T(8,128)(2,1)S(1)}, u32[]{:S(2)}, u32[]{:S(2)}) %collective-permute-start.16) | collective-permute-done | bytes 131104 | tf_op jit(solution)/shard_map/ppermute | solution.py:318
  93.4 8.1 %shard_map.114 = (bf16[64,1024]{1,0:T(8,128)(2,1)S(1)}, bf16[64,1024]{1,0:T(8,128)(2,1)S(1)}, bf16[64,1024]{1,0:T(8,128)(2,1)S(1)}, bf16[64,1024]{1,0:T(8,128)(2,1)S(1)}) custom-call(bf16[64,1024]{1,0:T(8,128)(2,1)S(1)} %get-tuple-element.38.refs_0_, bf16[64,1024]{1,0:T(8,128)(2,1)S(1)} %collective-permute-done.3.refs_1_, ...), custom_call_target="tpu_custom_call" | custom-call | tf_op jit(solution)/shard_map/pallas_call | solution.py:122
  101.6 2.4 %collective-permute-start.18 = (bf16[64,1024]{1,0:T(8,128)(2,1)S(1)}, bf16[64,1024]{1,0:T(8,128)(2,1)S(1)}, u32[]{:S(2)}, u32[]{:S(2)}) collective-permute-start(bf16[64,1024]{1,0:T(8,128)(2,1)S(1)} %get-tuple-element.48), channel_id=1, source_target_pairs={{0,24},{8,16},{16,8},{24,0},{1,25},{9,17},{17,9},{25,1},{2,26},{10... | collective-permute-start | bytes 393224 | tf_op jit(solution)/shard_map/ppermute | solution.py:318
  103.9 0.8 collective-permute-start.19
  104.7 1.3 %collective-permute-start.20 = (bf16[64,1024]{1,0:T(8,128)(2,1)S(1)}, bf16[64,1024]{1,0:T(8,128)(2,1)S(1)}, u32[]{:S(2)}, u32[]{:S(2)}) collective-permute-start(bf16[64,1024]{1,0:T(8,128)(2,1)S(1)} %get-tuple-element.50), channel_id=1, source_target_pairs={{0,8},{8,0},{16,24},{24,16},{1,9},{9,1},{17,25},{25,17},{2,10},{10... | collective-permute-start | bytes 393224 | tf_op jit(solution)/shard_map/ppermute | solution.py:318
  106.0 0.0 copy-done.1
  106.0 1.3 %shard_map.116 = (bf16[4,64,1024]{2,1,0:T(8,128)(2,1)}, bf16[4,64,1024]{2,1,0:T(8,128)(2,1)}) custom-call(s32[5]{0:T(128)S(1)} %compare_select_fusion.place_ref, bf16[64,1024]{1,0:T(8,128)(2,1)S(1)} %get-tuple-element.44.refs_0_, bf16[4,64,1024]{2,1,0:T(8,128)(2,1)S(1)} %bitcast.16), custom_call_target="tpu_custom_call" | custom-call | tf_op jit(solution)/shard_map/pallas_call | solution.py:261
  107.3 0.0 copy-done.3
  107.3 0.0 copy-done.4
  107.3 1.8 %shard_map.115 = (f32[4,64,1024]{2,1,0:T(8,128)}, f32[4,64]{1,0:T(4,128)}, f32[4,64]{1,0:T(4,128)}) custom-call(s32[5]{0:T(128)S(1)} %compare_select_fusion.place_ref, f32[8,128]{1,0:T(8,128)S(1)} %get-tuple-element.45.clip_ref, f32[4,64,1024]{2,1,0:T(8,128)S(1)} %get-tuple-element.36.grad_ref, f32[4,64,1024]{2,1,0:T(8,128)S(1)} %bitcast.15, ...), custom_call_target="tpu_custom_call" | custom-call | tf_op jit(solution)/shard_map/pallas_call | solution.py:307
  109.2 0.4 collective-permute-done.18.refs_0_
  109.5 5.4 %collective-permute-done.19.refs_1_ = bf16[64,1024]{1,0:T(8,128)(2,1)S(1)} collective-permute-done((bf16[64,1024]{1,0:T(8,128)(2,1)S(1)}, bf16[64,1024]{1,0:T(8,128)(2,1)S(1)}, u32[]{:S(2)}, u32[]{:S(2)}) %collective-permute-start.19) | collective-permute-done | bytes 131104 | tf_op jit(solution)/shard_map/ppermute | solution.py:318
  115.0 0.0 collective-permute-done.20.refs_2_
  115.0 1.5 %shard_map.117 = (bf16[4,64,1024]{2,1,0:T(8,128)(2,1)}, bf16[4,64,1024]{2,1,0:T(8,128)(2,1)}) custom-call(s32[5]{0:T(128)S(1)} %compare_select_fusion.place_ref, bf16[64,1024]{1,0:T(8,128)(2,1)S(1)} %collective-permute-done.18.refs_0_, bf16[64,1024]{1,0:T(8,128)(2,1)S(1)} %collective-permute-done.19.refs_1_, ...), custom_call_target="tpu_custom_call", output_to_operand_aliasing={{0}: (5, {}), {1}: (6, {})} | custom-call | tf_op jit(solution)/shard_map/pallas_call | solution.py:261
  (4 shorter events, 0.0 us)
Async XLA Ops:
  0.6 52.5 %copy-start = (f32[1,4,64,1024]{3,2,1,0:T(8,128)S(1)}, f32[1,4,64,1024]{3,2,1,0:T(8,128)}, u32[]{:S(2)}) copy-start(f32[1,4,64,1024]{3,2,1,0:T(8,128)} %param.9) | copy-start | bytes 3145732
  0.7 1.7 %copy-start.2 = (bf16[1,1,4,256,1024]{4,3,2,1,0:T(8,128)(2,1)S(1)}, bf16[1,1,4,256,1024]{4,3,2,1,0:T(8,128)(2,1)}, u32[]{:S(2)}) copy-start(bf16[1,1,4,256,1024]{4,3,2,1,0:T(8,128)(2,1)} %param.7) | copy-start | bytes 6291460
  2.3 6.5 %copy-start.6 = (bf16[1,1,4,256]{3,2,1,0:T(4,128)(2,1)S(1)}, bf16[1,1,4,256]{3,2,1,0:T(4,128)(2,1)}, u32[]{:S(2)}) copy-start(bf16[1,1,4,256]{3,2,1,0:T(4,128)(2,1)} %param.8) | copy-start | bytes 6148
  3.1 50.1 %collective-permute-start = (bf16[4,64,1024]{2,1,0:T(8,128)(2,1)S(1)}, bf16[4,64,1024]{2,1,0:T(8,128)(2,1)S(1)}, u32[]{:S(2)}, u32[]{:S(2)}) collective-permute-start(bf16[4,64,1024]{2,1,0:T(8,128)(2,1)S(1)} %get-tuple-element.31), channel_id=1, source_target_pairs={{0,24},{8,16},{16,8},{24,0},{1,25},{9,17},{17,9},{25,1},{2,26},{10... | collective-permute-start | bytes 1572872 | tf_op jit(solution)/shard_map/ppermute | solution.py:318
  8.2 45.0 %collective-permute-start.1 = (bf16[4,64,1024]{2,1,0:T(8,128)(2,1)S(1)}, bf16[4,64,1024]{2,1,0:T(8,128)(2,1)S(1)}, u32[]{:S(2)}, u32[]{:S(2)}) collective-permute-start(bf16[4,64,1024]{2,1,0:T(8,128)(2,1)S(1)} %get-tuple-element.32), channel_id=1, source_target_pairs={{0,16},{8,24},{16,0},{24,8},{1,17},{9,25},{17,1},{25,9},{2,18},{10... | collective-permute-start | bytes 1572872 | tf_op jit(solution)/shard_map/ppermute | solution.py:318
  8.2 45.0 %collective-permute-start.2 = (bf16[4,64,1024]{2,1,0:T(8,128)(2,1)S(1)}, bf16[4,64,1024]{2,1,0:T(8,128)(2,1)S(1)}, u32[]{:S(2)}, u32[]{:S(2)}) collective-permute-start(bf16[4,64,1024]{2,1,0:T(8,128)(2,1)S(1)} %get-tuple-element.33), channel_id=1, source_target_pairs={{0,8},{8,0},{16,24},{24,16},{1,9},{9,1},{17,25},{25,17},{2,10},{10... | collective-permute-start | bytes 1572872 | tf_op jit(solution)/shard_map/ppermute | solution.py:318
  67.2 6.9 %collective-permute-start.3 = (bf16[64,1024]{1,0:T(8,128)(2,1)S(1)}, bf16[64,1024]{1,0:T(8,128)(2,1)S(1)}, u32[]{:S(2)}, u32[]{:S(2)}) collective-permute-start(bf16[64,1024]{1,0:T(8,128)(2,1)S(1)} %get-tuple-element.39), channel_id=1, source_target_pairs={{0,8},{8,0},{16,24},{24,16},{1,9},{9,1},{17,25},{25,17},{2,10},{10... | collective-permute-start | bytes 393224 | tf_op jit(solution)/shard_map/ppermute | solution.py:318
  67.9 8.6 %collective-permute-start.4 = (bf16[64,1024]{1,0:T(8,128)(2,1)S(1)}, bf16[64,1024]{1,0:T(8,128)(2,1)S(1)}, u32[]{:S(2)}, u32[]{:S(2)}) collective-permute-start(bf16[64,1024]{1,0:T(8,128)(2,1)S(1)} %get-tuple-element.40), channel_id=1, source_target_pairs={{0,16},{8,24},{16,0},{24,8},{1,17},{9,25},{17,1},{25,9},{2,18},{10... | collective-permute-start | bytes 393224 | tf_op jit(solution)/shard_map/ppermute | solution.py:318
  68.4 10.2 %collective-permute-start.10 = (bf16[64,1024]{1,0:T(8,128)(2,1)S(1)}, bf16[64,1024]{1,0:T(8,128)(2,1)S(1)}, u32[]{:S(2)}, u32[]{:S(2)}) collective-permute-start(bf16[64,1024]{1,0:T(8,128)(2,1)S(1)} %get-tuple-element.38.refs_0_), channel_id=1, source_target_pairs={{0,4},{2,6},{4,0},{6,2},{1,5},{3,7},{5,1},{7,3},{8,12},{10,14},{12... | collective-permute-start | bytes 393224 | tf_op jit(solution)/shard_map/ppermute | solution.py:318
  69.0 10.2 %collective-permute-start.6 = (bf16[64,1024]{1,0:T(8,128)(2,1)S(1)}, bf16[64,1024]{1,0:T(8,128)(2,1)S(1)}, u32[]{:S(2)}, u32[]{:S(2)}) collective-permute-start(bf16[64,1024]{1,0:T(8,128)(2,1)S(1)} %get-tuple-element.38.refs_0_), channel_id=1, source_target_pairs={{0,2},{2,0},{4,6},{6,4},{1,3},{3,1},{5,7},{7,5},{8,10},{10,8},{12,... | collective-permute-start | bytes 393224 | tf_op jit(solution)/shard_map/ppermute | solution.py:318
  74.2 6.5 %collective-permute-start.11 = (bf16[64,1024]{1,0:T(8,128)(2,1)S(1)}, bf16[64,1024]{1,0:T(8,128)(2,1)S(1)}, u32[]{:S(2)}, u32[]{:S(2)}) collective-permute-start(bf16[64,1024]{1,0:T(8,128)(2,1)S(1)} %collective-permute-done.3.refs_1_), channel_id=1, source_target_pairs={{0,4},{2,6},{4,0},{6,2},{1,5},{3,7},{5,1},{7,3},{8,12},{10,14},{12... | collective-permute-start | bytes 393224 | tf_op jit(solution)/shard_map/ppermute | solution.py:318
  76.5 5.9 %collective-permute-start.7 = (bf16[64,1024]{1,0:T(8,128)(2,1)S(1)}, bf16[64,1024]{1,0:T(8,128)(2,1)S(1)}, u32[]{:S(2)}, u32[]{:S(2)}) collective-permute-start(bf16[64,1024]{1,0:T(8,128)(2,1)S(1)} %collective-permute-done.3.refs_1_), channel_id=1, source_target_pairs={{0,2},{2,0},{4,6},{6,4},{1,3},{3,1},{5,7},{7,5},{8,10},{10,8},{12,... | collective-permute-start | bytes 393224 | tf_op jit(solution)/shard_map/ppermute | solution.py:318
  77.1 6.8 %collective-permute-start.5 = (bf16[64,1024]{1,0:T(8,128)(2,1)S(1)}, bf16[64,1024]{1,0:T(8,128)(2,1)S(1)}, u32[]{:S(2)}, u32[]{:S(2)}) collective-permute-start(bf16[64,1024]{1,0:T(8,128)(2,1)S(1)} %get-tuple-element.42), channel_id=1, source_target_pairs={{0,24},{8,16},{16,8},{24,0},{1,25},{9,17},{17,9},{25,1},{2,26},{10... | collective-permute-start | bytes 393224 | tf_op jit(solution)/shard_map/ppermute | solution.py:318
  78.6 6.8 %collective-permute-start.12 = (bf16[64,1024]{1,0:T(8,128)(2,1)S(1)}, bf16[64,1024]{1,0:T(8,128)(2,1)S(1)}, u32[]{:S(2)}, u32[]{:S(2)}) collective-permute-start(bf16[64,1024]{1,0:T(8,128)(2,1)S(1)} %collective-permute-done.4.refs_2_), channel_id=1, source_target_pairs={{0,4},{2,6},{4,0},{6,2},{1,5},{3,7},{5,1},{7,3},{8,12},{10,14},{12... | collective-permute-start | bytes 393224 | tf_op jit(solution)/shard_map/ppermute | solution.py:318
  79.1 7.6 %collective-permute-start.8 = (bf16[64,1024]{1,0:T(8,128)(2,1)S(1)}, bf16[64,1024]{1,0:T(8,128)(2,1)S(1)}, u32[]{:S(2)}, u32[]{:S(2)}) collective-permute-start(bf16[64,1024]{1,0:T(8,128)(2,1)S(1)} %collective-permute-done.4.refs_2_), channel_id=1, source_target_pairs={{0,2},{2,0},{4,6},{6,4},{1,3},{3,1},{5,7},{7,5},{8,10},{10,8},{12,... | collective-permute-start | bytes 393224 | tf_op jit(solution)/shard_map/ppermute | solution.py:318
  80.6 7.7 %collective-permute-start.15 = (bf16[64,1024]{1,0:T(8,128)(2,1)S(1)}, bf16[64,1024]{1,0:T(8,128)(2,1)S(1)}, u32[]{:S(2)}, u32[]{:S(2)}) collective-permute-start(bf16[64,1024]{1,0:T(8,128)(2,1)S(1)} %collective-permute-done.11.refs_9_), channel_id=1, source_target_pairs={{0,2},{2,0},{4,6},{6,4},{1,3},{3,1},{5,7},{7,5},{8,10},{10,8},{12,... | collective-permute-start | bytes 393224 | tf_op jit(solution)/shard_map/ppermute | solution.py:318
  82.4 7.8 %collective-permute-start.14 = (bf16[64,1024]{1,0:T(8,128)(2,1)S(1)}, bf16[64,1024]{1,0:T(8,128)(2,1)S(1)}, u32[]{:S(2)}, u32[]{:S(2)}) collective-permute-start(bf16[64,1024]{1,0:T(8,128)(2,1)S(1)} %collective-permute-done.6.refs_4_), channel_id=1, source_target_pairs={{0,4},{2,6},{4,0},{6,2},{1,5},{3,7},{5,1},{7,3},{8,12},{10,14},{12... | collective-permute-start | bytes 393224 | tf_op jit(solution)/shard_map/ppermute | solution.py:318
  83.9 6.3 %collective-permute-start.17 = (bf16[64,1024]{1,0:T(8,128)(2,1)S(1)}, bf16[64,1024]{1,0:T(8,128)(2,1)S(1)}, u32[]{:S(2)}, u32[]{:S(2)}) collective-permute-start(bf16[64,1024]{1,0:T(8,128)(2,1)S(1)} %collective-permute-done.5.refs_3_), channel_id=1, source_target_pairs={{0,6},{2,4},{4,2},{6,0},{1,7},{3,5},{5,3},{7,1},{8,14},{10,12},{12... | collective-permute-start | bytes 393224 | tf_op jit(solution)/shard_map/ppermute | solution.py:318
  85.4 6.6 %collective-permute-start.13 = (bf16[64,1024]{1,0:T(8,128)(2,1)S(1)}, bf16[64,1024]{1,0:T(8,128)(2,1)S(1)}, u32[]{:S(2)}, u32[]{:S(2)}) collective-permute-start(bf16[64,1024]{1,0:T(8,128)(2,1)S(1)} %collective-permute-done.5.refs_3_), channel_id=1, source_target_pairs={{0,4},{2,6},{4,0},{6,2},{1,5},{3,7},{5,1},{7,3},{8,12},{10,14},{12... | collective-permute-start | bytes 393224 | tf_op jit(solution)/shard_map/ppermute | solution.py:318
  86.7 5.3 %collective-permute-start.9 = (bf16[64,1024]{1,0:T(8,128)(2,1)S(1)}, bf16[64,1024]{1,0:T(8,128)(2,1)S(1)}, u32[]{:S(2)}, u32[]{:S(2)}) collective-permute-start(bf16[64,1024]{1,0:T(8,128)(2,1)S(1)} %collective-permute-done.5.refs_3_), channel_id=1, source_target_pairs={{0,2},{2,0},{4,6},{6,4},{1,3},{3,1},{5,7},{7,5},{8,10},{10,8},{12,... | collective-permute-start | bytes 393224 | tf_op jit(solution)/shard_map/ppermute | solution.py:318
  88.3 5.1 %collective-permute-start.16 = (bf16[64,1024]{1,0:T(8,128)(2,1)S(1)}, bf16[64,1024]{1,0:T(8,128)(2,1)S(1)}, u32[]{:S(2)}, u32[]{:S(2)}) collective-permute-start(bf16[64,1024]{1,0:T(8,128)(2,1)S(1)} %collective-permute-done.8.refs_6_), channel_id=1, source_target_pairs={{0,4},{2,6},{4,0},{6,2},{1,5},{3,7},{5,1},{7,3},{8,12},{10,14},{12... | collective-permute-start | bytes 393224 | tf_op jit(solution)/shard_map/ppermute | solution.py:318
  89.7 16.3 %copy-start.1 = (bf16[1,4,64,1024]{3,2,1,0:T(8,128)(2,1)S(1)}, bf16[1,4,64,1024]{3,2,1,0:T(8,128)(2,1)}, u32[]{:S(2)}) copy-start(bf16[1,4,64,1024]{3,2,1,0:T(8,128)(2,1)} %param.10) | copy-start | bytes 1572868
  89.7 17.6 %copy-start.3 = (f32[1,4,64]{2,1,0:T(4,128)S(1)}, f32[1,4,64]{2,1,0:T(4,128)}, u32[]{:S(2)}) copy-start(f32[1,4,64]{2,1,0:T(4,128)} %param.11) | copy-start | bytes 3076
  89.7 17.6 %copy-start.4 = (f32[1,4,64]{2,1,0:T(4,128)S(1)}, f32[1,4,64]{2,1,0:T(4,128)}, u32[]{:S(2)}) copy-start(f32[1,4,64]{2,1,0:T(4,128)} %param.12) | copy-start | bytes 3076
  89.7 17.6 %copy-start.5 = (f32[1,4,64]{2,1,0:T(4,128)S(1)}, f32[1,4,64]{2,1,0:T(4,128)}, u32[]{:S(2)}) copy-start(f32[1,4,64]{2,1,0:T(4,128)} %param.13) | copy-start | bytes 3076
  101.6 7.9 %collective-permute-start.18 = (bf16[64,1024]{1,0:T(8,128)(2,1)S(1)}, bf16[64,1024]{1,0:T(8,128)(2,1)S(1)}, u32[]{:S(2)}, u32[]{:S(2)}) collective-permute-start(bf16[64,1024]{1,0:T(8,128)(2,1)S(1)} %get-tuple-element.48), channel_id=1, source_target_pairs={{0,24},{8,16},{16,8},{24,0},{1,25},{9,17},{17,9},{25,1},{2,26},{10... | collective-permute-start | bytes 393224 | tf_op jit(solution)/shard_map/ppermute | solution.py:318
  103.9 11.0 %collective-permute-start.19 = (bf16[64,1024]{1,0:T(8,128)(2,1)S(1)}, bf16[64,1024]{1,0:T(8,128)(2,1)S(1)}, u32[]{:S(2)}, u32[]{:S(2)}) collective-permute-start(bf16[64,1024]{1,0:T(8,128)(2,1)S(1)} %get-tuple-element.49), channel_id=1, source_target_pairs={{0,16},{8,24},{16,0},{24,8},{1,17},{9,25},{17,1},{25,9},{2,18},{10... | collective-permute-start | bytes 393224 | tf_op jit(solution)/shard_map/ppermute | solution.py:318
  104.7 10.2 %collective-permute-start.20 = (bf16[64,1024]{1,0:T(8,128)(2,1)S(1)}, bf16[64,1024]{1,0:T(8,128)(2,1)S(1)}, u32[]{:S(2)}, u32[]{:S(2)}) collective-permute-start(bf16[64,1024]{1,0:T(8,128)(2,1)S(1)} %get-tuple-element.50), channel_id=1, source_target_pairs={{0,8},{8,0},{16,24},{24,16},{1,9},{9,1},{17,25},{25,17},{2,10},{10... | collective-permute-start | bytes 393224 | tf_op jit(solution)/shard_map/ppermute | solution.py:318

commit v8 on v6

--- a/solution.py
+++ b/solution.py
@@ -383,21 +383,20 @@
 
     pieces = [scaled[0]] + [None] * 3
     for offset in (2, 3, 1):
-        ready = after(scaled[offset], pieces[2]) if offset == 3 else scaled[offset]
-        pieces[offset] = swapped(ready, "shard", offset)
+        pieces[offset] = swapped(scaled[offset], "shard", offset)
     near, side, far = [None] * 4, [None] * 4, [None] * 4
     near[0] = swapped(pieces[0], "tensor", 1)
     side[0] = swapped(pieces[0], "tensor", 2)
-    far[0] = swapped(near[0], "tensor", 2)
+    far[0] = swapped(pieces[0], "tensor", 3)
     near[1] = swapped(pieces[1], "tensor", 1)
-    side[1] = swapped(pieces[1], "tensor", 2)
+    side[1] = swapped(after(pieces[1], near[0]), "tensor", 2)
     far[1] = swapped(side[1], "tensor", 1)
     near[2] = swapped(pieces[2], "tensor", 1)
-    side[2] = swapped(pieces[2], "tensor", 2)
+    side[2] = swapped(after(pieces[2], side[0]), "tensor", 2)
     far[2] = swapped(near[2], "tensor", 2)
-    near[3] = swapped(pieces[3], "tensor", 1)
-    side[3] = swapped(pieces[3], "tensor", 2)
-    far[3] = swapped(pieces[3], "tensor", 3)
+    near[3] = swapped(after(pieces[3], near[1]), "tensor", 1)
+    side[3] = swapped(after(pieces[3], near[1]), "tensor", 2)
+    far[3] = swapped(side[3], "tensor", 1)
     own_gram = block_gram(pieces[:3] + [after(pieces[3], far[1])])
     results = orthogonalize([pieces, near, side, far], own_gram)
 

time: 117 us -> 119 us (1.017)
  starting transfers between devices: 22.8 us -> 25.2 us
    ppermute x21, starting transfers between devices: 22.8 us -> 25.2 us  [swapped(): return lax.ppermute(array, axis, pairs)]
where the time goes in v8:
time: 119 us; the launch traced here: 118 us
  blocking collectives  56 us (47%)
  starting transfers between devices  25.2 us (21%)
  waiting for transfers between devices  18.3 us (15%)
  Pallas kernels  16.4 us (14%)
  local copies, waits for them, and re-layouts  1.71 us (1%)
    all_to_all x1, blocking collectives, per_device(): lax.all_to_all(jnp.broadcast_to(vector_grads[0], (shard_count, vector_cou...  44.3 us
    ppermute x21, starting transfers between devices, swapped(): return lax.ppermute(array, axis, pairs)  25.2 us
    ppermute x21, waiting for transfers between devices, swapped(): return lax.ppermute(array, axis, pairs)  18.3 us
    all_to_all x1, blocking collectives, per_device(): lax.all_to_all(figures.reshape(others * section_count, 1, LANES), MESH_AX...  11.7 us
    pallas_call x1, Pallas kernels, orthogonalize(): pl.pallas_call(functools.partial(orthogonalize_kernel, count, pieces), ou...  8.13 us
    pallas_call x3, Pallas kernels, on_device(): pl.pallas_call(kernel, out_shape=out_shape, in_specs=[pl.BlockSpec(memory...  4.2 us
    pallas_call x2, Pallas kernels, finished(): pl.pallas_call(functools.partial(end_kernel, offsets), out_shape=[jax.Sha...  2.74 us
  transfers between devices with their start and end apart: 21, of which 11 were waited for; matrix products, arithmetic and copies ran while one was open for 0% of the time, Pallas kernels for 3%

profile of v8, /device:TPU:0, one launch (start us, length us, event | category | flops | bytes accessed | tf_op | source)
XLA Modules:
  0.0 118.3 jit_solution(8243089058870902807)
XLA Ops:
  0.6 0.0 copy-start
  0.7 0.0 copy-start.2
  0.7 1.7 %copy-done.2 = bf16[1,1,4,256,1024]{4,3,2,1,0:T(8,128)(2,1)S(1)} copy-done((bf16[1,1,4,256,1024]{4,3,2,1,0:T(8,128)(2,1)S(1)}, bf16[1,1,4,256,1024]{4,3,2,1,0:T(8,128)(2,1)}, u32[]{:S(2)}) %copy-start.2) | copy-done | bytes 2097176
  2.3 0.7 shard_map.110
  3.1 5.1 %collective-permute-start = (bf16[4,64,1024]{2,1,0:T(8,128)(2,1)S(1)}, bf16[4,64,1024]{2,1,0:T(8,128)(2,1)S(1)}, u32[]{:S(2)}, u32[]{:S(2)}) collective-permute-start(bf16[4,64,1024]{2,1,0:T(8,128)(2,1)S(1)} %get-tuple-element.33), channel_id=1, source_target_pairs={{0,24},{8,16},{16,8},{24,0},{1,25},{9,17},{17,9},{25,1},{2,26},{10... | collective-permute-start | bytes 1572872 | tf_op jit(solution)/shard_map/ppermute | solution.py:321
  8.2 0.0 collective-permute-start.1
  8.2 0.6 collective-permute-start.2
  8.8 0.0 copy-done.6
  8.8 44.3 %all_to_all.10.refs_4_ = bf16[4,4,256]{2,1,0:T(4,128)(2,1)S(1)} all-to-all(bf16[4,4,256]{2,1,0:T(4,128)(2,1)S(1)} %broadcast_in_dim.28), channel_id=1, replica_groups=mesh['shard'=4,'tensor'=4,'section'=2] {'shard'}, dimensions={0} | all-to-all | bytes 16384 | tf_op jit(solution)/shard_map/all_to_all | solution.py:350
  53.1 0.0 collective-permute-done.refs_0_
  53.2 0.0 collective-permute-done.1.refs_1_
  53.2 0.0 collective-permute-done.2.refs_2_
  53.2 0.0 copy-done
  53.2 1.3 %shard_map.111 = (f32[4,64,1024]{2,1,0:T(8,128)S(1)}, f32[4,256]{1,0:T(4,128)S(1)}, f32[16,2,1,128]{3,2,1,0:T(1,128)S(1)}) custom-call(s32[5]{0:T(128)S(1)} %compare_select_fusion.place_ref, bf16[4,64,1024]{2,1,0:T(8,128)(2,1)S(1)} %collective-permute-done.refs_0_, bf16[4,64,1024]{2,1,0:T(8,128)(2,1)S(1)} %collective-permute-done.1.refs_1_, ...), custom_call_target="tpu_custom_call" | custom-call | tf_op jit(solution)/shard_map/pallas_call | solution.py:310
  54.5 11.7 %all_to_all.11.figures_ref = f32[32,1,128]{2,1,0:T(1,128)S(1)} all-to-all(f32[32,1,128]{2,1,0:T(1,128)S(1)} %bitcast.19), channel_id=1, replica_groups=mesh['shard'=4,'tensor'=4,'section'=2] {'shard','tensor','section'}, dimensions={0} | all-to-all | bytes 32768 | tf_op jit(solution)/shard_map/all_to_all | solution.py:369
  66.2 1.0 shard_map.112
  67.2 0.6 collective-permute-start.3
  67.9 0.5 collective-permute-start.6
  68.4 0.5 collective-permute-start.4
  68.9 3.3 %collective-permute-start.5 = (bf16[64,1024]{1,0:T(8,128)(2,1)S(1)}, bf16[64,1024]{1,0:T(8,128)(2,1)S(1)}, u32[]{:S(2)}, u32[]{:S(2)}) collective-permute-start(bf16[64,1024]{1,0:T(8,128)(2,1)S(1)} %get-tuple-element.43), channel_id=1, source_target_pairs={{0,24},{8,16},{16,8},{24,0},{1,25},{9,17},{17,9},{25,1},{2,26},{10... | collective-permute-start | bytes 393224 | tf_op jit(solution)/shard_map/ppermute | solution.py:321
  72.2 1.7 %collective-permute-done.3.refs_1_ = bf16[64,1024]{1,0:T(8,128)(2,1)S(1)} collective-permute-done((bf16[64,1024]{1,0:T(8,128)(2,1)S(1)}, bf16[64,1024]{1,0:T(8,128)(2,1)S(1)}, u32[]{:S(2)}, u32[]{:S(2)}) %collective-permute-start.3) | collective-permute-done | bytes 131104 | tf_op jit(solution)/shard_map/ppermute | solution.py:321
  73.9 0.3 collective-permute-start.7
  74.2 0.0 collective-permute-done.6.refs_4_
  74.2 0.4 collective-permute-start.11
  74.6 1.6 %collective-permute-start.10 = (bf16[64,1024]{1,0:T(8,128)(2,1)S(1)}, bf16[64,1024]{1,0:T(8,128)(2,1)S(1)}, u32[]{:S(2)}, u32[]{:S(2)}) collective-permute-start(bf16[64,1024]{1,0:T(8,128)(2,1)S(1)} %get-tuple-element.40.refs_0_), channel_id=1, source_target_pairs={{0,4},{2,6},{4,0},{6,2},{1,5},{3,7},{5,1},{7,3},{8,12},{10,14},{12... | collective-permute-start | bytes 393224 | tf_op jit(solution)/shard_map/ppermute | solution.py:321
  76.2 4.8 %collective-permute-done.4.refs_2_ = bf16[64,1024]{1,0:T(8,128)(2,1)S(1)} collective-permute-done((bf16[64,1024]{1,0:T(8,128)(2,1)S(1)}, bf16[64,1024]{1,0:T(8,128)(2,1)S(1)}, u32[]{:S(2)}, u32[]{:S(2)}) %collective-permute-start.4) | collective-permute-done | bytes 131104 | tf_op jit(solution)/shard_map/ppermute | solution.py:321
  81.0 1.2 collective-permute-start.8
  82.2 0.0 collective-permute-done.5.refs_3_
  82.2 0.0 collective-permute-done.7.refs_5_
  82.2 0.5 collective-permute-start.13
  82.7 0.0 collective-permute-done.11.refs_9_
  82.7 0.9 collective-permute-start.15
  83.6 2.1 %collective-permute-start.14 = (bf16[64,1024]{1,0:T(8,128)(2,1)S(1)}, bf16[64,1024]{1,0:T(8,128)(2,1)S(1)}, u32[]{:S(2)}, u32[]{:S(2)}) collective-permute-start(bf16[64,1024]{1,0:T(8,128)(2,1)S(1)} %get-tuple-element.40.refs_0_), channel_id=1, source_target_pairs={{0,6},{2,4},{4,2},{6,0},{1,7},{3,5},{5,3},{7,1},{8,14},{10,12},{12... | collective-permute-start | bytes 393224 | tf_op jit(solution)/shard_map/ppermute | solution.py:321
  85.7 0.0 collective-permute-done.10.refs_8_
  85.7 0.5 collective-permute-start.12
  86.2 1.3 %collective-permute-done.8.refs_6_ = bf16[64,1024]{1,0:T(8,128)(2,1)S(1)} collective-permute-done((bf16[64,1024]{1,0:T(8,128)(2,1)S(1)}, bf16[64,1024]{1,0:T(8,128)(2,1)S(1)}, u32[]{:S(2)}, u32[]{:S(2)}) %collective-permute-start.8) | collective-permute-done | bytes 131104 | tf_op jit(solution)/shard_map/ppermute | solution.py:321
  87.4 1.2 collective-permute-start.9
  88.6 1.1 collective-permute-done.13.refs_11_
  89.7 0.2 collective-permute-start.16
  89.9 0.4 collective-permute-done.15.refs_13_
  90.3 1.2 collective-permute-start.17
  91.4 0.6 shard_map.113.refs_16_
  92.0 0.0 copy-start.1
  92.0 0.0 copy-start.3
  92.0 0.0 copy-start.4
  92.0 0.0 copy-start.5
  92.0 1.0 collective-permute-done.14.refs_12_
  93.0 0.4 collective-permute-done.12.refs_10_
  93.4 1.4 %collective-permute-done.16.refs_14_ = bf16[64,1024]{1,0:T(8,128)(2,1)S(1)} collective-permute-done((bf16[64,1024]{1,0:T(8,128)(2,1)S(1)}, bf16[64,1024]{1,0:T(8,128)(2,1)S(1)}, u32[]{:S(2)}, u32[]{:S(2)}) %collective-permute-start.16) | collective-permute-done | bytes 131104 | tf_op jit(solution)/shard_map/ppermute | solution.py:321
  94.8 0.0 collective-permute-done.9.refs_7_
  94.8 0.6 collective-permute-done.17.refs_15_
  95.4 8.1 %shard_map.114 = (bf16[64,1024]{1,0:T(8,128)(2,1)S(1)}, bf16[64,1024]{1,0:T(8,128)(2,1)S(1)}, bf16[64,1024]{1,0:T(8,128)(2,1)S(1)}, bf16[64,1024]{1,0:T(8,128)(2,1)S(1)}) custom-call(bf16[64,1024]{1,0:T(8,128)(2,1)S(1)} %get-tuple-element.40.refs_0_, bf16[64,1024]{1,0:T(8,128)(2,1)S(1)} %collective-permute-done.3.refs_1_, ...), custom_call_target="tpu_custom_call" | custom-call | tf_op jit(solution)/shard_map/pallas_call | solution.py:125
  103.5 1.6 %collective-permute-start.18 = (bf16[64,1024]{1,0:T(8,128)(2,1)S(1)}, bf16[64,1024]{1,0:T(8,128)(2,1)S(1)}, u32[]{:S(2)}, u32[]{:S(2)}) collective-permute-start(bf16[64,1024]{1,0:T(8,128)(2,1)S(1)} %get-tuple-element.52), channel_id=1, source_target_pairs={{0,24},{8,16},{16,8},{24,0},{1,25},{9,17},{17,9},{25,1},{2,26},{10... | collective-permute-start | bytes 393224 | tf_op jit(solution)/shard_map/ppermute | solution.py:321
  105.1 1.3 %collective-permute-start.19 = (bf16[64,1024]{1,0:T(8,128)(2,1)S(1)}, bf16[64,1024]{1,0:T(8,128)(2,1)S(1)}, u32[]{:S(2)}, u32[]{:S(2)}) collective-permute-start(bf16[64,1024]{1,0:T(8,128)(2,1)S(1)} %get-tuple-element.53), channel_id=1, source_target_pairs={{0,16},{8,24},{16,0},{24,8},{1,17},{9,25},{17,1},{25,9},{2,18},{10... | collective-permute-start | bytes 393224 | tf_op jit(solution)/shard_map/ppermute | solution.py:321
  106.4 1.6 %collective-permute-start.20 = (bf16[64,1024]{1,0:T(8,128)(2,1)S(1)}, bf16[64,1024]{1,0:T(8,128)(2,1)S(1)}, u32[]{:S(2)}, u32[]{:S(2)}) collective-permute-start(bf16[64,1024]{1,0:T(8,128)(2,1)S(1)} %get-tuple-element.54), channel_id=1, source_target_pairs={{0,8},{8,0},{16,24},{24,16},{1,9},{9,1},{17,25},{25,17},{2,10},{10... | collective-permute-start | bytes 393224 | tf_op jit(solution)/shard_map/ppermute | solution.py:321
  108.0 1.3 %shard_map.116 = (bf16[4,64,1024]{2,1,0:T(8,128)(2,1)}, bf16[4,64,1024]{2,1,0:T(8,128)(2,1)}) custom-call(s32[5]{0:T(128)S(1)} %compare_select_fusion.place_ref, bf16[64,1024]{1,0:T(8,128)(2,1)S(1)} %get-tuple-element.48.refs_0_, bf16[4,64,1024]{2,1,0:T(8,128)(2,1)S(1)} %bitcast.16), custom_call_target="tpu_custom_call" | custom-call | tf_op jit(solution)/shard_map/pallas_call | solution.py:264
  109.3 0.0 copy-done.3
  109.3 0.0 copy-done.4
  109.3 0.0 copy-done.5
  109.3 1.8 %shard_map.115 = (f32[4,64,1024]{2,1,0:T(8,128)}, f32[4,64]{1,0:T(4,128)}, f32[4,64]{1,0:T(4,128)}) custom-call(s32[5]{0:T(128)S(1)} %compare_select_fusion.place_ref, f32[8,128]{1,0:T(8,128)S(1)} %get-tuple-element.49.clip_ref, f32[4,64,1024]{2,1,0:T(8,128)S(1)} %get-tuple-element.38.grad_ref, f32[4,64,1024]{2,1,0:T(8,128)S(1)} %bitcast.15, ...), custom_call_target="tpu_custom_call" | custom-call | tf_op jit(solution)/shard_map/pallas_call | solution.py:310
  111.1 0.3 collective-permute-done.18.refs_0_
  111.4 5.4 %collective-permute-done.19.refs_1_ = bf16[64,1024]{1,0:T(8,128)(2,1)S(1)} collective-permute-done((bf16[64,1024]{1,0:T(8,128)(2,1)S(1)}, bf16[64,1024]{1,0:T(8,128)(2,1)S(1)}, u32[]{:S(2)}, u32[]{:S(2)}) %collective-permute-start.19) | collective-permute-done | bytes 131104 | tf_op jit(solution)/shard_map/ppermute | solution.py:321
  116.8 0.0 collective-permute-done.20.refs_2_
  116.8 1.5 %shard_map.117 = (bf16[4,64,1024]{2,1,0:T(8,128)(2,1)}, bf16[4,64,1024]{2,1,0:T(8,128)(2,1)}) custom-call(s32[5]{0:T(128)S(1)} %compare_select_fusion.place_ref, bf16[64,1024]{1,0:T(8,128)(2,1)S(1)} %collective-permute-done.18.refs_0_, bf16[64,1024]{1,0:T(8,128)(2,1)S(1)} %collective-permute-done.19.refs_1_, ...), custom_call_target="tpu_custom_call", output_to_operand_aliasing={{0}: (5, {}), {1}: (6, {})} | custom-call | tf_op jit(solution)/shard_map/pallas_call | solution.py:264
  (4 shorter events, 0.0 us)
Async XLA Ops:
  0.6 52.5 %copy-start = (f32[1,4,64,1024]{3,2,1,0:T(8,128)S(1)}, f32[1,4,64,1024]{3,2,1,0:T(8,128)}, u32[]{:S(2)}) copy-start(f32[1,4,64,1024]{3,2,1,0:T(8,128)} %param.9) | copy-start | bytes 3145732
  0.7 1.7 %copy-start.2 = (bf16[1,1,4,256,1024]{4,3,2,1,0:T(8,128)(2,1)S(1)}, bf16[1,1,4,256,1024]{4,3,2,1,0:T(8,128)(2,1)}, u32[]{:S(2)}) copy-start(bf16[1,1,4,256,1024]{4,3,2,1,0:T(8,128)(2,1)} %param.7) | copy-start | bytes 6291460
  2.3 6.5 %copy-start.6 = (bf16[1,1,4,256]{3,2,1,0:T(4,128)(2,1)S(1)}, bf16[1,1,4,256]{3,2,1,0:T(4,128)(2,1)}, u32[]{:S(2)}) copy-start(bf16[1,1,4,256]{3,2,1,0:T(4,128)(2,1)} %param.8) | copy-start | bytes 6148
  3.1 50.1 %collective-permute-start = (bf16[4,64,1024]{2,1,0:T(8,128)(2,1)S(1)}, bf16[4,64,1024]{2,1,0:T(8,128)(2,1)S(1)}, u32[]{:S(2)}, u32[]{:S(2)}) collective-permute-start(bf16[4,64,1024]{2,1,0:T(8,128)(2,1)S(1)} %get-tuple-element.33), channel_id=1, source_target_pairs={{0,24},{8,16},{16,8},{24,0},{1,25},{9,17},{17,9},{25,1},{2,26},{10... | collective-permute-start | bytes 1572872 | tf_op jit(solution)/shard_map/ppermute | solution.py:321
  8.2 45.0 %collective-permute-start.1 = (bf16[4,64,1024]{2,1,0:T(8,128)(2,1)S(1)}, bf16[4,64,1024]{2,1,0:T(8,128)(2,1)S(1)}, u32[]{:S(2)}, u32[]{:S(2)}) collective-permute-start(bf16[4,64,1024]{2,1,0:T(8,128)(2,1)S(1)} %get-tuple-element.34), channel_id=1, source_target_pairs={{0,16},{8,24},{16,0},{24,8},{1,17},{9,25},{17,1},{25,9},{2,18},{10... | collective-permute-start | bytes 1572872 | tf_op jit(solution)/shard_map/ppermute | solution.py:321
  8.2 45.0 %collective-permute-start.2 = (bf16[4,64,1024]{2,1,0:T(8,128)(2,1)S(1)}, bf16[4,64,1024]{2,1,0:T(8,128)(2,1)S(1)}, u32[]{:S(2)}, u32[]{:S(2)}) collective-permute-start(bf16[4,64,1024]{2,1,0:T(8,128)(2,1)S(1)} %get-tuple-element.35), channel_id=1, source_target_pairs={{0,8},{8,0},{16,24},{24,16},{1,9},{9,1},{17,25},{25,17},{2,10},{10... | collective-permute-start | bytes 1572872 | tf_op jit(solution)/shard_map/ppermute | solution.py:321
  67.2 6.7 %collective-permute-start.3 = (bf16[64,1024]{1,0:T(8,128)(2,1)S(1)}, bf16[64,1024]{1,0:T(8,128)(2,1)S(1)}, u32[]{:S(2)}, u32[]{:S(2)}) collective-permute-start(bf16[64,1024]{1,0:T(8,128)(2,1)S(1)} %get-tuple-element.41), channel_id=1, source_target_pairs={{0,8},{8,0},{16,24},{24,16},{1,9},{9,1},{17,25},{25,17},{2,10},{10... | collective-permute-start | bytes 393224 | tf_op jit(solution)/shard_map/ppermute | solution.py:321
  67.9 6.3 %collective-permute-start.6 = (bf16[64,1024]{1,0:T(8,128)(2,1)S(1)}, bf16[64,1024]{1,0:T(8,128)(2,1)S(1)}, u32[]{:S(2)}, u32[]{:S(2)}) collective-permute-start(bf16[64,1024]{1,0:T(8,128)(2,1)S(1)} %get-tuple-element.40.refs_0_), channel_id=1, source_target_pairs={{0,2},{2,0},{4,6},{6,4},{1,3},{3,1},{5,7},{7,5},{8,10},{10,8},{12,... | collective-permute-start | bytes 393224 | tf_op jit(solution)/shard_map/ppermute | solution.py:321
  68.4 12.6 %collective-permute-start.4 = (bf16[64,1024]{1,0:T(8,128)(2,1)S(1)}, bf16[64,1024]{1,0:T(8,128)(2,1)S(1)}, u32[]{:S(2)}, u32[]{:S(2)}) collective-permute-start(bf16[64,1024]{1,0:T(8,128)(2,1)S(1)} %get-tuple-element.42), channel_id=1, source_target_pairs={{0,16},{8,24},{16,0},{24,8},{1,17},{9,25},{17,1},{25,9},{2,18},{10... | collective-permute-start | bytes 393224 | tf_op jit(solution)/shard_map/ppermute | solution.py:321
  68.9 13.2 %collective-permute-start.5 = (bf16[64,1024]{1,0:T(8,128)(2,1)S(1)}, bf16[64,1024]{1,0:T(8,128)(2,1)S(1)}, u32[]{:S(2)}, u32[]{:S(2)}) collective-permute-start(bf16[64,1024]{1,0:T(8,128)(2,1)S(1)} %get-tuple-element.43), channel_id=1, source_target_pairs={{0,24},{8,16},{16,8},{24,0},{1,25},{9,17},{17,9},{25,1},{2,26},{10... | collective-permute-start | bytes 393224 | tf_op jit(solution)/shard_map/ppermute | solution.py:321
  73.9 8.3 %collective-permute-start.7 = (bf16[64,1024]{1,0:T(8,128)(2,1)S(1)}, bf16[64,1024]{1,0:T(8,128)(2,1)S(1)}, u32[]{:S(2)}, u32[]{:S(2)}) collective-permute-start(bf16[64,1024]{1,0:T(8,128)(2,1)S(1)} %collective-permute-done.3.refs_1_), channel_id=1, source_target_pairs={{0,2},{2,0},{4,6},{6,4},{1,3},{3,1},{5,7},{7,5},{8,10},{10,8},{12,... | collective-permute-start | bytes 393224 | tf_op jit(solution)/shard_map/ppermute | solution.py:321
  74.2 8.5 %collective-permute-start.11 = (bf16[64,1024]{1,0:T(8,128)(2,1)S(1)}, bf16[64,1024]{1,0:T(8,128)(2,1)S(1)}, u32[]{:S(2)}, u32[]{:S(2)}) collective-permute-start(bf16[64,1024]{1,0:T(8,128)(2,1)S(1)} %collective-permute-done.3.refs_1_), channel_id=1, source_target_pairs={{0,4},{2,6},{4,0},{6,2},{1,5},{3,7},{5,1},{7,3},{8,12},{10,14},{12... | collective-permute-start | bytes 393224 | tf_op jit(solution)/shard_map/ppermute | solution.py:321
  74.6 11.1 %collective-permute-start.10 = (bf16[64,1024]{1,0:T(8,128)(2,1)S(1)}, bf16[64,1024]{1,0:T(8,128)(2,1)S(1)}, u32[]{:S(2)}, u32[]{:S(2)}) collective-permute-start(bf16[64,1024]{1,0:T(8,128)(2,1)S(1)} %get-tuple-element.40.refs_0_), channel_id=1, source_target_pairs={{0,4},{2,6},{4,0},{6,2},{1,5},{3,7},{5,1},{7,3},{8,12},{10,14},{12... | collective-permute-start | bytes 393224 | tf_op jit(solution)/shard_map/ppermute | solution.py:321
  81.0 6.4 %collective-permute-start.8 = (bf16[64,1024]{1,0:T(8,128)(2,1)S(1)}, bf16[64,1024]{1,0:T(8,128)(2,1)S(1)}, u32[]{:S(2)}, u32[]{:S(2)}) collective-permute-start(bf16[64,1024]{1,0:T(8,128)(2,1)S(1)} %collective-permute-done.4.refs_2_), channel_id=1, source_target_pairs={{0,2},{2,0},{4,6},{6,4},{1,3},{3,1},{5,7},{7,5},{8,10},{10,8},{12,... | collective-permute-start | bytes 393224 | tf_op jit(solution)/shard_map/ppermute | solution.py:321
  82.2 7.5 %collective-permute-start.13 = (bf16[64,1024]{1,0:T(8,128)(2,1)S(1)}, bf16[64,1024]{1,0:T(8,128)(2,1)S(1)}, u32[]{:S(2)}, u32[]{:S(2)}) collective-permute-start(bf16[64,1024]{1,0:T(8,128)(2,1)S(1)} %collective-permute-done.5.refs_3_), channel_id=1, source_target_pairs={{0,4},{2,6},{4,0},{6,2},{1,5},{3,7},{5,1},{7,3},{8,12},{10,14},{12... | collective-permute-start | bytes 393224 | tf_op jit(solution)/shard_map/ppermute | solution.py:321
  82.7 7.6 %collective-permute-start.15 = (bf16[64,1024]{1,0:T(8,128)(2,1)S(1)}, bf16[64,1024]{1,0:T(8,128)(2,1)S(1)}, u32[]{:S(2)}, u32[]{:S(2)}) collective-permute-start(bf16[64,1024]{1,0:T(8,128)(2,1)S(1)} %collective-permute-done.11.refs_9_), channel_id=1, source_target_pairs={{0,2},{2,0},{4,6},{6,4},{1,3},{3,1},{5,7},{7,5},{8,10},{10,8},{12,... | collective-permute-start | bytes 393224 | tf_op jit(solution)/shard_map/ppermute | solution.py:321
  83.6 9.4 %collective-permute-start.14 = (bf16[64,1024]{1,0:T(8,128)(2,1)S(1)}, bf16[64,1024]{1,0:T(8,128)(2,1)S(1)}, u32[]{:S(2)}, u32[]{:S(2)}) collective-permute-start(bf16[64,1024]{1,0:T(8,128)(2,1)S(1)} %get-tuple-element.40.refs_0_), channel_id=1, source_target_pairs={{0,6},{2,4},{4,2},{6,0},{1,7},{3,5},{5,3},{7,1},{8,14},{10,12},{12... | collective-permute-start | bytes 393224 | tf_op jit(solution)/shard_map/ppermute | solution.py:321
  85.7 7.7 %collective-permute-start.12 = (bf16[64,1024]{1,0:T(8,128)(2,1)S(1)}, bf16[64,1024]{1,0:T(8,128)(2,1)S(1)}, u32[]{:S(2)}, u32[]{:S(2)}) collective-permute-start(bf16[64,1024]{1,0:T(8,128)(2,1)S(1)} %collective-permute-done.4.refs_2_), channel_id=1, source_target_pairs={{0,4},{2,6},{4,0},{6,2},{1,5},{3,7},{5,1},{7,3},{8,12},{10,14},{12... | collective-permute-start | bytes 393224 | tf_op jit(solution)/shard_map/ppermute | solution.py:321
  87.4 7.4 %collective-permute-start.9 = (bf16[64,1024]{1,0:T(8,128)(2,1)S(1)}, bf16[64,1024]{1,0:T(8,128)(2,1)S(1)}, u32[]{:S(2)}, u32[]{:S(2)}) collective-permute-start(bf16[64,1024]{1,0:T(8,128)(2,1)S(1)} %collective-permute-done.5.refs_3_), channel_id=1, source_target_pairs={{0,2},{2,0},{4,6},{6,4},{1,3},{3,1},{5,7},{7,5},{8,10},{10,8},{12,... | collective-permute-start | bytes 393224 | tf_op jit(solution)/shard_map/ppermute | solution.py:321
  89.7 5.1 %collective-permute-start.16 = (bf16[64,1024]{1,0:T(8,128)(2,1)S(1)}, bf16[64,1024]{1,0:T(8,128)(2,1)S(1)}, u32[]{:S(2)}, u32[]{:S(2)}) collective-permute-start(bf16[64,1024]{1,0:T(8,128)(2,1)S(1)} %collective-permute-done.8.refs_6_), channel_id=1, source_target_pairs={{0,4},{2,6},{4,0},{6,2},{1,5},{3,7},{5,1},{7,3},{8,12},{10,14},{12... | collective-permute-start | bytes 393224 | tf_op jit(solution)/shard_map/ppermute | solution.py:321
  90.3 5.1 %collective-permute-start.17 = (bf16[64,1024]{1,0:T(8,128)(2,1)S(1)}, bf16[64,1024]{1,0:T(8,128)(2,1)S(1)}, u32[]{:S(2)}, u32[]{:S(2)}) collective-permute-start(bf16[64,1024]{1,0:T(8,128)(2,1)S(1)} %collective-permute-done.13.refs_11_), channel_id=1, source_target_pairs={{0,2},{2,0},{4,6},{6,4},{1,3},{3,1},{5,7},{7,5},{8,10},{10,8},{12,... | collective-permute-start | bytes 393224 | tf_op jit(solution)/shard_map/ppermute | solution.py:321
  92.0 16.0 %copy-start.1 = (bf16[1,4,64,1024]{3,2,1,0:T(8,128)(2,1)S(1)}, bf16[1,4,64,1024]{3,2,1,0:T(8,128)(2,1)}, u32[]{:S(2)}) copy-start(bf16[1,4,64,1024]{3,2,1,0:T(8,128)(2,1)} %param.10) | copy-start | bytes 1572868
  92.0 17.3 %copy-start.3 = (f32[1,4,64]{2,1,0:T(4,128)S(1)}, f32[1,4,64]{2,1,0:T(4,128)}, u32[]{:S(2)}) copy-start(f32[1,4,64]{2,1,0:T(4,128)} %param.11) | copy-start | bytes 3076
  92.0 17.3 %copy-start.4 = (f32[1,4,64]{2,1,0:T(4,128)S(1)}, f32[1,4,64]{2,1,0:T(4,128)}, u32[]{:S(2)}) copy-start(f32[1,4,64]{2,1,0:T(4,128)} %param.12) | copy-start | bytes 3076
  92.0 17.3 %copy-start.5 = (f32[1,4,64]{2,1,0:T(4,128)S(1)}, f32[1,4,64]{2,1,0:T(4,128)}, u32[]{:S(2)}) copy-start(f32[1,4,64]{2,1,0:T(4,128)} %param.13) | copy-start | bytes 3076
  103.5 7.9 %collective-permute-start.18 = (bf16[64,1024]{1,0:T(8,128)(2,1)S(1)}, bf16[64,1024]{1,0:T(8,128)(2,1)S(1)}, u32[]{:S(2)}, u32[]{:S(2)}) collective-permute-start(bf16[64,1024]{1,0:T(8,128)(2,1)S(1)} %get-tuple-element.52), channel_id=1, source_target_pairs={{0,24},{8,16},{16,8},{24,0},{1,25},{9,17},{17,9},{25,1},{2,26},{10... | collective-permute-start | bytes 393224 | tf_op jit(solution)/shard_map/ppermute | solution.py:321
  105.1 11.7 %collective-permute-start.19 = (bf16[64,1024]{1,0:T(8,128)(2,1)S(1)}, bf16[64,1024]{1,0:T(8,128)(2,1)S(1)}, u32[]{:S(2)}, u32[]{:S(2)}) collective-permute-start(bf16[64,1024]{1,0:T(8,128)(2,1)S(1)} %get-tuple-element.53), channel_id=1, source_target_pairs={{0,16},{8,24},{16,0},{24,8},{1,17},{9,25},{17,1},{25,9},{2,18},{10... | collective-permute-start | bytes 393224 | tf_op jit(solution)/shard_map/ppermute | solution.py:321
  106.4 10.4 %collective-permute-start.20 = (bf16[64,1024]{1,0:T(8,128)(2,1)S(1)}, bf16[64,1024]{1,0:T(8,128)(2,1)S(1)}, u32[]{:S(2)}, u32[]{:S(2)}) collective-permute-start(bf16[64,1024]{1,0:T(8,128)(2,1)S(1)} %get-tuple-element.54), channel_id=1, source_target_pairs={{0,8},{8,0},{16,24},{24,16},{1,9},{9,1},{17,25},{25,17},{2,10},{10... | collective-permute-start | bytes 393224 | tf_op jit(solution)/shard_map/ppermute | solution.py:321
